TPU v7x, 32 devices: a whole 2x2x4 slice. The times are simulated.
32 devices in a mesh: groups: 2 (over x), frame: 16 (over z, y, core).
Axes of the slice: x: 2, y: 2, z: 4, core: 2. Of those that a mesh axis runs over, the one named last changes fastest.
Arguments:
- latent: bfloat16 [128, 32, 1152], P(('groups', 'frame')), parts along dimension 0, may hold values from -6 to 6
- ln_gain: float32 [1152], replicated, may hold values from 0.1 to 1.9
- q_gain: float32 [72], replicated, may hold values from 0.1 to 1.9
- k_gain: float32 [72], replicated, may hold values from 0.1 to 1.9
- w_qkv: bfloat16 [1152, 3456], replicated, may hold values from -0.1875 to 0.1875
- w_out: bfloat16 [1152, 1152], replicated, may hold values from -0.5 to 0.5
Outputs:
- result: bfloat16 [128, 32, 1152], P(('groups', 'frame')), parts along dimension 0
There are 2 independent parts, one for each index of `groups`. A program takes and returns all parts, laid end to end along the dimension named above; an argument that names none is the same for every part. Nothing has to cross between parts.
All inputs are finite; a program needn't handle non-finite values.
Results may differ from a plain program's by a relative error of at most 0.006.
Values may be sent and summed in bfloat16 or wider, within the bound.
No kernel may reach another device: no remote copies, remote signals or barrier semaphores. Data moves between devices by JAX's collectives and lax.ppermute only.
A program may use at most 64 MiB of HBM per device.

v0:
```python
import functools
import math

import jax
import jax.numpy as jnp
from jax import lax
from jax.experimental import pallas as pl
from jax.experimental.pallas import tpu as pltpu
from jax.sharding import PartitionSpec as P

HEADS = 16
HEAD_DIM = 72
LANES = 128
EPS = 1e-06
EXP2_SCALE = HEAD_DIM**-0.5 * math.log2(math.e)


def dot(a, b):
    return jnp.dot(a, b, preferred_element_type=jnp.float32)


def held_kernel(
    ln_ref, qg_ref, kg_ref, wqkv_ref, gains_out, member_out, spread_out, wq_out, ln, qg, kg, sems
):
    width = wq_out.shape[1]
    pairs = [(ln_ref, ln), (qg_ref, qg), (kg_ref, kg), (wqkv_ref.at[:, pl.ds(0, width)], wq_out)]
    copies = [pltpu.make_async_copy(src, dst, sems.at[i]) for i, (src, dst) in enumerate(pairs)]
    for copy in copies:
        copy.start()

    def belongs(feature, lane):
        head = jnp.where(lane >= HEADS, lane - HEADS, lane)
        first = head * HEAD_DIM
        held = (feature >= first) & (feature < first + HEAD_DIM) & (lane < 2 * HEADS)
        return held.astype(jnp.float32).astype(jnp.bfloat16)

    for out, axis in ((member_out, 0), (spread_out, 1)):
        feature = lax.broadcasted_iota(jnp.int32, out.shape, axis)
        out[...] = belongs(feature, lax.broadcasted_iota(jnp.int32, out.shape, 1 - axis))
    for copy in copies[:3]:
        copy.wait()
    gains_out[0:1, :] = ln[...].reshape(1, width)
    gains_out[1:2, :] = jnp.concatenate([qg[...].reshape(1, HEAD_DIM)] * HEADS, axis=1)
    gains_out[2:3, :] = jnp.concatenate([kg[...].reshape(1, HEAD_DIM)] * HEADS, axis=1)
    copies[3].wait()


def tokens_kernel(
    x_ref,
    gains_ref,
    member_ref,
    spread_ref,
    wq,
    wqkv_hbm,
    wout_hbm,
    o_ref,
    wkv,
    wout,
    normed,
    mixed_q,
    mixed_k,
    queries,
    keys,
    values,
    attended,
    same,
    sems,
):
    frames, positions, width = x_ref.shape
    tokens = frames * positions
    bf16, f32 = jnp.bfloat16, jnp.float32

    pairs = [
        (wqkv_hbm.at[:, pl.ds(width, width)], wkv.at[:, pl.ds(0, width)]),
        (wqkv_hbm.at[:, pl.ds(2 * width, width)], wkv.at[:, pl.ds(width, width)]),
        (wout_hbm, wout),
    ]
    copies = [pltpu.make_async_copy(src, dst, sems.at[i]) for i, (src, dst) in enumerate(pairs)]
    copies[0].start()

    gain = gains_ref[0:1, :]
    step = max(1, 16 // positions)
    for frame in range(0, frames, step):
        x = x_ref[frame : frame + step].astype(f32).reshape(step * positions, width)
        center = x - jnp.mean(x, axis=-1, keepdims=True)
        spread = jnp.mean(center * center, axis=-1, keepdims=True)
        rows = slice(frame * positions, (frame + step) * positions)
        normed[rows, :] = (center * lax.rsqrt(spread + EPS) * gain).astype(bf16)

    def head_norm(mixed, row, out):
        squares = mixed[...] * mixed[...]
        high = squares.astype(bf16)
        low = (squares - high.astype(f32)).astype(bf16)
        total = dot(jnp.concatenate([high, low], axis=0), member_ref[...])
        total = total[:tokens] + total[tokens:]
        inverse = lax.rsqrt(total * (1.0 / HEAD_DIM) + EPS)
        high = inverse.astype(bf16)
        low = (inverse - high.astype(f32)).astype(bf16)
        lane = lax.broadcasted_iota(jnp.int32, inverse.shape, 1)
        parts = jnp.where(lane < HEADS, high, low)[:, : 2 * HEADS]
        out[...] = (mixed[...] * dot(parts, spread_ref[...]) * gains_ref[row : row + 1, :]).astype(bf16)

    copies[1].start()
    mixed_q[...] = dot(normed[...], wq[...])
    head_norm(mixed_q, 1, queries)
    copies[0].wait()
    copies[2].start()
    mixed_k[...] = dot(normed[...], wkv[:, :width])
    head_norm(mixed_k, 2, keys)
    copies[1].wait()
    values[...] = dot(normed[...], wkv[:, width:]).astype(bf16)

    place = lax.broadcasted_iota(jnp.int32, (tokens, tokens), 0) % positions
    other = lax.broadcasted_iota(jnp.int32, (tokens, tokens), 1) % positions
    same[...] = (place == other).astype(f32)

    held = None
    for pair in range(HEADS // 2):
        window = slice(pair * LANES, (pair + 2) * LANES)
        lane = lax.broadcasted_iota(jnp.int32, (1, 2 * LANES), 1)
        begin = pair * (2 * HEAD_DIM - LANES)
        mine = [(lane >= begin + h * HEAD_DIM) & (lane < begin + (h + 1) * HEAD_DIM) for h in range(2)]
        zero = jnp.zeros((), bf16)
        key, value = (
            jnp.concatenate([jnp.where(own, ref[:, window], zero) for own in mine], axis=0)
            for ref in (keys, values)
        )
        scores = lax.dot_general(
            queries[:, window], key, (((1,), (1,)), ((), ())), preferred_element_type=f32
        )
        weights = []
        for h in range(2):
            part = jnp.exp2(scores[:, h * tokens : (h + 1) * tokens] * EXP2_SCALE) * same[...]
            weights.append((part / jnp.sum(part, axis=-1, keepdims=True)).astype(bf16))
        both = dot(jnp.concatenate(weights, axis=1), value)
        first = both[:, :LANES]
        if held is not None:
            first = first + held
        held = both[:, LANES:]
        attended[:, pair * LANES : (pair + 1) * LANES] = first.astype(bf16)
    attended[:, HEADS // 2 * LANES :] = held.astype(bf16)

    copies[2].wait()
    branch = dot(attended[...], wout[...])
    o_ref[...] = (x_ref[...].astype(f32) + branch.reshape(x_ref.shape)).astype(bf16)


def body(latent, ln_gain, q_gain, k_gain, w_qkv, w_out):
    device_count = lax.axis_size("frame")
    rows, columns, model = latent.shape
    tokens = rows * columns
    per_peer = tokens // device_count
    exchange = functools.partial(
        lax.all_to_all, axis_name="frame", split_axis=0, concat_axis=0, tiled=True
    )
    gathered = exchange(latent.reshape(device_count, per_peer, model))
    in_vmem = pl.BlockSpec(memory_space=pltpu.VMEM)
    in_hbm = pl.BlockSpec(memory_space=pltpu.HBM)
    bf16, f32 = jnp.bfloat16, jnp.float32
    held = [pltpu.with_memory_space_constraint(a, pltpu.HBM) for a in (ln_gain, q_gain, k_gain, w_qkv, w_out)]
    gains, member, spread, wq = pl.pallas_call(
        held_kernel,
        out_shape=(
            pltpu.VMEM((8, model), f32),
            pltpu.VMEM((model, LANES), bf16),
            pltpu.VMEM((2 * HEADS, model), bf16),
            pltpu.VMEM((model, model), bf16),
        ),
        in_specs=[in_hbm] * 4,
        out_specs=[in_vmem] * 4,
        scratch_shapes=[
            pltpu.VMEM((model,), f32),
            pltpu.VMEM((HEAD_DIM,), f32),
            pltpu.VMEM((HEAD_DIM,), f32),
            pltpu.SemaphoreType.DMA((4,)),
        ],
        compiler_params=pltpu.CompilerParams(vmem_limit_bytes=8 * 1024 * 1024),
        cost_estimate=pl.CostEstimate(flops=0, bytes_accessed=4 * model * model, transcendentals=0),
        name="held",
    )(*held[:4])
    result = pl.pallas_call(
        tokens_kernel,
        out_shape=jax.ShapeDtypeStruct(gathered.shape, bf16),
        in_specs=[in_vmem] * 5 + [in_hbm] * 2,
        out_specs=in_vmem,
        scratch_shapes=[
            pltpu.VMEM((model, 2 * model), bf16),
            pltpu.VMEM(w_out.shape, bf16),
            pltpu.VMEM((tokens, model), bf16),
            pltpu.VMEM((tokens, model), f32),
            pltpu.VMEM((tokens, model), f32),
            pltpu.VMEM((tokens, model), bf16),
            pltpu.VMEM((tokens, model), bf16),
            pltpu.VMEM((tokens, model), bf16),
            pltpu.VMEM((tokens, model), bf16),
            pltpu.VMEM((tokens, tokens), f32),
            pltpu.SemaphoreType.DMA((3,)),
        ],
        compiler_params=pltpu.CompilerParams(vmem_limit_bytes=40 * 1024 * 1024),
        name="tokens",
    )(gathered, gains, member, spread, wq, *held[3:])
    return exchange(result).reshape(latent.shape)


def solution(mesh):
    placed = (P(("groups", "frame"), None, None), P(), P(), P(), P(), P())
    return jax.shard_map(
        body,
        mesh=mesh,
        in_specs=placed,
        out_specs=P(("groups", "frame"), None, None),
        check_vma=False,
    )
```

profile of v0, /device:TPU:0, one launch (start us, length us, event | category | flops | bytes accessed | tf_op | source)
XLA Modules:
  0.0 38.4 jit_solution(10756743590627165826)
XLA Ops:
  0.0 7.4 %all-to-all-start = ((bf16[16,8,1152]{2,1,0:T(8,128)(2,1)}), bf16[16,8,1152]{2,1,0:T(8,128)(2,1)S(1)}, u32[]{:S(2)}, u32[]{:S(2)}) async-start(bf16[16,8,1152]{2,1,0:T(8,128)(2,1)} %bitcast.3), calls=%async_computation | async-start | bytes 589824 | tf_op jit(solution)/shard_map/all_to_all | solution.py:156
  7.4 1.8 %held.1 = (f32[8,1152]{1,0:T(8,128)S(1)}, bf16[1152,128]{1,0:T(8,128)(2,1)S(1)}, bf16[32,1152]{1,0:T(8,128)(2,1)S(1)}, bf16[1152,1152]{1,0:T(8,128)(2,1)S(1)}) custom-call(f32[1152]{0:T(1024)} %ln_ref.1, f32[72]{0:T(128)} %qg_ref.1, f32[72]{0:T(128)} %kg_ref.1, bf16[1152,3456]{1,0:T(8,128)(2,1)} %wqkv_hbm.1), custom_call_target="tpu_custom_call" | custom-call | bytes 5308416 | tf_op jit(solution)/shard_map/held/pallas_call | solution.py:161
  9.2 8.7 %all-to-all-done.x_ref = bf16[16,8,1152]{2,1,0:T(8,128)(2,1)S(1)} async-done(((bf16[16,8,1152]{2,1,0:T(8,128)(2,1)}), bf16[16,8,1152]{2,1,0:T(8,128)(2,1)S(1)}, u32[]{:S(2)}, u32[]{:S(2)}) %all-to-all-start) | async-done | bytes 294944 | tf_op jit(solution)/shard_map/all_to_all | solution.py:156
  18.0 6.2 %tokens.1 = bf16[16,8,1152]{2,1,0:T(8,128)(2,1)S(1)} custom-call(bf16[16,8,1152]{2,1,0:T(8,128)(2,1)S(1)} %all-to-all-done.x_ref, f32[8,1152]{1,0:T(8,128)S(1)} %get-tuple-element.9.gains_ref, bf16[1152,128]{1,0:T(8,128)(2,1)S(1)} %get-tuple-element.10.member_ref, bf16[32,1152]{1,0:T(8,128)(2,1)S(1)} %get-tuple-element.11.spread_ref, ...), custom_call_target="tpu_custom_call" | custom-call | tf_op jit(solution)/shard_map/tokens/pallas_call | solution.py:181
  24.2 13.5 %all_to_all.10 = bf16[16,8,1152]{2,1,0:T(8,128)(2,1)S(1)} all-to-all(bf16[16,8,1152]{2,1,0:T(8,128)(2,1)S(1)} %tokens.1), channel_id=1, replica_groups=mesh['groups'=2,'frame'=16] {'frame'}, dimensions={0} | all-to-all | bytes 589824 | tf_op jit(solution)/shard_map/all_to_all | solution.py:202
  37.6 0.7 %copy.8 = bf16[4,32,1152]{2,1,0:T(8,128)(2,1)} copy(bf16[4,32,1152]{2,1,0:T(8,128)(2,1)S(1)} %bitcast.2) | data formatting | bytes 589824
Async XLA Ops:
  0.0 18.0 %all-to-all-start = ((bf16[16,8,1152]{2,1,0:T(8,128)(2,1)}), bf16[16,8,1152]{2,1,0:T(8,128)(2,1)S(1)}, u32[]{:S(2)}, u32[]{:S(2)}) async-start(bf16[16,8,1152]{2,1,0:T(8,128)(2,1)} %bitcast.3), calls=%async_computation | async-start | bytes 589824 | tf_op jit(solution)/shard_map/all_to_all | solution.py:156
where the time goes:
time: 38.6 us; the launch traced here: 38.4 us
  blocking collectives  13.5 us (35%)
  waiting for transfers between devices  8.73 us (23%)
  Pallas kernels  8.02 us (21%)
  starting transfers between devices  7.39 us (19%)
  local copies, waits for them, and re-layouts  0.71 us (2%)
    all_to_all x1, blocking collectives, body(): return exchange(result).reshape(latent.shape)  13.5 us
    all_to_all x1, waiting for transfers between devices, body(): gathered = exchange(latent.reshape(device_count, per_peer, model))  8.73 us
    all_to_all x1, starting transfers between devices, body(): gathered = exchange(latent.reshape(device_count, per_peer, model))  7.39 us
    pallas_call x1, Pallas kernels, body(): pl.pallas_call(tokens_kernel, out_shape=jax.ShapeDtypeStruct(gathered.sha...  6.18 us
    pallas_call x1, Pallas kernels, body(): pl.pallas_call(held_kernel, out_shape=(pltpu.VMEM((8, model), f32), pltpu...  1.84 us
  transfers between devices with their start and end apart: 1, of which 1 were waited for; matrix products, arithmetic and copies ran while one was open for 0% of the time, Pallas kernels for 5%

commit v1 on v0

--- a/solution.py
+++ b/solution.py
@@ -60,8 +60,10 @@
     mixed_q,
     mixed_k,
     queries,
+    queries_t,
     keys,
-    values,
+    values_t,
+    attended_t,
     attended,
     same,
     sems,
@@ -70,11 +72,7 @@
     tokens = frames * positions
     bf16, f32 = jnp.bfloat16, jnp.float32
 
-    pairs = [
-        (wqkv_hbm.at[:, pl.ds(width, width)], wkv.at[:, pl.ds(0, width)]),
-        (wqkv_hbm.at[:, pl.ds(2 * width, width)], wkv.at[:, pl.ds(width, width)]),
-        (wout_hbm, wout),
-    ]
+    pairs = [(wqkv_hbm.at[:, pl.ds(width, 2 * width)], wkv), (wout_hbm, wout)]
     copies = [pltpu.make_async_copy(src, dst, sems.at[i]) for i, (src, dst) in enumerate(pairs)]
     copies[0].start()
 
@@ -104,43 +102,39 @@
     mixed_q[...] = dot(normed[...], wq[...])
     head_norm(mixed_q, 1, queries)
     copies[0].wait()
-    copies[2].start()
     mixed_k[...] = dot(normed[...], wkv[:, :width])
+    queries_t[...] = queries[...].T
+    values_t[...] = dot(normed[...], wkv[:, width:]).astype(bf16).T
     head_norm(mixed_k, 2, keys)
-    copies[1].wait()
-    values[...] = dot(normed[...], wkv[:, width:]).astype(bf16)
 
     place = lax.broadcasted_iota(jnp.int32, (tokens, tokens), 0) % positions
     other = lax.broadcasted_iota(jnp.int32, (tokens, tokens), 1) % positions
     same[...] = (place == other).astype(f32)
 
-    held = None
+    row = lax.broadcasted_iota(jnp.int32, (2 * LANES, tokens), 0)
     for pair in range(HEADS // 2):
         window = slice(pair * LANES, (pair + 2) * LANES)
-        lane = lax.broadcasted_iota(jnp.int32, (1, 2 * LANES), 1)
         begin = pair * (2 * HEAD_DIM - LANES)
-        mine = [(lane >= begin + h * HEAD_DIM) & (lane < begin + (h + 1) * HEAD_DIM) for h in range(2)]
-        zero = jnp.zeros((), bf16)
-        key, value = (
-            jnp.concatenate([jnp.where(own, ref[:, window], zero) for own in mine], axis=0)
-            for ref in (keys, values)
-        )
-        scores = lax.dot_general(
-            queries[:, window], key, (((1,), (1,)), ((), ())), preferred_element_type=f32
-        )
+        query = queries_t[window, :]
+        both = [
+            jnp.where((row >= begin + h * HEAD_DIM) & (row < begin + (h + 1) * HEAD_DIM), query, jnp.zeros((), bf16))
+            for h in range(2)
+        ]
+        scores = dot(keys[:, window], jnp.concatenate(both, axis=1))
         weights = []
         for h in range(2):
             part = jnp.exp2(scores[:, h * tokens : (h + 1) * tokens] * EXP2_SCALE) * same[...]
-            weights.append((part / jnp.sum(part, axis=-1, keepdims=True)).astype(bf16))
-        both = dot(jnp.concatenate(weights, axis=1), value)
-        first = both[:, :LANES]
-        if held is not None:
-            first = first + held
-        held = both[:, LANES:]
-        attended[:, pair * LANES : (pair + 1) * LANES] = first.astype(bf16)
-    attended[:, HEADS // 2 * LANES :] = held.astype(bf16)
-
-    copies[2].wait()
+            weights.append((part * (1.0 / jnp.sum(part, axis=0, keepdims=True))).astype(bf16))
+        features = slice(pair * 2 * HEAD_DIM, (pair + 1) * 2 * HEAD_DIM)
+        heads_out = dot(values_t[features, :], jnp.concatenate(weights, axis=1))
+        for h in range(2):
+            first = (2 * pair + h) * HEAD_DIM
+            attended_t[first : first + HEAD_DIM, :] = heads_out[
+                h * HEAD_DIM : (h + 1) * HEAD_DIM, h * tokens : (h + 1) * tokens
+            ]
+    attended[...] = attended_t[...].astype(bf16).T
+
+    copies[1].wait()
     branch = dot(attended[...], wout[...])
     o_ref[...] = (x_ref[...].astype(f32) + branch.reshape(x_ref.shape)).astype(bf16)
 
@@ -190,11 +184,13 @@
             pltpu.VMEM((tokens, model), f32),
             pltpu.VMEM((tokens, model), f32),
             pltpu.VMEM((tokens, model), bf16),
-            pltpu.VMEM((tokens, model), bf16),
-            pltpu.VMEM((tokens, model), bf16),
+            pltpu.VMEM((model, tokens), bf16),
+            pltpu.VMEM((tokens, model), bf16),
+            pltpu.VMEM((model, tokens), bf16),
+            pltpu.VMEM((model, tokens), f32),
             pltpu.VMEM((tokens, model), bf16),
             pltpu.VMEM((tokens, tokens), f32),
-            pltpu.SemaphoreType.DMA((3,)),
+            pltpu.SemaphoreType.DMA((2,)),
         ],
         compiler_params=pltpu.CompilerParams(vmem_limit_bytes=40 * 1024 * 1024),
         name="tokens",

time: 38.6 us -> 37.8 us (0.979)
  Pallas kernels: 8.02 us -> 7.14 us
    pallas_call x1, Pallas kernels: 6.18 us -> 5.3 us  [body(): pl.pallas_call(tokens_kernel, out_shape=jax.ShapeDtypeStruct(gathered.sha...]
where the time goes in v1:
time: 37.8 us; the launch traced here: 37.5 us
  blocking collectives  13.5 us (36%)
  waiting for transfers between devices  8.73 us (23%)
  starting transfers between devices  7.39 us (20%)
  Pallas kernels  7.14 us (19%)
  local copies, waits for them, and re-layouts  0.71 us (2%)
    all_to_all x1, blocking collectives, body(): return exchange(result).reshape(latent.shape)  13.5 us
    all_to_all x1, waiting for transfers between devices, body(): gathered = exchange(latent.reshape(device_count, per_peer, model))  8.73 us
    all_to_all x1, starting transfers between devices, body(): gathered = exchange(latent.reshape(device_count, per_peer, model))  7.39 us
    pallas_call x1, Pallas kernels, body(): pl.pallas_call(tokens_kernel, out_shape=jax.ShapeDtypeStruct(gathered.sha...  5.3 us
    pallas_call x1, Pallas kernels, body(): pl.pallas_call(held_kernel, out_shape=(pltpu.VMEM((8, model), f32), pltpu...  1.84 us
  transfers between devices with their start and end apart: 1, of which 1 were waited for; matrix products, arithmetic and copies ran while one was open for 0% of the time, Pallas kernels for 5%

profile of v1, /device:TPU:0, one launch (start us, length us, event | category | flops | bytes accessed | tf_op | source)
XLA Modules:
  0.0 37.5 jit_solution(11522742314454861939)
XLA Ops:
  0.0 7.4 %all-to-all-start = ((bf16[16,8,1152]{2,1,0:T(8,128)(2,1)}), bf16[16,8,1152]{2,1,0:T(8,128)(2,1)S(1)}, u32[]{:S(2)}, u32[]{:S(2)}) async-start(bf16[16,8,1152]{2,1,0:T(8,128)(2,1)} %bitcast.3), calls=%async_computation | async-start | bytes 589824 | tf_op jit(solution)/shard_map/all_to_all | solution.py:150
  7.4 1.8 %held.1 = (f32[8,1152]{1,0:T(8,128)S(1)}, bf16[1152,128]{1,0:T(8,128)(2,1)S(1)}, bf16[32,1152]{1,0:T(8,128)(2,1)S(1)}, bf16[1152,1152]{1,0:T(8,128)(2,1)S(1)}) custom-call(f32[1152]{0:T(1024)} %ln_ref.1, f32[72]{0:T(128)} %qg_ref.1, f32[72]{0:T(128)} %kg_ref.1, bf16[1152,3456]{1,0:T(8,128)(2,1)} %wqkv_hbm.1), custom_call_target="tpu_custom_call" | custom-call | bytes 5308416 | tf_op jit(solution)/shard_map/held/pallas_call | solution.py:155
  9.2 8.7 %all-to-all-done.x_ref = bf16[16,8,1152]{2,1,0:T(8,128)(2,1)S(1)} async-done(((bf16[16,8,1152]{2,1,0:T(8,128)(2,1)}), bf16[16,8,1152]{2,1,0:T(8,128)(2,1)S(1)}, u32[]{:S(2)}, u32[]{:S(2)}) %all-to-all-start) | async-done | bytes 294944 | tf_op jit(solution)/shard_map/all_to_all | solution.py:150
  18.0 5.3 %tokens.1 = bf16[16,8,1152]{2,1,0:T(8,128)(2,1)S(1)} custom-call(bf16[16,8,1152]{2,1,0:T(8,128)(2,1)S(1)} %all-to-all-done.x_ref, f32[8,1152]{1,0:T(8,128)S(1)} %get-tuple-element.9.gains_ref, bf16[1152,128]{1,0:T(8,128)(2,1)S(1)} %get-tuple-element.10.member_ref, bf16[32,1152]{1,0:T(8,128)(2,1)S(1)} %get-tuple-element.11.spread_ref, ...), custom_call_target="tpu_custom_call" | custom-call | tf_op jit(solution)/shard_map/tokens/pallas_call | solution.py:175
  23.3 13.5 %all_to_all.10 = bf16[16,8,1152]{2,1,0:T(8,128)(2,1)S(1)} all-to-all(bf16[16,8,1152]{2,1,0:T(8,128)(2,1)S(1)} %tokens.1), channel_id=1, replica_groups=mesh['groups'=2,'frame'=16] {'frame'}, dimensions={0} | all-to-all | bytes 589824 | tf_op jit(solution)/shard_map/all_to_all | solution.py:198
  36.8 0.7 %copy.8 = bf16[4,32,1152]{2,1,0:T(8,128)(2,1)} copy(bf16[4,32,1152]{2,1,0:T(8,128)(2,1)S(1)} %bitcast.2) | data formatting | bytes 589824
Async XLA Ops:
  0.0 18.0 %all-to-all-start = ((bf16[16,8,1152]{2,1,0:T(8,128)(2,1)}), bf16[16,8,1152]{2,1,0:T(8,128)(2,1)S(1)}, u32[]{:S(2)}, u32[]{:S(2)}) async-start(bf16[16,8,1152]{2,1,0:T(8,128)(2,1)} %bitcast.3), calls=%async_computation | async-start | bytes 589824 | tf_op jit(solution)/shard_map/all_to_all | solution.py:150

commit v2 on v1

--- a/solution.py
+++ b/solution.py
@@ -72,7 +72,11 @@
     tokens = frames * positions
     bf16, f32 = jnp.bfloat16, jnp.float32
 
-    pairs = [(wqkv_hbm.at[:, pl.ds(width, 2 * width)], wkv), (wout_hbm, wout)]
+    pairs = [
+        (wqkv_hbm.at[:, pl.ds(width, width)], wkv.at[:, pl.ds(0, width)]),
+        (wqkv_hbm.at[:, pl.ds(2 * width, width)], wkv.at[:, pl.ds(width, width)]),
+        (wout_hbm, wout),
+    ]
     copies = [pltpu.make_async_copy(src, dst, sems.at[i]) for i, (src, dst) in enumerate(pairs)]
     copies[0].start()
 
@@ -102,10 +106,12 @@
     mixed_q[...] = dot(normed[...], wq[...])
     head_norm(mixed_q, 1, queries)
     copies[0].wait()
+    copies[2].start()
     mixed_k[...] = dot(normed[...], wkv[:, :width])
     queries_t[...] = queries[...].T
+    head_norm(mixed_k, 2, keys)
+    copies[1].wait()
     values_t[...] = dot(normed[...], wkv[:, width:]).astype(bf16).T
-    head_norm(mixed_k, 2, keys)
 
     place = lax.broadcasted_iota(jnp.int32, (tokens, tokens), 0) % positions
     other = lax.broadcasted_iota(jnp.int32, (tokens, tokens), 1) % positions
@@ -134,7 +140,7 @@
             ]
     attended[...] = attended_t[...].astype(bf16).T
 
-    copies[1].wait()
+    copies[2].wait()
     branch = dot(attended[...], wout[...])
     o_ref[...] = (x_ref[...].astype(f32) + branch.reshape(x_ref.shape)).astype(bf16)
 
@@ -190,7 +196,7 @@
             pltpu.VMEM((model, tokens), f32),
             pltpu.VMEM((tokens, model), bf16),
             pltpu.VMEM((tokens, tokens), f32),
-            pltpu.SemaphoreType.DMA((2,)),
+            pltpu.SemaphoreType.DMA((3,)),
         ],
         compiler_params=pltpu.CompilerParams(vmem_limit_bytes=40 * 1024 * 1024),
         name="tokens",

time: 37.8 us -> 37.1 us (0.981)
  Pallas kernels: 7.14 us -> 6.5 us
    pallas_call x1, Pallas kernels: 5.3 us -> 4.66 us  [body(): pl.pallas_call(tokens_kernel, out_shape=jax.ShapeDtypeStruct(gathered.sha...]
where the time goes in v2:
time: 37.1 us; the launch traced here: 36.8 us
  blocking collectives  13.5 us (36%)
  waiting for transfers between devices  8.73 us (24%)
  starting transfers between devices  7.39 us (20%)
  Pallas kernels  6.5 us (18%)
  local copies, waits for them, and re-layouts  0.71 us (2%)
    all_to_all x1, blocking collectives, body(): return exchange(result).reshape(latent.shape)  13.5 us
    all_to_all x1, waiting for transfers between devices, body(): gathered = exchange(latent.reshape(device_count, per_peer, model))  8.73 us
    all_to_all x1, starting transfers between devices, body(): gathered = exchange(latent.reshape(device_count, per_peer, model))  7.39 us
    pallas_call x1, Pallas kernels, body(): pl.pallas_call(tokens_kernel, out_shape=jax.ShapeDtypeStruct(gathered.sha...  4.66 us
    pallas_call x1, Pallas kernels, body(): pl.pallas_call(held_kernel, out_shape=(pltpu.VMEM((8, model), f32), pltpu...  1.84 us
  transfers between devices with their start and end apart: 1, of which 1 were waited for; matrix products, arithmetic and copies ran while one was open for 0% of the time, Pallas kernels for 5%

profile of v2, /device:TPU:0, one launch (start us, length us, event | category | flops | bytes accessed | tf_op | source)
XLA Modules:
  0.0 36.8 jit_solution(2601905959494367092)
XLA Ops:
  0.0 7.4 %all-to-all-start = ((bf16[16,8,1152]{2,1,0:T(8,128)(2,1)}), bf16[16,8,1152]{2,1,0:T(8,128)(2,1)S(1)}, u32[]{:S(2)}, u32[]{:S(2)}) async-start(bf16[16,8,1152]{2,1,0:T(8,128)(2,1)} %bitcast.3), calls=%async_computation | async-start | bytes 589824 | tf_op jit(solution)/shard_map/all_to_all | solution.py:156
  7.4 1.8 %held.1 = (f32[8,1152]{1,0:T(8,128)S(1)}, bf16[1152,128]{1,0:T(8,128)(2,1)S(1)}, bf16[32,1152]{1,0:T(8,128)(2,1)S(1)}, bf16[1152,1152]{1,0:T(8,128)(2,1)S(1)}) custom-call(f32[1152]{0:T(1024)} %ln_ref.1, f32[72]{0:T(128)} %qg_ref.1, f32[72]{0:T(128)} %kg_ref.1, bf16[1152,3456]{1,0:T(8,128)(2,1)} %wqkv_hbm.1), custom_call_target="tpu_custom_call" | custom-call | bytes 5308416 | tf_op jit(solution)/shard_map/held/pallas_call | solution.py:161
  9.2 8.7 %all-to-all-done.x_ref = bf16[16,8,1152]{2,1,0:T(8,128)(2,1)S(1)} async-done(((bf16[16,8,1152]{2,1,0:T(8,128)(2,1)}), bf16[16,8,1152]{2,1,0:T(8,128)(2,1)S(1)}, u32[]{:S(2)}, u32[]{:S(2)}) %all-to-all-start) | async-done | bytes 294944 | tf_op jit(solution)/shard_map/all_to_all | solution.py:156
  18.0 4.7 %tokens.1 = bf16[16,8,1152]{2,1,0:T(8,128)(2,1)S(1)} custom-call(bf16[16,8,1152]{2,1,0:T(8,128)(2,1)S(1)} %all-to-all-done.x_ref, f32[8,1152]{1,0:T(8,128)S(1)} %get-tuple-element.9.gains_ref, bf16[1152,128]{1,0:T(8,128)(2,1)S(1)} %get-tuple-element.10.member_ref, bf16[32,1152]{1,0:T(8,128)(2,1)S(1)} %get-tuple-element.11.spread_ref, ...), custom_call_target="tpu_custom_call" | custom-call | tf_op jit(solution)/shard_map/tokens/pallas_call | solution.py:181
  22.6 13.5 %all_to_all.10 = bf16[16,8,1152]{2,1,0:T(8,128)(2,1)S(1)} all-to-all(bf16[16,8,1152]{2,1,0:T(8,128)(2,1)S(1)} %tokens.1), channel_id=1, replica_groups=mesh['groups'=2,'frame'=16] {'frame'}, dimensions={0} | all-to-all | bytes 589824 | tf_op jit(solution)/shard_map/all_to_all | solution.py:204
  36.1 0.7 %copy.8 = bf16[4,32,1152]{2,1,0:T(8,128)(2,1)} copy(bf16[4,32,1152]{2,1,0:T(8,128)(2,1)S(1)} %bitcast.2) | data formatting | bytes 589824
Async XLA Ops:
  0.0 18.0 %all-to-all-start = ((bf16[16,8,1152]{2,1,0:T(8,128)(2,1)}), bf16[16,8,1152]{2,1,0:T(8,128)(2,1)S(1)}, u32[]{:S(2)}, u32[]{:S(2)}) async-start(bf16[16,8,1152]{2,1,0:T(8,128)(2,1)} %bitcast.3), calls=%async_computation | async-start | bytes 589824 | tf_op jit(solution)/shard_map/all_to_all | solution.py:156

commit v3 on v2

--- a/solution.py
+++ b/solution.py
@@ -19,37 +19,26 @@
     return jnp.dot(a, b, preferred_element_type=jnp.float32)
 
 
-def held_kernel(
-    ln_ref, qg_ref, kg_ref, wqkv_ref, gains_out, member_out, spread_out, wq_out, ln, qg, kg, sems
-):
+def held_kernel(ln_ref, qg_ref, kg_ref, wqkv_ref, gain_out, head_gains_out, wq_out, ln, qg, kg, sems):
     width = wq_out.shape[1]
     pairs = [(ln_ref, ln), (qg_ref, qg), (kg_ref, kg), (wqkv_ref.at[:, pl.ds(0, width)], wq_out)]
     copies = [pltpu.make_async_copy(src, dst, sems.at[i]) for i, (src, dst) in enumerate(pairs)]
     for copy in copies:
         copy.start()
-
-    def belongs(feature, lane):
-        head = jnp.where(lane >= HEADS, lane - HEADS, lane)
-        first = head * HEAD_DIM
-        held = (feature >= first) & (feature < first + HEAD_DIM) & (lane < 2 * HEADS)
-        return held.astype(jnp.float32).astype(jnp.bfloat16)
-
-    for out, axis in ((member_out, 0), (spread_out, 1)):
-        feature = lax.broadcasted_iota(jnp.int32, out.shape, axis)
-        out[...] = belongs(feature, lax.broadcasted_iota(jnp.int32, out.shape, 1 - axis))
     for copy in copies[:3]:
         copy.wait()
-    gains_out[0:1, :] = ln[...].reshape(1, width)
-    gains_out[1:2, :] = jnp.concatenate([qg[...].reshape(1, HEAD_DIM)] * HEADS, axis=1)
-    gains_out[2:3, :] = jnp.concatenate([kg[...].reshape(1, HEAD_DIM)] * HEADS, axis=1)
+    gain_out[...] = ln[...].reshape(1, width)
+    for i, held in enumerate((qg, kg)):
+        row = held[...].reshape(1, HEAD_DIM)
+        row = jnp.concatenate([row, jnp.zeros((1, LANES - HEAD_DIM), jnp.float32)], axis=1)
+        head_gains_out[i] = jnp.broadcast_to(row, (LANES, LANES)).T[:HEAD_DIM]
     copies[3].wait()
 
 
 def tokens_kernel(
     x_ref,
-    gains_ref,
-    member_ref,
-    spread_ref,
+    gain_ref,
+    head_gains_ref,
     wq,
     wqkv_hbm,
     wout_hbm,
@@ -57,10 +46,9 @@
     wkv,
     wout,
     normed,
-    mixed_q,
-    mixed_k,
-    queries,
+    mixed,
     queries_t,
+    keys_t,
     keys,
     values_t,
     attended_t,
@@ -80,7 +68,7 @@
     copies = [pltpu.make_async_copy(src, dst, sems.at[i]) for i, (src, dst) in enumerate(pairs)]
     copies[0].start()
 
-    gain = gains_ref[0:1, :]
+    gain = gain_ref[...]
     step = max(1, 16 // positions)
     for frame in range(0, frames, step):
         x = x_ref[frame : frame + step].astype(f32).reshape(step * positions, width)
@@ -89,27 +77,25 @@
         rows = slice(frame * positions, (frame + step) * positions)
         normed[rows, :] = (center * lax.rsqrt(spread + EPS) * gain).astype(bf16)
 
-    def head_norm(mixed, row, out):
-        squares = mixed[...] * mixed[...]
-        high = squares.astype(bf16)
-        low = (squares - high.astype(f32)).astype(bf16)
-        total = dot(jnp.concatenate([high, low], axis=0), member_ref[...])
-        total = total[:tokens] + total[tokens:]
-        inverse = lax.rsqrt(total * (1.0 / HEAD_DIM) + EPS)
-        high = inverse.astype(bf16)
-        low = (inverse - high.astype(f32)).astype(bf16)
-        lane = lax.broadcasted_iota(jnp.int32, inverse.shape, 1)
-        parts = jnp.where(lane < HEADS, high, low)[:, : 2 * HEADS]
-        out[...] = (mixed[...] * dot(parts, spread_ref[...]) * gains_ref[row : row + 1, :]).astype(bf16)
+    def head_norm(mixed, which):
+        for pair in range(HEADS // 2):
+            heads = []
+            for first in (2 * pair * HEAD_DIM, (2 * pair + 1) * HEAD_DIM):
+                head = mixed[first : first + HEAD_DIM, :]
+                total = jnp.sum(head * head, axis=0, keepdims=True)
+                heads.append(head * lax.rsqrt(total * (1.0 / HEAD_DIM) + EPS) * head_gains_ref[which])
+            yield slice(2 * pair * HEAD_DIM, (2 * pair + 2) * HEAD_DIM), jnp.concatenate(heads, axis=0).astype(bf16)
 
     copies[1].start()
-    mixed_q[...] = dot(normed[...], wq[...])
-    head_norm(mixed_q, 1, queries)
+    mixed[...] = dot(normed[...], wq[...]).T
+    for rows, heads in head_norm(mixed, 0):
+        queries_t[rows, :] = heads
     copies[0].wait()
     copies[2].start()
-    mixed_k[...] = dot(normed[...], wkv[:, :width])
-    queries_t[...] = queries[...].T
-    head_norm(mixed_k, 2, keys)
+    mixed[...] = dot(normed[...], wkv[:, :width]).T
+    for rows, heads in head_norm(mixed, 1):
+        keys_t[rows, :] = heads
+    keys[...] = keys_t[...].T
     copies[1].wait()
     values_t[...] = dot(normed[...], wkv[:, width:]).astype(bf16).T
 
@@ -158,16 +144,15 @@
     in_hbm = pl.BlockSpec(memory_space=pltpu.HBM)
     bf16, f32 = jnp.bfloat16, jnp.float32
     held = [pltpu.with_memory_space_constraint(a, pltpu.HBM) for a in (ln_gain, q_gain, k_gain, w_qkv, w_out)]
-    gains, member, spread, wq = pl.pallas_call(
+    gain, head_gains, wq = pl.pallas_call(
         held_kernel,
         out_shape=(
-            pltpu.VMEM((8, model), f32),
-            pltpu.VMEM((model, LANES), bf16),
-            pltpu.VMEM((2 * HEADS, model), bf16),
+            pltpu.VMEM((1, model), f32),
+            pltpu.VMEM((2, HEAD_DIM, LANES), f32),
             pltpu.VMEM((model, model), bf16),
         ),
         in_specs=[in_hbm] * 4,
-        out_specs=[in_vmem] * 4,
+        out_specs=[in_vmem] * 3,
         scratch_shapes=[
             pltpu.VMEM((model,), f32),
             pltpu.VMEM((HEAD_DIM,), f32),
@@ -181,15 +166,14 @@
     result = pl.pallas_call(
         tokens_kernel,
         out_shape=jax.ShapeDtypeStruct(gathered.shape, bf16),
-        in_specs=[in_vmem] * 5 + [in_hbm] * 2,
+        in_specs=[in_vmem] * 4 + [in_hbm] * 2,
         out_specs=in_vmem,
         scratch_shapes=[
             pltpu.VMEM((model, 2 * model), bf16),
             pltpu.VMEM(w_out.shape, bf16),
             pltpu.VMEM((tokens, model), bf16),
-            pltpu.VMEM((tokens, model), f32),
-            pltpu.VMEM((tokens, model), f32),
-            pltpu.VMEM((tokens, model), bf16),
+            pltpu.VMEM((model, tokens), f32),
+            pltpu.VMEM((model, tokens), bf16),
             pltpu.VMEM((model, tokens), bf16),
             pltpu.VMEM((tokens, model), bf16),
             pltpu.VMEM((model, tokens), bf16),
@@ -200,7 +184,7 @@
         ],
         compiler_params=pltpu.CompilerParams(vmem_limit_bytes=40 * 1024 * 1024),
         name="tokens",
-    )(gathered, gains, member, spread, wq, *held[3:])
+    )(gathered, gain, head_gains, wq, *held[3:])
     return exchange(result).reshape(latent.shape)
 
 

time: 37.1 us -> 37.4 us (level)
  no operation moved by 1% of the time
where the time goes in v3:
time: 37.4 us; the launch traced here: 37.1 us
  blocking collectives  13.5 us (36%)
  waiting for transfers between devices  8.73 us (23%)
  starting transfers between devices  7.39 us (20%)
  Pallas kernels  6.71 us (18%)
  local copies, waits for them, and re-layouts  0.71 us (2%)
    all_to_all x1, blocking collectives, body(): return exchange(result).reshape(latent.shape)  13.5 us
    all_to_all x1, waiting for transfers between devices, body(): gathered = exchange(latent.reshape(device_count, per_peer, model))  8.73 us
    all_to_all x1, starting transfers between devices, body(): gathered = exchange(latent.reshape(device_count, per_peer, model))  7.39 us
    pallas_call x1, Pallas kernels, body(): pl.pallas_call(tokens_kernel, out_shape=jax.ShapeDtypeStruct(gathered.sha...  4.88 us
    pallas_call x1, Pallas kernels, body(): pl.pallas_call(held_kernel, out_shape=(pltpu.VMEM((1, model), f32), pltpu...  1.84 us
  transfers between devices with their start and end apart: 1, of which 1 were waited for; matrix products, arithmetic and copies ran while one was open for 0% of the time, Pallas kernels for 5%

profile of v3, /device:TPU:0, one launch (start us, length us, event | category | flops | bytes accessed | tf_op | source)
XLA Modules:
  0.0 37.1 jit_solution(760615524465750539)
XLA Ops:
  0.0 7.4 %all-to-all-start = ((bf16[16,8,1152]{2,1,0:T(8,128)(2,1)}), bf16[16,8,1152]{2,1,0:T(8,128)(2,1)S(1)}, u32[]{:S(2)}, u32[]{:S(2)}) async-start(bf16[16,8,1152]{2,1,0:T(8,128)(2,1)} %bitcast.3), calls=%async_computation | async-start | bytes 589824 | tf_op jit(solution)/shard_map/all_to_all | solution.py:142
  7.4 1.8 %held.1 = (f32[1,1152]{1,0:T(1,128)S(1)}, f32[2,72,128]{2,1,0:T(8,128)S(1)}, bf16[1152,1152]{1,0:T(8,128)(2,1)S(1)}) custom-call(f32[1152]{0:T(1024)} %ln_ref.1, f32[72]{0:T(128)} %qg_ref.1, f32[72]{0:T(128)} %kg_ref.1, bf16[1152,3456]{1,0:T(8,128)(2,1)} %wqkv_hbm.1), custom_call_target="tpu_custom_call" | custom-call | bytes 5308416 | tf_op jit(solution)/shard_map/held/pallas_call | solution.py:147
  9.2 8.7 %all-to-all-done.x_ref = bf16[16,8,1152]{2,1,0:T(8,128)(2,1)S(1)} async-done(((bf16[16,8,1152]{2,1,0:T(8,128)(2,1)}), bf16[16,8,1152]{2,1,0:T(8,128)(2,1)S(1)}, u32[]{:S(2)}, u32[]{:S(2)}) %all-to-all-start) | async-done | bytes 294944 | tf_op jit(solution)/shard_map/all_to_all | solution.py:142
  18.0 4.9 %tokens.1 = bf16[16,8,1152]{2,1,0:T(8,128)(2,1)S(1)} custom-call(bf16[16,8,1152]{2,1,0:T(8,128)(2,1)S(1)} %all-to-all-done.x_ref, f32[1,1152]{1,0:T(1,128)S(1)} %get-tuple-element.8.gain_ref, f32[2,72,128]{2,1,0:T(8,128)S(1)} %get-tuple-element.9.head_gains_ref, bf16[1152,1152]{1,0:T(8,128)(2,1)S(1)} %get-tuple-element.10.wq, bf16[1152,3456]{1,0:T(8,128)(2,1)} %wqkv_hbm.1, ...), custom_call_target="tpu_custom_call" | custom-call | tf_op jit(solution)/shard_map/tokens/pallas_call | solution.py:166
  22.9 13.5 %all_to_all.10 = bf16[16,8,1152]{2,1,0:T(8,128)(2,1)S(1)} all-to-all(bf16[16,8,1152]{2,1,0:T(8,128)(2,1)S(1)} %tokens.1), channel_id=1, replica_groups=mesh['groups'=2,'frame'=16] {'frame'}, dimensions={0} | all-to-all | bytes 589824 | tf_op jit(solution)/shard_map/all_to_all | solution.py:188
  36.3 0.7 %copy.8 = bf16[4,32,1152]{2,1,0:T(8,128)(2,1)} copy(bf16[4,32,1152]{2,1,0:T(8,128)(2,1)S(1)} %bitcast.2) | data formatting | bytes 589824
Async XLA Ops:
  0.0 18.0 %all-to-all-start = ((bf16[16,8,1152]{2,1,0:T(8,128)(2,1)}), bf16[16,8,1152]{2,1,0:T(8,128)(2,1)S(1)}, u32[]{:S(2)}, u32[]{:S(2)}) async-start(bf16[16,8,1152]{2,1,0:T(8,128)(2,1)} %bitcast.3), calls=%async_computation | async-start | bytes 589824 | tf_op jit(solution)/shard_map/all_to_all | solution.py:142

commit v4 on v2

--- a/solution.py
+++ b/solution.py
@@ -150,8 +150,10 @@
     rows, columns, model = latent.shape
     tokens = rows * columns
     per_peer = tokens // device_count
+    half = device_count // 2
+    order = [part * half + i for i in range(half) for part in range(2)]
     exchange = functools.partial(
-        lax.all_to_all, axis_name="frame", split_axis=0, concat_axis=0, tiled=True
+        lax.all_to_all, axis_name="frame", split_axis=0, concat_axis=0, axis_index_groups=[order], tiled=True
     )
     gathered = exchange(latent.reshape(device_count, per_peer, model))
     in_vmem = pl.BlockSpec(memory_space=pltpu.VMEM)

time: 37.1 us -> 37.6 us (1.013)
  no operation moved by 1% of the time
where the time goes in v4:
time: 37.6 us; the launch traced here: 37.3 us
  blocking collectives  13.7 us (36%)
  waiting for transfers between devices  9.01 us (24%)
  starting transfers between devices  7.39 us (20%)
  Pallas kernels  6.5 us (17%)
  local copies, waits for them, and re-layouts  0.71 us (2%)
    all_to_all x1, blocking collectives, body(): return exchange(result).reshape(latent.shape)  13.7 us
    all_to_all x1, waiting for transfers between devices, body(): gathered = exchange(latent.reshape(device_count, per_peer, model))  9.01 us
    all_to_all x1, starting transfers between devices, body(): gathered = exchange(latent.reshape(device_count, per_peer, model))  7.39 us
    pallas_call x1, Pallas kernels, body(): pl.pallas_call(tokens_kernel, out_shape=jax.ShapeDtypeStruct(gathered.sha...  4.66 us
    pallas_call x1, Pallas kernels, body(): pl.pallas_call(held_kernel, out_shape=(pltpu.VMEM((8, model), f32), pltpu...  1.84 us
  transfers between devices with their start and end apart: 1, of which 1 were waited for; matrix products, arithmetic and copies ran while one was open for 0% of the time, Pallas kernels for 5%

profile of v4, /device:TPU:0, one launch (start us, length us, event | category | flops | bytes accessed | tf_op | source)
XLA Modules:
  0.0 37.3 jit_solution(17447049760713509731)
XLA Ops:
  0.0 7.4 %all-to-all-start = ((bf16[16,8,1152]{2,1,0:T(8,128)(2,1)}), bf16[16,8,1152]{2,1,0:T(8,128)(2,1)S(1)}, u32[]{:S(2)}, u32[]{:S(2)}) async-start(bf16[16,8,1152]{2,1,0:T(8,128)(2,1)} %bitcast.3), calls=%async_computation | async-start | bytes 589824 | tf_op jit(solution)/shard_map/all_to_all | solution.py:158
  7.4 1.8 %held.1 = (f32[8,1152]{1,0:T(8,128)S(1)}, bf16[1152,128]{1,0:T(8,128)(2,1)S(1)}, bf16[32,1152]{1,0:T(8,128)(2,1)S(1)}, bf16[1152,1152]{1,0:T(8,128)(2,1)S(1)}) custom-call(f32[1152]{0:T(1024)} %ln_ref.1, f32[72]{0:T(128)} %qg_ref.1, f32[72]{0:T(128)} %kg_ref.1, bf16[1152,3456]{1,0:T(8,128)(2,1)} %wqkv_hbm.1), custom_call_target="tpu_custom_call" | custom-call | bytes 5308416 | tf_op jit(solution)/shard_map/held/pallas_call | solution.py:163
  9.2 9.0 %all-to-all-done.x_ref = bf16[16,8,1152]{2,1,0:T(8,128)(2,1)S(1)} async-done(((bf16[16,8,1152]{2,1,0:T(8,128)(2,1)}), bf16[16,8,1152]{2,1,0:T(8,128)(2,1)S(1)}, u32[]{:S(2)}, u32[]{:S(2)}) %all-to-all-start) | async-done | bytes 294944 | tf_op jit(solution)/shard_map/all_to_all | solution.py:158
  18.2 4.7 %tokens.1 = bf16[16,8,1152]{2,1,0:T(8,128)(2,1)S(1)} custom-call(bf16[16,8,1152]{2,1,0:T(8,128)(2,1)S(1)} %all-to-all-done.x_ref, f32[8,1152]{1,0:T(8,128)S(1)} %get-tuple-element.9.gains_ref, bf16[1152,128]{1,0:T(8,128)(2,1)S(1)} %get-tuple-element.10.member_ref, bf16[32,1152]{1,0:T(8,128)(2,1)S(1)} %get-tuple-element.11.spread_ref, ...), custom_call_target="tpu_custom_call" | custom-call | tf_op jit(solution)/shard_map/tokens/pallas_call | solution.py:183
  22.9 13.7 %all_to_all.10 = bf16[16,8,1152]{2,1,0:T(8,128)(2,1)S(1)} all-to-all(bf16[16,8,1152]{2,1,0:T(8,128)(2,1)S(1)} %tokens.1), channel_id=1, replica_groups={{0,8,1,9,2,10,3,11,4,12,5,13,6,14,7,15},{16,24,17,25,18,26,19,27,20,28,..., dimensions={0} | all-to-all | bytes 589824 | tf_op jit(solution)/shard_map/all_to_all | solution.py:206
  36.6 0.7 %copy.8 = bf16[4,32,1152]{2,1,0:T(8,128)(2,1)} copy(bf16[4,32,1152]{2,1,0:T(8,128)(2,1)S(1)} %bitcast.2) | data formatting | bytes 589824
Async XLA Ops:
  0.0 18.2 %all-to-all-start = ((bf16[16,8,1152]{2,1,0:T(8,128)(2,1)}), bf16[16,8,1152]{2,1,0:T(8,128)(2,1)S(1)}, u32[]{:S(2)}, u32[]{:S(2)}) async-start(bf16[16,8,1152]{2,1,0:T(8,128)(2,1)} %bitcast.3), calls=%async_computation | async-start | bytes 589824 | tf_op jit(solution)/shard_map/all_to_all | solution.py:158

commit v5 on v1

--- a/solution.py
+++ b/solution.py
@@ -72,7 +72,10 @@
     tokens = frames * positions
     bf16, f32 = jnp.bfloat16, jnp.float32
 
-    pairs = [(wqkv_hbm.at[:, pl.ds(width, 2 * width)], wkv), (wout_hbm, wout)]
+    cut = (width // LANES + 1) // 2 * LANES
+    bounds = [(0, cut), (cut, width), (width, 2 * width)]
+    pairs = [(wqkv_hbm.at[:, pl.ds(width + a, b - a)], wkv.at[:, pl.ds(a, b - a)]) for a, b in bounds]
+    pairs += [(wout_hbm, wout)]
     copies = [pltpu.make_async_copy(src, dst, sems.at[i]) for i, (src, dst) in enumerate(pairs)]
     copies[0].start()
 
@@ -100,10 +103,15 @@
 
     copies[1].start()
     mixed_q[...] = dot(normed[...], wq[...])
+    copies[0].wait()
+    copies[2].start()
+    mixed_k[:, :cut] = dot(normed[...], wkv[:, :cut])
     head_norm(mixed_q, 1, queries)
-    copies[0].wait()
-    mixed_k[...] = dot(normed[...], wkv[:, :width])
+    copies[1].wait()
+    copies[3].start()
+    mixed_k[:, cut:] = dot(normed[...], wkv[:, cut:width])
     queries_t[...] = queries[...].T
+    copies[2].wait()
     values_t[...] = dot(normed[...], wkv[:, width:]).astype(bf16).T
     head_norm(mixed_k, 2, keys)
 
@@ -134,7 +142,7 @@
             ]
     attended[...] = attended_t[...].astype(bf16).T
 
-    copies[1].wait()
+    copies[3].wait()
     branch = dot(attended[...], wout[...])
     o_ref[...] = (x_ref[...].astype(f32) + branch.reshape(x_ref.shape)).astype(bf16)
 
@@ -190,7 +198,7 @@
             pltpu.VMEM((model, tokens), f32),
             pltpu.VMEM((tokens, model), bf16),
             pltpu.VMEM((tokens, tokens), f32),
-            pltpu.SemaphoreType.DMA((2,)),
+            pltpu.SemaphoreType.DMA((4,)),
         ],
         compiler_params=pltpu.CompilerParams(vmem_limit_bytes=40 * 1024 * 1024),
         name="tokens",

time: 37.8 us -> 38.1 us (level)
  no operation moved by 1% of the time
where the time goes in v5:
time: 38.1 us; the launch traced here: 37.8 us
  blocking collectives  13.5 us (35%)
  waiting for transfers between devices  8.73 us (23%)
  Pallas kernels  7.42 us (19%)
  starting transfers between devices  7.39 us (19%)
  local copies, waits for them, and re-layouts  0.71 us (2%)
    all_to_all x1, blocking collectives, body(): return exchange(result).reshape(latent.shape)  13.5 us
    all_to_all x1, waiting for transfers between devices, body(): gathered = exchange(latent.reshape(device_count, per_peer, model))  8.73 us
    all_to_all x1, starting transfers between devices, body(): gathered = exchange(latent.reshape(device_count, per_peer, model))  7.39 us
    pallas_call x1, Pallas kernels, body(): pl.pallas_call(tokens_kernel, out_shape=jax.ShapeDtypeStruct(gathered.sha...  5.59 us
    pallas_call x1, Pallas kernels, body(): pl.pallas_call(held_kernel, out_shape=(pltpu.VMEM((8, model), f32), pltpu...  1.84 us
  transfers between devices with their start and end apart: 1, of which 1 were waited for; matrix products, arithmetic and copies ran while one was open for 0% of the time, Pallas kernels for 5%

profile of v5, /device:TPU:0, one launch (start us, length us, event | category | flops | bytes accessed | tf_op | source)
XLA Modules:
  0.0 37.8 jit_solution(12964812318362211485)
XLA Ops:
  0.0 7.4 %all-to-all-start = ((bf16[16,8,1152]{2,1,0:T(8,128)(2,1)}), bf16[16,8,1152]{2,1,0:T(8,128)(2,1)S(1)}, u32[]{:S(2)}, u32[]{:S(2)}) async-start(bf16[16,8,1152]{2,1,0:T(8,128)(2,1)} %bitcast.3), calls=%async_computation | async-start | bytes 589824 | tf_op jit(solution)/shard_map/all_to_all | solution.py:158
  7.4 1.8 %held.1 = (f32[8,1152]{1,0:T(8,128)S(1)}, bf16[1152,128]{1,0:T(8,128)(2,1)S(1)}, bf16[32,1152]{1,0:T(8,128)(2,1)S(1)}, bf16[1152,1152]{1,0:T(8,128)(2,1)S(1)}) custom-call(f32[1152]{0:T(1024)} %ln_ref.1, f32[72]{0:T(128)} %qg_ref.1, f32[72]{0:T(128)} %kg_ref.1, bf16[1152,3456]{1,0:T(8,128)(2,1)} %wqkv_hbm.1), custom_call_target="tpu_custom_call" | custom-call | bytes 5308416 | tf_op jit(solution)/shard_map/held/pallas_call | solution.py:163
  9.2 8.7 %all-to-all-done.x_ref = bf16[16,8,1152]{2,1,0:T(8,128)(2,1)S(1)} async-done(((bf16[16,8,1152]{2,1,0:T(8,128)(2,1)}), bf16[16,8,1152]{2,1,0:T(8,128)(2,1)S(1)}, u32[]{:S(2)}, u32[]{:S(2)}) %all-to-all-start) | async-done | bytes 294944 | tf_op jit(solution)/shard_map/all_to_all | solution.py:158
  18.0 5.6 %tokens.1 = bf16[16,8,1152]{2,1,0:T(8,128)(2,1)S(1)} custom-call(bf16[16,8,1152]{2,1,0:T(8,128)(2,1)S(1)} %all-to-all-done.x_ref, f32[8,1152]{1,0:T(8,128)S(1)} %get-tuple-element.9.gains_ref, bf16[1152,128]{1,0:T(8,128)(2,1)S(1)} %get-tuple-element.10.member_ref, bf16[32,1152]{1,0:T(8,128)(2,1)S(1)} %get-tuple-element.11.spread_ref, ...), custom_call_target="tpu_custom_call" | custom-call | tf_op jit(solution)/shard_map/tokens/pallas_call | solution.py:183
  23.6 13.5 %all_to_all.10 = bf16[16,8,1152]{2,1,0:T(8,128)(2,1)S(1)} all-to-all(bf16[16,8,1152]{2,1,0:T(8,128)(2,1)S(1)} %tokens.1), channel_id=1, replica_groups=mesh['groups'=2,'frame'=16] {'frame'}, dimensions={0} | all-to-all | bytes 589824 | tf_op jit(solution)/shard_map/all_to_all | solution.py:206
  37.0 0.7 %copy.8 = bf16[4,32,1152]{2,1,0:T(8,128)(2,1)} copy(bf16[4,32,1152]{2,1,0:T(8,128)(2,1)S(1)} %bitcast.2) | data formatting | bytes 589824
Async XLA Ops:
  0.0 18.0 %all-to-all-start = ((bf16[16,8,1152]{2,1,0:T(8,128)(2,1)}), bf16[16,8,1152]{2,1,0:T(8,128)(2,1)S(1)}, u32[]{:S(2)}, u32[]{:S(2)}) async-start(bf16[16,8,1152]{2,1,0:T(8,128)(2,1)} %bitcast.3), calls=%async_computation | async-start | bytes 589824 | tf_op jit(solution)/shard_map/all_to_all | solution.py:158

commit v6 on v2

--- a/solution.py
+++ b/solution.py
@@ -66,6 +66,8 @@
     attended_t,
     attended,
     same,
+    stacks,
+    weights,
     sems,
 ):
     frames, positions, width = x_ref.shape
@@ -105,34 +107,36 @@
     copies[1].start()
     mixed_q[...] = dot(normed[...], wq[...])
     head_norm(mixed_q, 1, queries)
+    queries_t[...] = queries[...].T
+
+    row = lax.broadcasted_iota(jnp.int32, (2 * LANES, tokens), 0)
+    for pair in range(HEADS // 2):
+        begin = pair * (2 * HEAD_DIM - LANES)
+        query = queries_t[pair * LANES : (pair + 2) * LANES, :]
+        for h in range(2):
+            mine = (row >= begin + h * HEAD_DIM) & (row < begin + (h + 1) * HEAD_DIM)
+            stacks[pair, :, h * tokens : (h + 1) * tokens] = jnp.where(mine, query, jnp.zeros((), bf16))
+
+    place = lax.broadcasted_iota(jnp.int32, (tokens, tokens), 0) % positions
+    other = lax.broadcasted_iota(jnp.int32, (tokens, tokens), 1) % positions
+    same[...] = (place == other).astype(f32)
+
     copies[0].wait()
     copies[2].start()
     mixed_k[...] = dot(normed[...], wkv[:, :width])
-    queries_t[...] = queries[...].T
     head_norm(mixed_k, 2, keys)
+
+    for pair in range(HEADS // 2):
+        scores = dot(keys[:, pair * LANES : (pair + 2) * LANES], stacks[pair])
+        for h in range(2):
+            lanes = slice(h * tokens, (h + 1) * tokens)
+            part = jnp.exp2(scores[:, lanes] * EXP2_SCALE) * same[...]
+            weights[pair, :, lanes] = (part * (1.0 / jnp.sum(part, axis=0, keepdims=True))).astype(bf16)
+
     copies[1].wait()
     values_t[...] = dot(normed[...], wkv[:, width:]).astype(bf16).T
-
-    place = lax.broadcasted_iota(jnp.int32, (tokens, tokens), 0) % positions
-    other = lax.broadcasted_iota(jnp.int32, (tokens, tokens), 1) % positions
-    same[...] = (place == other).astype(f32)
-
-    row = lax.broadcasted_iota(jnp.int32, (2 * LANES, tokens), 0)
     for pair in range(HEADS // 2):
-        window = slice(pair * LANES, (pair + 2) * LANES)
-        begin = pair * (2 * HEAD_DIM - LANES)
-        query = queries_t[window, :]
-        both = [
-            jnp.where((row >= begin + h * HEAD_DIM) & (row < begin + (h + 1) * HEAD_DIM), query, jnp.zeros((), bf16))
-            for h in range(2)
-        ]
-        scores = dot(keys[:, window], jnp.concatenate(both, axis=1))
-        weights = []
-        for h in range(2):
-            part = jnp.exp2(scores[:, h * tokens : (h + 1) * tokens] * EXP2_SCALE) * same[...]
-            weights.append((part * (1.0 / jnp.sum(part, axis=0, keepdims=True))).astype(bf16))
-        features = slice(pair * 2 * HEAD_DIM, (pair + 1) * 2 * HEAD_DIM)
-        heads_out = dot(values_t[features, :], jnp.concatenate(weights, axis=1))
+        heads_out = dot(values_t[pair * 2 * HEAD_DIM : (pair + 1) * 2 * HEAD_DIM, :], weights[pair])
         for h in range(2):
             first = (2 * pair + h) * HEAD_DIM
             attended_t[first : first + HEAD_DIM, :] = heads_out[
@@ -196,6 +200,8 @@
             pltpu.VMEM((model, tokens), f32),
             pltpu.VMEM((tokens, model), bf16),
             pltpu.VMEM((tokens, tokens), f32),
+            pltpu.VMEM((HEADS // 2, 2 * LANES, 2 * tokens), bf16),
+            pltpu.VMEM((HEADS // 2, tokens, 2 * tokens), bf16),
             pltpu.SemaphoreType.DMA((3,)),
         ],
         compiler_params=pltpu.CompilerParams(vmem_limit_bytes=40 * 1024 * 1024),

time: 37.1 us -> 37.6 us (1.013)
  Pallas kernels: 6.5 us -> 6.96 us
    pallas_call x1, Pallas kernels: 4.66 us -> 5.12 us  [body(): pl.pallas_call(tokens_kernel, out_shape=jax.ShapeDtypeStruct(gathered.sha...]
where the time goes in v6:
time: 37.6 us; the launch traced here: 37.3 us
  blocking collectives  13.5 us (36%)
  waiting for transfers between devices  8.73 us (23%)
  starting transfers between devices  7.39 us (20%)
  Pallas kernels  6.96 us (19%)
  local copies, waits for them, and re-layouts  0.71 us (2%)
    all_to_all x1, blocking collectives, body(): return exchange(result).reshape(latent.shape)  13.5 us
    all_to_all x1, waiting for transfers between devices, body(): gathered = exchange(latent.reshape(device_count, per_peer, model))  8.73 us
    all_to_all x1, starting transfers between devices, body(): gathered = exchange(latent.reshape(device_count, per_peer, model))  7.39 us
    pallas_call x1, Pallas kernels, body(): pl.pallas_call(tokens_kernel, out_shape=jax.ShapeDtypeStruct(gathered.sha...  5.12 us
    pallas_call x1, Pallas kernels, body(): pl.pallas_call(held_kernel, out_shape=(pltpu.VMEM((8, model), f32), pltpu...  1.84 us
  transfers between devices with their start and end apart: 1, of which 1 were waited for; matrix products, arithmetic and copies ran while one was open for 0% of the time, Pallas kernels for 5%

profile of v6, /device:TPU:0, one launch (start us, length us, event | category | flops | bytes accessed | tf_op | source)
XLA Modules:
  0.0 37.3 jit_solution(2645618668391654623)
XLA Ops:
  0.0 7.4 %all-to-all-start = ((bf16[16,8,1152]{2,1,0:T(8,128)(2,1)}), bf16[16,8,1152]{2,1,0:T(8,128)(2,1)S(1)}, u32[]{:S(2)}, u32[]{:S(2)}) async-start(bf16[16,8,1152]{2,1,0:T(8,128)(2,1)} %bitcast.3), calls=%async_computation | async-start | bytes 589824 | tf_op jit(solution)/shard_map/all_to_all | solution.py:160
  7.4 1.8 %held.1 = (f32[8,1152]{1,0:T(8,128)S(1)}, bf16[1152,128]{1,0:T(8,128)(2,1)S(1)}, bf16[32,1152]{1,0:T(8,128)(2,1)S(1)}, bf16[1152,1152]{1,0:T(8,128)(2,1)S(1)}) custom-call(f32[1152]{0:T(1024)} %ln_ref.1, f32[72]{0:T(128)} %qg_ref.1, f32[72]{0:T(128)} %kg_ref.1, bf16[1152,3456]{1,0:T(8,128)(2,1)} %wqkv_hbm.1), custom_call_target="tpu_custom_call" | custom-call | bytes 5308416 | tf_op jit(solution)/shard_map/held/pallas_call | solution.py:165
  9.2 8.7 %all-to-all-done.x_ref = bf16[16,8,1152]{2,1,0:T(8,128)(2,1)S(1)} async-done(((bf16[16,8,1152]{2,1,0:T(8,128)(2,1)}), bf16[16,8,1152]{2,1,0:T(8,128)(2,1)S(1)}, u32[]{:S(2)}, u32[]{:S(2)}) %all-to-all-start) | async-done | bytes 294944 | tf_op jit(solution)/shard_map/all_to_all | solution.py:160
  18.0 5.1 %tokens.1 = bf16[16,8,1152]{2,1,0:T(8,128)(2,1)S(1)} custom-call(bf16[16,8,1152]{2,1,0:T(8,128)(2,1)S(1)} %all-to-all-done.x_ref, f32[8,1152]{1,0:T(8,128)S(1)} %get-tuple-element.9.gains_ref, bf16[1152,128]{1,0:T(8,128)(2,1)S(1)} %get-tuple-element.10.member_ref, bf16[32,1152]{1,0:T(8,128)(2,1)S(1)} %get-tuple-element.11.spread_ref, ...), custom_call_target="tpu_custom_call" | custom-call | tf_op jit(solution)/shard_map/tokens/pallas_call | solution.py:185
  23.1 13.5 %all_to_all.10 = bf16[16,8,1152]{2,1,0:T(8,128)(2,1)S(1)} all-to-all(bf16[16,8,1152]{2,1,0:T(8,128)(2,1)S(1)} %tokens.1), channel_id=1, replica_groups=mesh['groups'=2,'frame'=16] {'frame'}, dimensions={0} | all-to-all | bytes 589824 | tf_op jit(solution)/shard_map/all_to_all | solution.py:210
  36.6 0.7 %copy.8 = bf16[4,32,1152]{2,1,0:T(8,128)(2,1)} copy(bf16[4,32,1152]{2,1,0:T(8,128)(2,1)S(1)} %bitcast.2) | data formatting | bytes 589824
Async XLA Ops:
  0.0 18.0 %all-to-all-start = ((bf16[16,8,1152]{2,1,0:T(8,128)(2,1)}), bf16[16,8,1152]{2,1,0:T(8,128)(2,1)S(1)}, u32[]{:S(2)}, u32[]{:S(2)}) async-start(bf16[16,8,1152]{2,1,0:T(8,128)(2,1)} %bitcast.3), calls=%async_computation | async-start | bytes 589824 | tf_op jit(solution)/shard_map/all_to_all | solution.py:160

commit v7 on v2

--- a/solution.py
+++ b/solution.py
@@ -20,7 +20,7 @@
 
 
 def held_kernel(
-    ln_ref, qg_ref, kg_ref, wqkv_ref, gains_out, member_out, spread_out, wq_out, ln, qg, kg, sems
+    ln_ref, qg_ref, kg_ref, wqkv_ref, gains_out, columns_out, member_out, spread_out, wq_out, ln, qg, kg, sems
 ):
     width = wq_out.shape[1]
     pairs = [(ln_ref, ln), (qg_ref, qg), (kg_ref, kg), (wqkv_ref.at[:, pl.ds(0, width)], wq_out)]
@@ -40,14 +40,16 @@
     for copy in copies[:3]:
         copy.wait()
     gains_out[0:1, :] = ln[...].reshape(1, width)
-    gains_out[1:2, :] = jnp.concatenate([qg[...].reshape(1, HEAD_DIM)] * HEADS, axis=1)
-    gains_out[2:3, :] = jnp.concatenate([kg[...].reshape(1, HEAD_DIM)] * HEADS, axis=1)
+    row = jnp.concatenate([qg[...].reshape(1, HEAD_DIM), jnp.zeros((1, LANES - HEAD_DIM), jnp.float32)], axis=1)
+    columns_out[...] = jnp.broadcast_to(row, (LANES, LANES)).T[:HEAD_DIM]
+    gains_out[1:2, :] = jnp.concatenate([kg[...].reshape(1, HEAD_DIM)] * HEADS, axis=1)
     copies[3].wait()
 
 
 def tokens_kernel(
     x_ref,
     gains_ref,
+    columns_ref,
     member_ref,
     spread_ref,
     wq,
@@ -59,7 +61,6 @@
     normed,
     mixed_q,
     mixed_k,
-    queries,
     queries_t,
     keys,
     values_t,
@@ -103,13 +104,19 @@
         out[...] = (mixed[...] * dot(parts, spread_ref[...]) * gains_ref[row : row + 1, :]).astype(bf16)
 
     copies[1].start()
-    mixed_q[...] = dot(normed[...], wq[...])
-    head_norm(mixed_q, 1, queries)
+    mixed_q[...] = dot(normed[...], wq[...]).T
+    for pair in range(HEADS // 2):
+        heads = []
+        for first in (2 * pair * HEAD_DIM, (2 * pair + 1) * HEAD_DIM):
+            head = mixed_q[first : first + HEAD_DIM, :]
+            total = jnp.sum(head * head, axis=0, keepdims=True)
+            heads.append(head * lax.rsqrt(total * (1.0 / HEAD_DIM) + EPS) * columns_ref[...])
+        rows = slice(2 * pair * HEAD_DIM, (2 * pair + 2) * HEAD_DIM)
+        queries_t[rows, :] = jnp.concatenate(heads, axis=0).astype(bf16)
     copies[0].wait()
     copies[2].start()
     mixed_k[...] = dot(normed[...], wkv[:, :width])
-    queries_t[...] = queries[...].T
-    head_norm(mixed_k, 2, keys)
+    head_norm(mixed_k, 1, keys)
     copies[1].wait()
     values_t[...] = dot(normed[...], wkv[:, width:]).astype(bf16).T
 
@@ -158,16 +165,17 @@
     in_hbm = pl.BlockSpec(memory_space=pltpu.HBM)
     bf16, f32 = jnp.bfloat16, jnp.float32
     held = [pltpu.with_memory_space_constraint(a, pltpu.HBM) for a in (ln_gain, q_gain, k_gain, w_qkv, w_out)]
-    gains, member, spread, wq = pl.pallas_call(
+    gains, columns, member, spread, wq = pl.pallas_call(
         held_kernel,
         out_shape=(
             pltpu.VMEM((8, model), f32),
+            pltpu.VMEM((HEAD_DIM, LANES), f32),
             pltpu.VMEM((model, LANES), bf16),
             pltpu.VMEM((2 * HEADS, model), bf16),
             pltpu.VMEM((model, model), bf16),
         ),
         in_specs=[in_hbm] * 4,
-        out_specs=[in_vmem] * 4,
+        out_specs=[in_vmem] * 5,
         scratch_shapes=[
             pltpu.VMEM((model,), f32),
             pltpu.VMEM((HEAD_DIM,), f32),
@@ -181,15 +189,14 @@
     result = pl.pallas_call(
         tokens_kernel,
         out_shape=jax.ShapeDtypeStruct(gathered.shape, bf16),
-        in_specs=[in_vmem] * 5 + [in_hbm] * 2,
+        in_specs=[in_vmem] * 6 + [in_hbm] * 2,
         out_specs=in_vmem,
         scratch_shapes=[
             pltpu.VMEM((model, 2 * model), bf16),
             pltpu.VMEM(w_out.shape, bf16),
             pltpu.VMEM((tokens, model), bf16),
+            pltpu.VMEM((model, tokens), f32),
             pltpu.VMEM((tokens, model), f32),
-            pltpu.VMEM((tokens, model), f32),
-            pltpu.VMEM((tokens, model), bf16),
             pltpu.VMEM((model, tokens), bf16),
             pltpu.VMEM((tokens, model), bf16),
             pltpu.VMEM((model, tokens), bf16),
@@ -200,7 +207,7 @@
         ],
         compiler_params=pltpu.CompilerParams(vmem_limit_bytes=40 * 1024 * 1024),
         name="tokens",
-    )(gathered, gains, member, spread, wq, *held[3:])
+    )(gathered, gains, columns, member, spread, wq, *held[3:])
     return exchange(result).reshape(latent.shape)
 
 

time: 37.1 us -> 37 us (level)
  no operation moved by 1% of the time
where the time goes in v7:
time: 37 us; the launch traced here: 36.7 us
  blocking collectives  13.5 us (36%)
  waiting for transfers between devices  8.73 us (24%)
  starting transfers between devices  7.39 us (20%)
  Pallas kernels  6.36 us (17%)
  local copies, waits for them, and re-layouts  0.71 us (2%)
    all_to_all x1, blocking collectives, body(): return exchange(result).reshape(latent.shape)  13.5 us
    all_to_all x1, waiting for transfers between devices, body(): gathered = exchange(latent.reshape(device_count, per_peer, model))  8.73 us
    all_to_all x1, starting transfers between devices, body(): gathered = exchange(latent.reshape(device_count, per_peer, model))  7.39 us
    pallas_call x1, Pallas kernels, body(): pl.pallas_call(tokens_kernel, out_shape=jax.ShapeDtypeStruct(gathered.sha...  4.52 us
    pallas_call x1, Pallas kernels, body(): pl.pallas_call(held_kernel, out_shape=(pltpu.VMEM((8, model), f32), pltpu...  1.84 us
  transfers between devices with their start and end apart: 1, of which 1 were waited for; matrix products, arithmetic and copies ran while one was open for 0% of the time, Pallas kernels for 5%

profile of v7, /device:TPU:0, one launch (start us, length us, event | category | flops | bytes accessed | tf_op | source)
XLA Modules:
  0.0 36.7 jit_solution(3833801989135242062)
XLA Ops:
  0.0 7.4 %all-to-all-start = ((bf16[16,8,1152]{2,1,0:T(8,128)(2,1)}), bf16[16,8,1152]{2,1,0:T(8,128)(2,1)S(1)}, u32[]{:S(2)}, u32[]{:S(2)}) async-start(bf16[16,8,1152]{2,1,0:T(8,128)(2,1)} %bitcast.3), calls=%async_computation | async-start | bytes 589824 | tf_op jit(solution)/shard_map/all_to_all | solution.py:163
  7.4 1.8 %held.1 = (f32[8,1152]{1,0:T(8,128)S(1)}, f32[72,128]{1,0:T(8,128)S(1)}, bf16[1152,128]{1,0:T(8,128)(2,1)S(1)}, bf16[32,1152]{1,0:T(8,128)(2,1)S(1)}, bf16[1152,1152]{1,0:T(8,128)(2,1)S(1)}) custom-call(f32[1152]{0:T(1024)} %ln_ref.1, f32[72]{0:T(128)} %qg_ref.1, f32[72]{0:T(128)} %kg_ref.1, bf16[1152,3456]{1,0:T(8,128)(2,1)} %wqkv_hbm.1), custom_call_target="tpu_custom_call" | custom-call | bytes 5308416 | tf_op jit(solution)/shard_map/held/pallas_call | solution.py:168
  9.2 8.7 %all-to-all-done.x_ref = bf16[16,8,1152]{2,1,0:T(8,128)(2,1)S(1)} async-done(((bf16[16,8,1152]{2,1,0:T(8,128)(2,1)}), bf16[16,8,1152]{2,1,0:T(8,128)(2,1)S(1)}, u32[]{:S(2)}, u32[]{:S(2)}) %all-to-all-start) | async-done | bytes 294944 | tf_op jit(solution)/shard_map/all_to_all | solution.py:163
  18.0 4.5 %tokens.1 = bf16[16,8,1152]{2,1,0:T(8,128)(2,1)S(1)} custom-call(bf16[16,8,1152]{2,1,0:T(8,128)(2,1)S(1)} %all-to-all-done.x_ref, f32[8,1152]{1,0:T(8,128)S(1)} %get-tuple-element.10.gains_ref, f32[72,128]{1,0:T(8,128)S(1)} %get-tuple-element.11.columns_ref, bf16[1152,128]{1,0:T(8,128)(2,1)S(1)} %get-tuple-element.12.member_ref, ...), custom_call_target="tpu_custom_call" | custom-call | tf_op jit(solution)/shard_map/tokens/pallas_call | solution.py:189
  22.5 13.5 %all_to_all.10 = bf16[16,8,1152]{2,1,0:T(8,128)(2,1)S(1)} all-to-all(bf16[16,8,1152]{2,1,0:T(8,128)(2,1)S(1)} %tokens.1), channel_id=1, replica_groups=mesh['groups'=2,'frame'=16] {'frame'}, dimensions={0} | all-to-all | bytes 589824 | tf_op jit(solution)/shard_map/all_to_all | solution.py:211
  36.0 0.7 %copy.8 = bf16[4,32,1152]{2,1,0:T(8,128)(2,1)} copy(bf16[4,32,1152]{2,1,0:T(8,128)(2,1)S(1)} %bitcast.2) | data formatting | bytes 589824
Async XLA Ops:
  0.0 18.0 %all-to-all-start = ((bf16[16,8,1152]{2,1,0:T(8,128)(2,1)}), bf16[16,8,1152]{2,1,0:T(8,128)(2,1)S(1)}, u32[]{:S(2)}, u32[]{:S(2)}) async-start(bf16[16,8,1152]{2,1,0:T(8,128)(2,1)} %bitcast.3), calls=%async_computation | async-start | bytes 589824 | tf_op jit(solution)/shard_map/all_to_all | solution.py:163

commit v8 on v7

--- a/solution.py
+++ b/solution.py
@@ -73,13 +73,34 @@
     tokens = frames * positions
     bf16, f32 = jnp.bfloat16, jnp.float32
 
-    pairs = [
+    blocks = 4
+    depth = width // blocks
+    parts = [
         (wqkv_hbm.at[:, pl.ds(width, width)], wkv.at[:, pl.ds(0, width)]),
         (wqkv_hbm.at[:, pl.ds(2 * width, width)], wkv.at[:, pl.ds(width, width)]),
         (wout_hbm, wout),
     ]
-    copies = [pltpu.make_async_copy(src, dst, sems.at[i]) for i, (src, dst) in enumerate(pairs)]
-    copies[0].start()
+
+    def copies_of(part):
+        src, dst = parts[part]
+        return [
+            pltpu.make_async_copy(
+                src.at[pl.ds(i * depth, depth)], dst.at[pl.ds(i * depth, depth)], sems.at[part, i]
+            )
+            for i in range(blocks)
+        ]
+
+    copies = [copies_of(part) for part in range(len(parts))]
+
+    def start(part):
+        for copy in copies[part]:
+            copy.start()
+
+    def wait(part):
+        for copy in copies[part]:
+            copy.wait()
+
+    start(0)
 
     gain = gains_ref[0:1, :]
     step = max(1, 16 // positions)
@@ -103,7 +124,7 @@
         parts = jnp.where(lane < HEADS, high, low)[:, : 2 * HEADS]
         out[...] = (mixed[...] * dot(parts, spread_ref[...]) * gains_ref[row : row + 1, :]).astype(bf16)
 
-    copies[1].start()
+    start(1)
     mixed_q[...] = dot(normed[...], wq[...]).T
     for pair in range(HEADS // 2):
         heads = []
@@ -113,11 +134,11 @@
             heads.append(head * lax.rsqrt(total * (1.0 / HEAD_DIM) + EPS) * columns_ref[...])
         rows = slice(2 * pair * HEAD_DIM, (2 * pair + 2) * HEAD_DIM)
         queries_t[rows, :] = jnp.concatenate(heads, axis=0).astype(bf16)
-    copies[0].wait()
-    copies[2].start()
+    wait(0)
+    start(2)
     mixed_k[...] = dot(normed[...], wkv[:, :width])
     head_norm(mixed_k, 1, keys)
-    copies[1].wait()
+    wait(1)
     values_t[...] = dot(normed[...], wkv[:, width:]).astype(bf16).T
 
     place = lax.broadcasted_iota(jnp.int32, (tokens, tokens), 0) % positions
@@ -147,7 +168,7 @@
             ]
     attended[...] = attended_t[...].astype(bf16).T
 
-    copies[2].wait()
+    wait(2)
     branch = dot(attended[...], wout[...])
     o_ref[...] = (x_ref[...].astype(f32) + branch.reshape(x_ref.shape)).astype(bf16)
 
@@ -203,7 +224,7 @@
             pltpu.VMEM((model, tokens), f32),
             pltpu.VMEM((tokens, model), bf16),
             pltpu.VMEM((tokens, tokens), f32),
-            pltpu.SemaphoreType.DMA((3,)),
+            pltpu.SemaphoreType.DMA((3, 4)),
         ],
         compiler_params=pltpu.CompilerParams(vmem_limit_bytes=40 * 1024 * 1024),
         name="tokens",

time: 37 us -> 37.5 us (1.014)
  Pallas kernels: 6.36 us -> 6.88 us
    pallas_call x1, Pallas kernels: 4.52 us -> 5.04 us  [body(): pl.pallas_call(tokens_kernel, out_shape=jax.ShapeDtypeStruct(gathered.sha...]
where the time goes in v8:
time: 37.5 us; the launch traced here: 37.2 us
  blocking collectives  13.5 us (36%)
  waiting for transfers between devices  8.73 us (23%)
  starting transfers between devices  7.39 us (20%)
  Pallas kernels  6.88 us (18%)
  local copies, waits for them, and re-layouts  0.71 us (2%)
    all_to_all x1, blocking collectives, body(): return exchange(result).reshape(latent.shape)  13.5 us
    all_to_all x1, waiting for transfers between devices, body(): gathered = exchange(latent.reshape(device_count, per_peer, model))  8.73 us
    all_to_all x1, starting transfers between devices, body(): gathered = exchange(latent.reshape(device_count, per_peer, model))  7.39 us
    pallas_call x1, Pallas kernels, body(): pl.pallas_call(tokens_kernel, out_shape=jax.ShapeDtypeStruct(gathered.sha...  5.04 us
    pallas_call x1, Pallas kernels, body(): pl.pallas_call(held_kernel, out_shape=(pltpu.VMEM((8, model), f32), pltpu...  1.84 us
  transfers between devices with their start and end apart: 1, of which 1 were waited for; matrix products, arithmetic and copies ran while one was open for 0% of the time, Pallas kernels for 5%

profile of v8, /device:TPU:0, one launch (start us, length us, event | category | flops | bytes accessed | tf_op | source)
XLA Modules:
  0.0 37.2 jit_solution(3844890954526329643)
XLA Ops:
  0.0 7.4 %all-to-all-start = ((bf16[16,8,1152]{2,1,0:T(8,128)(2,1)}), bf16[16,8,1152]{2,1,0:T(8,128)(2,1)S(1)}, u32[]{:S(2)}, u32[]{:S(2)}) async-start(bf16[16,8,1152]{2,1,0:T(8,128)(2,1)} %bitcast.3), calls=%async_computation | async-start | bytes 589824 | tf_op jit(solution)/shard_map/all_to_all | solution.py:184
  7.4 1.8 %held.1 = (f32[8,1152]{1,0:T(8,128)S(1)}, f32[72,128]{1,0:T(8,128)S(1)}, bf16[1152,128]{1,0:T(8,128)(2,1)S(1)}, bf16[32,1152]{1,0:T(8,128)(2,1)S(1)}, bf16[1152,1152]{1,0:T(8,128)(2,1)S(1)}) custom-call(f32[1152]{0:T(1024)} %ln_ref.1, f32[72]{0:T(128)} %qg_ref.1, f32[72]{0:T(128)} %kg_ref.1, bf16[1152,3456]{1,0:T(8,128)(2,1)} %wqkv_hbm.1), custom_call_target="tpu_custom_call" | custom-call | bytes 5308416 | tf_op jit(solution)/shard_map/held/pallas_call | solution.py:189
  9.2 8.7 %all-to-all-done.x_ref = bf16[16,8,1152]{2,1,0:T(8,128)(2,1)S(1)} async-done(((bf16[16,8,1152]{2,1,0:T(8,128)(2,1)}), bf16[16,8,1152]{2,1,0:T(8,128)(2,1)S(1)}, u32[]{:S(2)}, u32[]{:S(2)}) %all-to-all-start) | async-done | bytes 294944 | tf_op jit(solution)/shard_map/all_to_all | solution.py:184
  18.0 5.0 %tokens.1 = bf16[16,8,1152]{2,1,0:T(8,128)(2,1)S(1)} custom-call(bf16[16,8,1152]{2,1,0:T(8,128)(2,1)S(1)} %all-to-all-done.x_ref, f32[8,1152]{1,0:T(8,128)S(1)} %get-tuple-element.10.gains_ref, f32[72,128]{1,0:T(8,128)S(1)} %get-tuple-element.11.columns_ref, bf16[1152,128]{1,0:T(8,128)(2,1)S(1)} %get-tuple-element.12.member_ref, ...), custom_call_target="tpu_custom_call" | custom-call | tf_op jit(solution)/shard_map/tokens/pallas_call | solution.py:210
  23.0 13.5 %all_to_all.10 = bf16[16,8,1152]{2,1,0:T(8,128)(2,1)S(1)} all-to-all(bf16[16,8,1152]{2,1,0:T(8,128)(2,1)S(1)} %tokens.1), channel_id=1, replica_groups=mesh['groups'=2,'frame'=16] {'frame'}, dimensions={0} | all-to-all | bytes 589824 | tf_op jit(solution)/shard_map/all_to_all | solution.py:232
  36.5 0.7 %copy.8 = bf16[4,32,1152]{2,1,0:T(8,128)(2,1)} copy(bf16[4,32,1152]{2,1,0:T(8,128)(2,1)S(1)} %bitcast.2) | data formatting | bytes 589824
Async XLA Ops:
  0.0 18.0 %all-to-all-start = ((bf16[16,8,1152]{2,1,0:T(8,128)(2,1)}), bf16[16,8,1152]{2,1,0:T(8,128)(2,1)S(1)}, u32[]{:S(2)}, u32[]{:S(2)}) async-start(bf16[16,8,1152]{2,1,0:T(8,128)(2,1)} %bitcast.3), calls=%async_computation | async-start | bytes 589824 | tf_op jit(solution)/shard_map/all_to_all | solution.py:184

commit v9 on v7

--- a/solution.py
+++ b/solution.py
@@ -73,13 +73,16 @@
     tokens = frames * positions
     bf16, f32 = jnp.bfloat16, jnp.float32
 
+    bounds = [(0, 32), (32, width - 32)]
     pairs = [
-        (wqkv_hbm.at[:, pl.ds(width, width)], wkv.at[:, pl.ds(0, width)]),
-        (wqkv_hbm.at[:, pl.ds(2 * width, width)], wkv.at[:, pl.ds(width, width)]),
-        (wout_hbm, wout),
+        (wqkv_hbm.at[pl.ds(row, rows), pl.ds(part * width, width)], wkv.at[pl.ds(row, rows), pl.ds((part - 1) * width, width)])
+        for part in (1, 2)
+        for row, rows in bounds
     ]
+    pairs += [(wout_hbm, wout)]
     copies = [pltpu.make_async_copy(src, dst, sems.at[i]) for i, (src, dst) in enumerate(pairs)]
     copies[0].start()
+    copies[1].start()
 
     gain = gains_ref[0:1, :]
     step = max(1, 16 // positions)
@@ -103,8 +106,10 @@
         parts = jnp.where(lane < HEADS, high, low)[:, : 2 * HEADS]
         out[...] = (mixed[...] * dot(parts, spread_ref[...]) * gains_ref[row : row + 1, :]).astype(bf16)
 
-    copies[1].start()
     mixed_q[...] = dot(normed[...], wq[...]).T
+    copies[0].wait()
+    copies[2].start()
+    copies[3].start()
     for pair in range(HEADS // 2):
         heads = []
         for first in (2 * pair * HEAD_DIM, (2 * pair + 1) * HEAD_DIM):
@@ -113,11 +118,12 @@
             heads.append(head * lax.rsqrt(total * (1.0 / HEAD_DIM) + EPS) * columns_ref[...])
         rows = slice(2 * pair * HEAD_DIM, (2 * pair + 2) * HEAD_DIM)
         queries_t[rows, :] = jnp.concatenate(heads, axis=0).astype(bf16)
-    copies[0].wait()
-    copies[2].start()
+    copies[1].wait()
     mixed_k[...] = dot(normed[...], wkv[:, :width])
+    copies[2].wait()
+    copies[4].start()
     head_norm(mixed_k, 1, keys)
-    copies[1].wait()
+    copies[3].wait()
     values_t[...] = dot(normed[...], wkv[:, width:]).astype(bf16).T
 
     place = lax.broadcasted_iota(jnp.int32, (tokens, tokens), 0) % positions
@@ -147,7 +153,7 @@
             ]
     attended[...] = attended_t[...].astype(bf16).T
 
-    copies[2].wait()
+    copies[4].wait()
     branch = dot(attended[...], wout[...])
     o_ref[...] = (x_ref[...].astype(f32) + branch.reshape(x_ref.shape)).astype(bf16)
 
@@ -203,7 +209,7 @@
             pltpu.VMEM((model, tokens), f32),
             pltpu.VMEM((tokens, model), bf16),
             pltpu.VMEM((tokens, tokens), f32),
-            pltpu.SemaphoreType.DMA((3,)),
+            pltpu.SemaphoreType.DMA((5,)),
         ],
         compiler_params=pltpu.CompilerParams(vmem_limit_bytes=40 * 1024 * 1024),
         name="tokens",

time: 37 us -> 37.4 us (1.011)
  Pallas kernels: 6.36 us -> 6.74 us
    pallas_call x1, Pallas kernels: 4.52 us -> 4.9 us  [body(): pl.pallas_call(tokens_kernel, out_shape=jax.ShapeDtypeStruct(gathered.sha...]
where the time goes in v9:
time: 37.4 us; the launch traced here: 37.1 us
  blocking collectives  13.5 us (36%)
  waiting for transfers between devices  8.73 us (23%)
  starting transfers between devices  7.39 us (20%)
  Pallas kernels  6.74 us (18%)
  local copies, waits for them, and re-layouts  0.71 us (2%)
    all_to_all x1, blocking collectives, body(): return exchange(result).reshape(latent.shape)  13.5 us
    all_to_all x1, waiting for transfers between devices, body(): gathered = exchange(latent.reshape(device_count, per_peer, model))  8.73 us
    all_to_all x1, starting transfers between devices, body(): gathered = exchange(latent.reshape(device_count, per_peer, model))  7.39 us
    pallas_call x1, Pallas kernels, body(): pl.pallas_call(tokens_kernel, out_shape=jax.ShapeDtypeStruct(gathered.sha...  4.9 us
    pallas_call x1, Pallas kernels, body(): pl.pallas_call(held_kernel, out_shape=(pltpu.VMEM((8, model), f32), pltpu...  1.84 us
  transfers between devices with their start and end apart: 1, of which 1 were waited for; matrix products, arithmetic and copies ran while one was open for 0% of the time, Pallas kernels for 5%

profile of v9, /device:TPU:0, one launch (start us, length us, event | category | flops | bytes accessed | tf_op | source)
XLA Modules:
  0.0 37.1 jit_solution(1158176864867226284)
XLA Ops:
  0.0 7.4 %all-to-all-start = ((bf16[16,8,1152]{2,1,0:T(8,128)(2,1)}), bf16[16,8,1152]{2,1,0:T(8,128)(2,1)S(1)}, u32[]{:S(2)}, u32[]{:S(2)}) async-start(bf16[16,8,1152]{2,1,0:T(8,128)(2,1)} %bitcast.3), calls=%async_computation | async-start | bytes 589824 | tf_op jit(solution)/shard_map/all_to_all | solution.py:169
  7.4 1.8 %held.1 = (f32[8,1152]{1,0:T(8,128)S(1)}, f32[72,128]{1,0:T(8,128)S(1)}, bf16[1152,128]{1,0:T(8,128)(2,1)S(1)}, bf16[32,1152]{1,0:T(8,128)(2,1)S(1)}, bf16[1152,1152]{1,0:T(8,128)(2,1)S(1)}) custom-call(f32[1152]{0:T(1024)} %ln_ref.1, f32[72]{0:T(128)} %qg_ref.1, f32[72]{0:T(128)} %kg_ref.1, bf16[1152,3456]{1,0:T(8,128)(2,1)} %wqkv_hbm.1), custom_call_target="tpu_custom_call" | custom-call | bytes 5308416 | tf_op jit(solution)/shard_map/held/pallas_call | solution.py:174
  9.2 8.7 %all-to-all-done.x_ref = bf16[16,8,1152]{2,1,0:T(8,128)(2,1)S(1)} async-done(((bf16[16,8,1152]{2,1,0:T(8,128)(2,1)}), bf16[16,8,1152]{2,1,0:T(8,128)(2,1)S(1)}, u32[]{:S(2)}, u32[]{:S(2)}) %all-to-all-start) | async-done | bytes 294944 | tf_op jit(solution)/shard_map/all_to_all | solution.py:169
  18.0 4.9 %tokens.1 = bf16[16,8,1152]{2,1,0:T(8,128)(2,1)S(1)} custom-call(bf16[16,8,1152]{2,1,0:T(8,128)(2,1)S(1)} %all-to-all-done.x_ref, f32[8,1152]{1,0:T(8,128)S(1)} %get-tuple-element.10.gains_ref, f32[72,128]{1,0:T(8,128)S(1)} %get-tuple-element.11.columns_ref, bf16[1152,128]{1,0:T(8,128)(2,1)S(1)} %get-tuple-element.12.member_ref, ...), custom_call_target="tpu_custom_call" | custom-call | tf_op jit(solution)/shard_map/tokens/pallas_call | solution.py:195
  22.9 13.5 %all_to_all.10 = bf16[16,8,1152]{2,1,0:T(8,128)(2,1)S(1)} all-to-all(bf16[16,8,1152]{2,1,0:T(8,128)(2,1)S(1)} %tokens.1), channel_id=1, replica_groups=mesh['groups'=2,'frame'=16] {'frame'}, dimensions={0} | all-to-all | bytes 589824 | tf_op jit(solution)/shard_map/all_to_all | solution.py:217
  36.4 0.7 %copy.8 = bf16[4,32,1152]{2,1,0:T(8,128)(2,1)} copy(bf16[4,32,1152]{2,1,0:T(8,128)(2,1)S(1)} %bitcast.2) | data formatting | bytes 589824
Async XLA Ops:
  0.0 18.0 %all-to-all-start = ((bf16[16,8,1152]{2,1,0:T(8,128)(2,1)}), bf16[16,8,1152]{2,1,0:T(8,128)(2,1)S(1)}, u32[]{:S(2)}, u32[]{:S(2)}) async-start(bf16[16,8,1152]{2,1,0:T(8,128)(2,1)} %bitcast.3), calls=%async_computation | async-start | bytes 589824 | tf_op jit(solution)/shard_map/all_to_all | solution.py:169

commit v10 on v7

--- a/solution.py
+++ b/solution.py
@@ -157,8 +157,9 @@
     rows, columns, model = latent.shape
     tokens = rows * columns
     per_peer = tokens // device_count
+    order = [4 * i + 2 * row + core for row in range(2) for i in range(device_count // 4) for core in range(2)]
     exchange = functools.partial(
-        lax.all_to_all, axis_name="frame", split_axis=0, concat_axis=0, tiled=True
+        lax.all_to_all, axis_name="frame", split_axis=0, concat_axis=0, axis_index_groups=[order], tiled=True
     )
     gathered = exchange(latent.reshape(device_count, per_peer, model))
     in_vmem = pl.BlockSpec(memory_space=pltpu.VMEM)

time: 37 us -> 36.8 us (level)
  no operation moved by 1% of the time
where the time goes in v10:
time: 36.8 us; the launch traced here: 36.6 us
  blocking collectives  13.4 us (36%)
  waiting for transfers between devices  8.73 us (24%)
  starting transfers between devices  7.39 us (20%)
  Pallas kernels  6.36 us (17%)
  local copies, waits for them, and re-layouts  0.71 us (2%)
    all_to_all x1, blocking collectives, body(): return exchange(result).reshape(latent.shape)  13.4 us
    all_to_all x1, waiting for transfers between devices, body(): gathered = exchange(latent.reshape(device_count, per_peer, model))  8.73 us
    all_to_all x1, starting transfers between devices, body(): gathered = exchange(latent.reshape(device_count, per_peer, model))  7.39 us
    pallas_call x1, Pallas kernels, body(): pl.pallas_call(tokens_kernel, out_shape=jax.ShapeDtypeStruct(gathered.sha...  4.52 us
    pallas_call x1, Pallas kernels, body(): pl.pallas_call(held_kernel, out_shape=(pltpu.VMEM((8, model), f32), pltpu...  1.84 us
  transfers between devices with their start and end apart: 1, of which 1 were waited for; matrix products, arithmetic and copies ran while one was open for 0% of the time, Pallas kernels for 5%

profile of v10, /device:TPU:0, one launch (start us, length us, event | category | flops | bytes accessed | tf_op | source)
XLA Modules:
  0.0 36.6 jit_solution(9897893468191706621)
XLA Ops:
  0.0 7.4 %all-to-all-start = ((bf16[16,8,1152]{2,1,0:T(8,128)(2,1)}), bf16[16,8,1152]{2,1,0:T(8,128)(2,1)S(1)}, u32[]{:S(2)}, u32[]{:S(2)}) async-start(bf16[16,8,1152]{2,1,0:T(8,128)(2,1)} %bitcast.3), calls=%async_computation | async-start | bytes 589824 | tf_op jit(solution)/shard_map/all_to_all | solution.py:164
  7.4 1.8 %held.1 = (f32[8,1152]{1,0:T(8,128)S(1)}, f32[72,128]{1,0:T(8,128)S(1)}, bf16[1152,128]{1,0:T(8,128)(2,1)S(1)}, bf16[32,1152]{1,0:T(8,128)(2,1)S(1)}, bf16[1152,1152]{1,0:T(8,128)(2,1)S(1)}) custom-call(f32[1152]{0:T(1024)} %ln_ref.1, f32[72]{0:T(128)} %qg_ref.1, f32[72]{0:T(128)} %kg_ref.1, bf16[1152,3456]{1,0:T(8,128)(2,1)} %wqkv_hbm.1), custom_call_target="tpu_custom_call" | custom-call | bytes 5308416 | tf_op jit(solution)/shard_map/held/pallas_call | solution.py:169
  9.2 8.7 %all-to-all-done.x_ref = bf16[16,8,1152]{2,1,0:T(8,128)(2,1)S(1)} async-done(((bf16[16,8,1152]{2,1,0:T(8,128)(2,1)}), bf16[16,8,1152]{2,1,0:T(8,128)(2,1)S(1)}, u32[]{:S(2)}, u32[]{:S(2)}) %all-to-all-start) | async-done | bytes 294944 | tf_op jit(solution)/shard_map/all_to_all | solution.py:164
  18.0 4.5 %tokens.1 = bf16[16,8,1152]{2,1,0:T(8,128)(2,1)S(1)} custom-call(bf16[16,8,1152]{2,1,0:T(8,128)(2,1)S(1)} %all-to-all-done.x_ref, f32[8,1152]{1,0:T(8,128)S(1)} %get-tuple-element.10.gains_ref, f32[72,128]{1,0:T(8,128)S(1)} %get-tuple-element.11.columns_ref, bf16[1152,128]{1,0:T(8,128)(2,1)S(1)} %get-tuple-element.12.member_ref, ...), custom_call_target="tpu_custom_call" | custom-call | tf_op jit(solution)/shard_map/tokens/pallas_call | solution.py:190
  22.5 13.4 %all_to_all.10 = bf16[16,8,1152]{2,1,0:T(8,128)(2,1)S(1)} all-to-all(bf16[16,8,1152]{2,1,0:T(8,128)(2,1)S(1)} %tokens.1), channel_id=1, replica_groups={{0,1,4,5,8,9,12,13,2,3,6,7,10,11,14,15},{16,17,20,21,24,25,28,29,18,19,..., dimensions={0} | all-to-all | bytes 589824 | tf_op jit(solution)/shard_map/all_to_all | solution.py:212
  35.8 0.7 %copy.8 = bf16[4,32,1152]{2,1,0:T(8,128)(2,1)} copy(bf16[4,32,1152]{2,1,0:T(8,128)(2,1)S(1)} %bitcast.2) | data formatting | bytes 589824
Async XLA Ops:
  0.0 18.0 %all-to-all-start = ((bf16[16,8,1152]{2,1,0:T(8,128)(2,1)}), bf16[16,8,1152]{2,1,0:T(8,128)(2,1)S(1)}, u32[]{:S(2)}, u32[]{:S(2)}) async-start(bf16[16,8,1152]{2,1,0:T(8,128)(2,1)} %bitcast.3), calls=%async_computation | async-start | bytes 589824 | tf_op jit(solution)/shard_map/all_to_all | solution.py:164

commit v11 on v10

--- a/solution.py
+++ b/solution.py
@@ -54,10 +54,8 @@
     spread_ref,
     wq,
     wqkv_hbm,
-    wout_hbm,
     o_ref,
     wkv,
-    wout,
     normed,
     mixed_q,
     mixed_k,
@@ -65,7 +63,6 @@
     keys,
     values_t,
     attended_t,
-    attended,
     same,
     sems,
 ):
@@ -76,7 +73,6 @@
     pairs = [
         (wqkv_hbm.at[:, pl.ds(width, width)], wkv.at[:, pl.ds(0, width)]),
         (wqkv_hbm.at[:, pl.ds(2 * width, width)], wkv.at[:, pl.ds(width, width)]),
-        (wout_hbm, wout),
     ]
     copies = [pltpu.make_async_copy(src, dst, sems.at[i]) for i, (src, dst) in enumerate(pairs)]
     copies[0].start()
@@ -114,7 +110,6 @@
         rows = slice(2 * pair * HEAD_DIM, (2 * pair + 2) * HEAD_DIM)
         queries_t[rows, :] = jnp.concatenate(heads, axis=0).astype(bf16)
     copies[0].wait()
-    copies[2].start()
     mixed_k[...] = dot(normed[...], wkv[:, :width])
     head_norm(mixed_k, 1, keys)
     copies[1].wait()
@@ -145,11 +140,7 @@
             attended_t[first : first + HEAD_DIM, :] = heads_out[
                 h * HEAD_DIM : (h + 1) * HEAD_DIM, h * tokens : (h + 1) * tokens
             ]
-    attended[...] = attended_t[...].astype(bf16).T
-
-    copies[2].wait()
-    branch = dot(attended[...], wout[...])
-    o_ref[...] = (x_ref[...].astype(f32) + branch.reshape(x_ref.shape)).astype(bf16)
+    o_ref[...] = attended_t[...].astype(bf16).T.reshape(o_ref.shape)
 
 
 def body(latent, ln_gain, q_gain, k_gain, w_qkv, w_out):
@@ -165,7 +156,7 @@
     in_vmem = pl.BlockSpec(memory_space=pltpu.VMEM)
     in_hbm = pl.BlockSpec(memory_space=pltpu.HBM)
     bf16, f32 = jnp.bfloat16, jnp.float32
-    held = [pltpu.with_memory_space_constraint(a, pltpu.HBM) for a in (ln_gain, q_gain, k_gain, w_qkv, w_out)]
+    held = [pltpu.with_memory_space_constraint(a, pltpu.HBM) for a in (ln_gain, q_gain, k_gain, w_qkv)]
     gains, columns, member, spread, wq = pl.pallas_call(
         held_kernel,
         out_shape=(
@@ -187,14 +178,13 @@
         cost_estimate=pl.CostEstimate(flops=0, bytes_accessed=4 * model * model, transcendentals=0),
         name="held",
     )(*held[:4])
-    result = pl.pallas_call(
+    attended = pl.pallas_call(
         tokens_kernel,
         out_shape=jax.ShapeDtypeStruct(gathered.shape, bf16),
-        in_specs=[in_vmem] * 6 + [in_hbm] * 2,
+        in_specs=[in_vmem] * 6 + [in_hbm],
         out_specs=in_vmem,
         scratch_shapes=[
             pltpu.VMEM((model, 2 * model), bf16),
-            pltpu.VMEM(w_out.shape, bf16),
             pltpu.VMEM((tokens, model), bf16),
             pltpu.VMEM((model, tokens), f32),
             pltpu.VMEM((tokens, model), f32),
@@ -202,14 +192,14 @@
             pltpu.VMEM((tokens, model), bf16),
             pltpu.VMEM((model, tokens), bf16),
             pltpu.VMEM((model, tokens), f32),
-            pltpu.VMEM((tokens, model), bf16),
             pltpu.VMEM((tokens, tokens), f32),
-            pltpu.SemaphoreType.DMA((3,)),
+            pltpu.SemaphoreType.DMA((2,)),
         ],
         compiler_params=pltpu.CompilerParams(vmem_limit_bytes=40 * 1024 * 1024),
         name="tokens",
     )(gathered, gains, columns, member, spread, wq, *held[3:])
-    return exchange(result).reshape(latent.shape)
+    branch = jnp.dot(exchange(attended).reshape(tokens, model), w_out, preferred_element_type=f32)
+    return (latent.astype(f32) + branch.reshape(latent.shape)).astype(bf16)
 
 
 def solution(mesh):

time: 36.8 us -> 38.9 us (1.057)
  local copies, waits for them, and re-layouts: 0.71 us -> 3.27 us
  waiting for transfers between devices: 8.73 us -> 7.2 us
  matrix products: 0 us -> 1.31 us
  Pallas kernels: 6.36 us -> 5.78 us
    unnamed x1 -> x8, local copies, waits for them, and re-layouts: 0.71 us -> 3.27 us
    all_to_all x1, waiting for transfers between devices: 8.73 us -> 7.2 us  [body(): gathered = exchange(latent.reshape(device_count, per_peer, model))]
    dot_general x0 -> x1, matrix products: none -> 1.31 us  [body(): jnp.dot(exchange(attended).reshape(tokens, model), w_out, preferred_eleme...]
    pallas_call x1, Pallas kernels: 4.52 us -> 3.94 us  [body(): pl.pallas_call(tokens_kernel, out_shape=jax.ShapeDtypeStruct(gathered.sha...]
where the time goes in v11:
time: 38.9 us; the launch traced here: 38.6 us
  blocking collectives  13.3 us (34%)
  starting transfers between devices  7.65 us (20%)
  waiting for transfers between devices  7.2 us (19%)
  Pallas kernels  5.78 us (15%)
  local copies, waits for them, and re-layouts  3.27 us (8%)
  matrix products  1.31 us (3%)
    all_to_all x1, blocking collectives, body(): exchange(attended).reshape(tokens, model)  13.3 us
    all_to_all x1, starting transfers between devices, body(): gathered = exchange(latent.reshape(device_count, per_peer, model))  7.65 us
    all_to_all x1, waiting for transfers between devices, body(): gathered = exchange(latent.reshape(device_count, per_peer, model))  7.2 us
    pallas_call x1, Pallas kernels, body(): pl.pallas_call(tokens_kernel, out_shape=jax.ShapeDtypeStruct(gathered.sha...  3.94 us
    unnamed x8, local copies, waits for them, and re-layouts  3.27 us
    pallas_call x1, Pallas kernels, body(): pl.pallas_call(held_kernel, out_shape=(pltpu.VMEM((8, model), f32), pltpu...  1.84 us
    dot_general x1, matrix products, body(): jnp.dot(exchange(attended).reshape(tokens, model), w_out, preferred_eleme...  1.31 us
  transfers between devices with their start and end apart: 1, of which 1 were waited for; matrix products, arithmetic and copies ran while one was open for 0% of the time, Pallas kernels for 5%

profile of v11, /device:TPU:0, one launch (start us, length us, event | category | flops | bytes accessed | tf_op | source)
XLA Modules:
  0.0 38.6 jit_solution(3151560003800241513)
XLA Ops:
  0.0 0.0 copy-start
  0.0 7.6 %all-to-all-start = ((bf16[16,8,1152]{2,1,0:T(8,128)(2,1)}), bf16[16,8,1152]{2,1,0:T(8,128)(2,1)S(1)}, u32[]{:S(2)}, u32[]{:S(2)}) async-start(bf16[16,8,1152]{2,1,0:T(8,128)(2,1)} %bitcast.10), calls=%async_computation | async-start | bytes 589824 | tf_op jit(solution)/shard_map/all_to_all | solution.py:155
  7.7 1.8 %held.1 = (f32[8,1152]{1,0:T(8,128)S(1)}, f32[72,128]{1,0:T(8,128)S(1)}, bf16[1152,128]{1,0:T(8,128)(2,1)S(1)}, bf16[32,1152]{1,0:T(8,128)(2,1)S(1)}, bf16[1152,1152]{1,0:T(8,128)(2,1)S(1)}) custom-call(f32[1152]{0:T(1024)} %ln_ref.1, f32[72]{0:T(128)} %qg_ref.1, f32[72]{0:T(128)} %kg_ref.1, bf16[1152,3456]{1,0:T(8,128)(2,1)} %wqkv_hbm.1), custom_call_target="tpu_custom_call" | custom-call | bytes 5308416 | tf_op jit(solution)/shard_map/held/pallas_call | solution.py:160
  9.5 0.0 copy-start.1
  9.5 1.5 %copy-done.1 = bf16[1152,1152]{1,0:T(8,128)(2,1)} copy-done((bf16[1152,1152]{1,0:T(8,128)(2,1)}, bf16[1152,1152]{1,0:T(8,128)(2,1)S(1)}, u32[]{:S(2)}) %copy-start.1) | copy-done | bytes 2654232
  11.0 7.2 %all-to-all-done.x_ref = bf16[16,8,1152]{2,1,0:T(8,128)(2,1)S(1)} async-done(((bf16[16,8,1152]{2,1,0:T(8,128)(2,1)}), bf16[16,8,1152]{2,1,0:T(8,128)(2,1)S(1)}, u32[]{:S(2)}, u32[]{:S(2)}) %all-to-all-start) | async-done | bytes 294944 | tf_op jit(solution)/shard_map/all_to_all | solution.py:155
  18.2 0.0 copy-start.2
  18.2 1.7 %copy-done.2 = bf16[1152,1152]{1,0:T(8,128)(2,1)S(1)} copy-done((bf16[1152,1152]{1,0:T(8,128)(2,1)S(1)}, bf16[1152,1152]{1,0:T(8,128)(2,1)}, u32[]{:S(2)}) %copy-start.2) | copy-done | bytes 2654232
  20.0 0.0 copy-start.3
  20.0 3.9 %tokens.1 = bf16[16,8,1152]{2,1,0:T(8,128)(2,1)S(1)} custom-call(bf16[16,8,1152]{2,1,0:T(8,128)(2,1)S(1)} %all-to-all-done.x_ref, f32[8,1152]{1,0:T(8,128)S(1)} %get-tuple-element.10.gains_ref, f32[72,128]{1,0:T(8,128)S(1)} %get-tuple-element.11.columns_ref, bf16[1152,128]{1,0:T(8,128)(2,1)S(1)} %get-tuple-element.12.member_ref, ...), custom_call_target="tpu_custom_call" | custom-call | tf_op jit(solution)/shard_map/tokens/pallas_call | solution.py:181
  23.9 13.3 %all_to_all.10 = bf16[16,8,1152]{2,1,0:T(8,128)(2,1)S(1)} all-to-all(bf16[16,8,1152]{2,1,0:T(8,128)(2,1)S(1)} %tokens.1), channel_id=1, replica_groups={{0,1,4,5,8,9,12,13,2,3,6,7,10,11,14,15},{16,17,20,21,24,25,28,29,18,19,..., dimensions={0} | all-to-all | bytes 589824 | tf_op jit(solution)/shard_map/all_to_all | solution.py:201
  37.3 0.0 copy-done
  37.3 0.0 copy-done.3
  37.3 1.3 %fusion.5 = bf16[4,32,1152]{2,1,0:T(8,128)(2,1)} fusion(bf16[4,32,1152]{2,1,0:T(8,128)(2,1)S(1)} %bitcast.11, bf16[1152,1152]{1,0:T(8,128)(2,1)S(1)} %copy-done, bf16[4,32,1152]{2,1,0:T(8,128)(2,1)S(1)} %copy-done.3), kind=kOutput, calls=%fused_computation.3 | convolution fusion | flops 340180992 | bytes 3538944 | tf_op jit(solution)/shard_map/dot_general | solution.py:201
Async XLA Ops:
  0.0 37.3 %copy-start = (bf16[1152,1152]{1,0:T(8,128)(2,1)S(1)}, bf16[1152,1152]{1,0:T(8,128)(2,1)}, u32[]{:S(2)}) copy-start(bf16[1152,1152]{1,0:T(8,128)(2,1)} %param.11) | copy-start | bytes 7962628
  0.0 18.2 %all-to-all-start = ((bf16[16,8,1152]{2,1,0:T(8,128)(2,1)}), bf16[16,8,1152]{2,1,0:T(8,128)(2,1)S(1)}, u32[]{:S(2)}, u32[]{:S(2)}) async-start(bf16[16,8,1152]{2,1,0:T(8,128)(2,1)} %bitcast.10), calls=%async_computation | async-start | bytes 589824 | tf_op jit(solution)/shard_map/all_to_all | solution.py:155
  9.5 1.5 %copy-start.1 = (bf16[1152,1152]{1,0:T(8,128)(2,1)}, bf16[1152,1152]{1,0:T(8,128)(2,1)S(1)}, u32[]{:S(2)}) copy-start(bf16[1152,1152]{1,0:T(8,128)(2,1)S(1)} %get-tuple-element.14.wq) | copy-start | bytes 7962628
  18.2 1.8 %copy-start.2 = (bf16[1152,1152]{1,0:T(8,128)(2,1)S(1)}, bf16[1152,1152]{1,0:T(8,128)(2,1)}, u32[]{:S(2)}) copy-start(bf16[1152,1152]{1,0:T(8,128)(2,1)} %copy-done.1) | copy-start | bytes 7962628
  20.0 17.3 %copy-start.3 = (bf16[4,32,1152]{2,1,0:T(8,128)(2,1)S(1)}, bf16[4,32,1152]{2,1,0:T(8,128)(2,1)}, u32[]{:S(2)}) copy-start(bf16[4,32,1152]{2,1,0:T(8,128)(2,1)} %param.6) | copy-start | bytes 884740

commit v12 on v10

--- a/solution.py
+++ b/solution.py
@@ -20,7 +20,7 @@
 
 
 def held_kernel(
-    ln_ref, qg_ref, kg_ref, wqkv_ref, gains_out, columns_out, member_out, spread_out, wq_out, ln, qg, kg, sems
+    positions, ln_ref, qg_ref, kg_ref, wqkv_ref, gains_out, columns_out, same_out, member_out, spread_out, wq_out, ln, qg, kg, sems
 ):
     width = wq_out.shape[1]
     pairs = [(ln_ref, ln), (qg_ref, qg), (kg_ref, kg), (wqkv_ref.at[:, pl.ds(0, width)], wq_out)]
@@ -37,6 +37,9 @@
     for out, axis in ((member_out, 0), (spread_out, 1)):
         feature = lax.broadcasted_iota(jnp.int32, out.shape, axis)
         out[...] = belongs(feature, lax.broadcasted_iota(jnp.int32, out.shape, 1 - axis))
+    place = lax.broadcasted_iota(jnp.int32, same_out.shape, 0) % positions
+    other = lax.broadcasted_iota(jnp.int32, same_out.shape, 1) % positions
+    same_out[...] = (place == other).astype(jnp.float32)
     for copy in copies[:3]:
         copy.wait()
     gains_out[0:1, :] = ln[...].reshape(1, width)
@@ -50,6 +53,7 @@
     x_ref,
     gains_ref,
     columns_ref,
+    same,
     member_ref,
     spread_ref,
     wq,
@@ -61,12 +65,11 @@
     normed,
     mixed_q,
     mixed_k,
-    queries_t,
     keys,
     values_t,
     attended_t,
     attended,
-    same,
+    stacks,
     sems,
 ):
     frames, positions, width = x_ref.shape
@@ -111,8 +114,13 @@
             head = mixed_q[first : first + HEAD_DIM, :]
             total = jnp.sum(head * head, axis=0, keepdims=True)
             heads.append(head * lax.rsqrt(total * (1.0 / HEAD_DIM) + EPS) * columns_ref[...])
-        rows = slice(2 * pair * HEAD_DIM, (2 * pair + 2) * HEAD_DIM)
-        queries_t[rows, :] = jnp.concatenate(heads, axis=0).astype(bf16)
+        begin = pair * (2 * HEAD_DIM - LANES)
+        for h, head in enumerate(heads):
+            above = begin + h * HEAD_DIM
+            below = 2 * LANES - above - HEAD_DIM
+            rows = [jnp.zeros((n, tokens), f32) for n in (above, below)]
+            rows = [part for part in (rows[0], head, rows[1]) if part.shape[0]]
+            stacks[pair, :, h * tokens : (h + 1) * tokens] = jnp.concatenate(rows, axis=0).astype(bf16)
     copies[0].wait()
     copies[2].start()
     mixed_k[...] = dot(normed[...], wkv[:, :width])
@@ -120,20 +128,8 @@
     copies[1].wait()
     values_t[...] = dot(normed[...], wkv[:, width:]).astype(bf16).T
 
-    place = lax.broadcasted_iota(jnp.int32, (tokens, tokens), 0) % positions
-    other = lax.broadcasted_iota(jnp.int32, (tokens, tokens), 1) % positions
-    same[...] = (place == other).astype(f32)
-
-    row = lax.broadcasted_iota(jnp.int32, (2 * LANES, tokens), 0)
     for pair in range(HEADS // 2):
-        window = slice(pair * LANES, (pair + 2) * LANES)
-        begin = pair * (2 * HEAD_DIM - LANES)
-        query = queries_t[window, :]
-        both = [
-            jnp.where((row >= begin + h * HEAD_DIM) & (row < begin + (h + 1) * HEAD_DIM), query, jnp.zeros((), bf16))
-            for h in range(2)
-        ]
-        scores = dot(keys[:, window], jnp.concatenate(both, axis=1))
+        scores = dot(keys[:, pair * LANES : (pair + 2) * LANES], stacks[pair])
         weights = []
         for h in range(2):
             part = jnp.exp2(scores[:, h * tokens : (h + 1) * tokens] * EXP2_SCALE) * same[...]
@@ -166,17 +162,18 @@
     in_hbm = pl.BlockSpec(memory_space=pltpu.HBM)
     bf16, f32 = jnp.bfloat16, jnp.float32
     held = [pltpu.with_memory_space_constraint(a, pltpu.HBM) for a in (ln_gain, q_gain, k_gain, w_qkv, w_out)]
-    gains, columns, member, spread, wq = pl.pallas_call(
-        held_kernel,
+    gains, columns, same, member, spread, wq = pl.pallas_call(
+        functools.partial(held_kernel, per_peer),
         out_shape=(
             pltpu.VMEM((8, model), f32),
             pltpu.VMEM((HEAD_DIM, LANES), f32),
+            pltpu.VMEM((tokens, tokens), f32),
             pltpu.VMEM((model, LANES), bf16),
             pltpu.VMEM((2 * HEADS, model), bf16),
             pltpu.VMEM((model, model), bf16),
         ),
         in_specs=[in_hbm] * 4,
-        out_specs=[in_vmem] * 5,
+        out_specs=[in_vmem] * 6,
         scratch_shapes=[
             pltpu.VMEM((model,), f32),
             pltpu.VMEM((HEAD_DIM,), f32),
@@ -190,7 +187,7 @@
     result = pl.pallas_call(
         tokens_kernel,
         out_shape=jax.ShapeDtypeStruct(gathered.shape, bf16),
-        in_specs=[in_vmem] * 6 + [in_hbm] * 2,
+        in_specs=[in_vmem] * 7 + [in_hbm] * 2,
         out_specs=in_vmem,
         scratch_shapes=[
             pltpu.VMEM((model, 2 * model), bf16),
@@ -198,17 +195,16 @@
             pltpu.VMEM((tokens, model), bf16),
             pltpu.VMEM((model, tokens), f32),
             pltpu.VMEM((tokens, model), f32),
-            pltpu.VMEM((model, tokens), bf16),
             pltpu.VMEM((tokens, model), bf16),
             pltpu.VMEM((model, tokens), bf16),
             pltpu.VMEM((model, tokens), f32),
             pltpu.VMEM((tokens, model), bf16),
-            pltpu.VMEM((tokens, tokens), f32),
+            pltpu.VMEM((HEADS // 2, 2 * LANES, 2 * tokens), bf16),
             pltpu.SemaphoreType.DMA((3,)),
         ],
         compiler_params=pltpu.CompilerParams(vmem_limit_bytes=40 * 1024 * 1024),
         name="tokens",
-    )(gathered, gains, columns, member, spread, wq, *held[3:])
+    )(gathered, gains, columns, same, member, spread, wq, *held[3:])
     return exchange(result).reshape(latent.shape)
 
 

time: 36.8 us -> 36.8 us (level)
  no operation moved by 1% of the time
where the time goes in v12:
time: 36.8 us; the launch traced here: 36.6 us
  blocking collectives  13.3 us (36%)
  waiting for transfers between devices  8.73 us (24%)
  starting transfers between devices  7.39 us (20%)
  Pallas kernels  6.36 us (17%)
  local copies, waits for them, and re-layouts  0.71 us (2%)
    all_to_all x1, blocking collectives, body(): return exchange(result).reshape(latent.shape)  13.3 us
    all_to_all x1, waiting for transfers between devices, body(): gathered = exchange(latent.reshape(device_count, per_peer, model))  8.73 us
    all_to_all x1, starting transfers between devices, body(): gathered = exchange(latent.reshape(device_count, per_peer, model))  7.39 us
    pallas_call x1, Pallas kernels, body(): pl.pallas_call(tokens_kernel, out_shape=jax.ShapeDtypeStruct(gathered.sha...  4.52 us
    pallas_call x1, Pallas kernels, body(): pl.pallas_call(functools.partial(held_kernel, per_peer), out_shape=(pltpu...  1.84 us
  transfers between devices with their start and end apart: 1, of which 1 were waited for; matrix products, arithmetic and copies ran while one was open for 0% of the time, Pallas kernels for 5%

profile of v12, /device:TPU:0, one launch (start us, length us, event | category | flops | bytes accessed | tf_op | source)
XLA Modules:
  0.0 36.6 jit_solution(8260415132105281338)
XLA Ops:
  0.0 7.4 %all-to-all-start = ((bf16[16,8,1152]{2,1,0:T(8,128)(2,1)}), bf16[16,8,1152]{2,1,0:T(8,128)(2,1)S(1)}, u32[]{:S(2)}, u32[]{:S(2)}) async-start(bf16[16,8,1152]{2,1,0:T(8,128)(2,1)} %bitcast.3), calls=%async_computation | async-start | bytes 589824 | tf_op jit(solution)/shard_map/all_to_all | solution.py:160
  7.4 1.8 %held.1 = (f32[8,1152]{1,0:T(8,128)S(1)}, f32[72,128]{1,0:T(8,128)S(1)}, f32[128,128]{1,0:T(8,128)S(1)}, bf16[1152,128]{1,0:T(8,128)(2,1)S(1)}, bf16[32,1152]{1,...) custom-call(f32[1152]{0:T(1024)} %ln_ref.1, f32[72]{0:T(128)} %qg_ref.1, f32[72]{0:T(128)} %kg_ref.1, bf16[1152,3456]{1,0:T(8,128)(2,1)} %wqkv_hbm.1), custom_call_target="tpu_custom_call" | custom-call | bytes 5308416 | tf_op jit(solution)/shard_map/held/pallas_call | solution.py:165
  9.2 8.7 %all-to-all-done.x_ref = bf16[16,8,1152]{2,1,0:T(8,128)(2,1)S(1)} async-done(((bf16[16,8,1152]{2,1,0:T(8,128)(2,1)}), bf16[16,8,1152]{2,1,0:T(8,128)(2,1)S(1)}, u32[]{:S(2)}, u32[]{:S(2)}) %all-to-all-start) | async-done | bytes 294944 | tf_op jit(solution)/shard_map/all_to_all | solution.py:160
  18.0 4.5 %tokens.1 = bf16[16,8,1152]{2,1,0:T(8,128)(2,1)S(1)} custom-call(bf16[16,8,1152]{2,1,0:T(8,128)(2,1)S(1)} %all-to-all-done.x_ref, f32[8,1152]{1,0:T(8,128)S(1)} %get-tuple-element.11.gains_ref, f32[72,128]{1,0:T(8,128)S(1)} %get-tuple-element.12.columns_ref, f32[128,128]{1,0:T(8,128)S(1)} %get-tuple-element.13.same, ...), custom_call_target="tpu_custom_call" | custom-call | tf_op jit(solution)/shard_map/tokens/pallas_call | solution.py:187
  22.5 13.3 %all_to_all.10 = bf16[16,8,1152]{2,1,0:T(8,128)(2,1)S(1)} all-to-all(bf16[16,8,1152]{2,1,0:T(8,128)(2,1)S(1)} %tokens.1), channel_id=1, replica_groups={{0,1,4,5,8,9,12,13,2,3,6,7,10,11,14,15},{16,17,20,21,24,25,28,29,18,19,..., dimensions={0} | all-to-all | bytes 589824 | tf_op jit(solution)/shard_map/all_to_all | solution.py:208
  35.8 0.7 %copy.8 = bf16[4,32,1152]{2,1,0:T(8,128)(2,1)} copy(bf16[4,32,1152]{2,1,0:T(8,128)(2,1)S(1)} %bitcast.2) | data formatting | bytes 589824
Async XLA Ops:
  0.0 18.0 %all-to-all-start = ((bf16[16,8,1152]{2,1,0:T(8,128)(2,1)}), bf16[16,8,1152]{2,1,0:T(8,128)(2,1)S(1)}, u32[]{:S(2)}, u32[]{:S(2)}) async-start(bf16[16,8,1152]{2,1,0:T(8,128)(2,1)} %bitcast.3), calls=%async_computation | async-start | bytes 589824 | tf_op jit(solution)/shard_map/all_to_all | solution.py:160

commit v13 on v12

--- a/solution.py
+++ b/solution.py
@@ -20,10 +20,10 @@
 
 
 def held_kernel(
-    positions, ln_ref, qg_ref, kg_ref, wqkv_ref, gains_out, columns_out, same_out, member_out, spread_out, wq_out, ln, qg, kg, sems
+    positions, ln_ref, qg_ref, kg_ref, wqkv_ref, gains_out, columns_out, same_out, member_out, spread_out, wk_out, ln, qg, kg, sems
 ):
-    width = wq_out.shape[1]
-    pairs = [(ln_ref, ln), (qg_ref, qg), (kg_ref, kg), (wqkv_ref.at[:, pl.ds(0, width)], wq_out)]
+    width = wk_out.shape[1]
+    pairs = [(ln_ref, ln), (qg_ref, qg), (kg_ref, kg), (wqkv_ref.at[:, pl.ds(width, width)], wk_out)]
     copies = [pltpu.make_async_copy(src, dst, sems.at[i]) for i, (src, dst) in enumerate(pairs)]
     for copy in copies:
         copy.start()
@@ -56,11 +56,11 @@
     same,
     member_ref,
     spread_ref,
-    wq,
+    wk,
     wqkv_hbm,
     wout_hbm,
     o_ref,
-    wkv,
+    wqv,
     wout,
     normed,
     mixed_q,
@@ -77,8 +77,8 @@
     bf16, f32 = jnp.bfloat16, jnp.float32
 
     pairs = [
-        (wqkv_hbm.at[:, pl.ds(width, width)], wkv.at[:, pl.ds(0, width)]),
-        (wqkv_hbm.at[:, pl.ds(2 * width, width)], wkv.at[:, pl.ds(width, width)]),
+        (wqkv_hbm.at[:, pl.ds(0, width)], wqv.at[:, pl.ds(0, width)]),
+        (wqkv_hbm.at[:, pl.ds(2 * width, width)], wqv.at[:, pl.ds(width, width)]),
         (wout_hbm, wout),
     ]
     copies = [pltpu.make_async_copy(src, dst, sems.at[i]) for i, (src, dst) in enumerate(pairs)]
@@ -107,7 +107,13 @@
         out[...] = (mixed[...] * dot(parts, spread_ref[...]) * gains_ref[row : row + 1, :]).astype(bf16)
 
     copies[1].start()
-    mixed_q[...] = dot(normed[...], wq[...]).T
+    mixed_k[...] = dot(normed[...], wk[...])
+    head_norm(mixed_k, 1, keys)
+    copies[0].wait()
+    copies[2].start()
+    mixed_q[...] = dot(normed[...], wqv[:, :width]).T
+    copies[1].wait()
+    values_t[...] = dot(normed[...], wqv[:, width:]).astype(bf16).T
     for pair in range(HEADS // 2):
         heads = []
         for first in (2 * pair * HEAD_DIM, (2 * pair + 1) * HEAD_DIM):
@@ -121,12 +127,6 @@
             rows = [jnp.zeros((n, tokens), f32) for n in (above, below)]
             rows = [part for part in (rows[0], head, rows[1]) if part.shape[0]]
             stacks[pair, :, h * tokens : (h + 1) * tokens] = jnp.concatenate(rows, axis=0).astype(bf16)
-    copies[0].wait()
-    copies[2].start()
-    mixed_k[...] = dot(normed[...], wkv[:, :width])
-    head_norm(mixed_k, 1, keys)
-    copies[1].wait()
-    values_t[...] = dot(normed[...], wkv[:, width:]).astype(bf16).T
 
     for pair in range(HEADS // 2):
         scores = dot(keys[:, pair * LANES : (pair + 2) * LANES], stacks[pair])
@@ -162,7 +162,7 @@
     in_hbm = pl.BlockSpec(memory_space=pltpu.HBM)
     bf16, f32 = jnp.bfloat16, jnp.float32
     held = [pltpu.with_memory_space_constraint(a, pltpu.HBM) for a in (ln_gain, q_gain, k_gain, w_qkv, w_out)]
-    gains, columns, same, member, spread, wq = pl.pallas_call(
+    gains, columns, same, member, spread, wk = pl.pallas_call(
         functools.partial(held_kernel, per_peer),
         out_shape=(
             pltpu.VMEM((8, model), f32),
@@ -204,7 +204,7 @@
         ],
         compiler_params=pltpu.CompilerParams(vmem_limit_bytes=40 * 1024 * 1024),
         name="tokens",
-    )(gathered, gains, columns, same, member, spread, wq, *held[3:])
+    )(gathered, gains, columns, same, member, spread, wk, *held[3:])
     return exchange(result).reshape(latent.shape)
 
 

time: 36.8 us -> 36.9 us (level)
  no operation moved by 1% of the time
where the time goes in v13:
time: 36.9 us; the launch traced here: 36.6 us
  blocking collectives  13.4 us (36%)
  waiting for transfers between devices  8.73 us (24%)
  starting transfers between devices  7.39 us (20%)
  Pallas kernels  6.45 us (17%)
  local copies, waits for them, and re-layouts  0.71 us (2%)
    all_to_all x1, blocking collectives, body(): return exchange(result).reshape(latent.shape)  13.4 us
    all_to_all x1, waiting for transfers between devices, body(): gathered = exchange(latent.reshape(device_count, per_peer, model))  8.73 us
    all_to_all x1, starting transfers between devices, body(): gathered = exchange(latent.reshape(device_count, per_peer, model))  7.39 us
    pallas_call x1, Pallas kernels, body(): pl.pallas_call(tokens_kernel, out_shape=jax.ShapeDtypeStruct(gathered.sha...  4.61 us
    pallas_call x1, Pallas kernels, body(): pl.pallas_call(functools.partial(held_kernel, per_peer), out_shape=(pltpu...  1.84 us
  transfers between devices with their start and end apart: 1, of which 1 were waited for; matrix products, arithmetic and copies ran while one was open for 0% of the time, Pallas kernels for 5%

profile of v13, /device:TPU:0, one launch (start us, length us, event | category | flops | bytes accessed | tf_op | source)
XLA Modules:
  0.0 36.6 jit_solution(7611023061616983706)
XLA Ops:
  0.0 7.4 %all-to-all-start = ((bf16[16,8,1152]{2,1,0:T(8,128)(2,1)}), bf16[16,8,1152]{2,1,0:T(8,128)(2,1)S(1)}, u32[]{:S(2)}, u32[]{:S(2)}) async-start(bf16[16,8,1152]{2,1,0:T(8,128)(2,1)} %bitcast.3), calls=%async_computation | async-start | bytes 589824 | tf_op jit(solution)/shard_map/all_to_all | solution.py:160
  7.4 1.8 %held.1 = (f32[8,1152]{1,0:T(8,128)S(1)}, f32[72,128]{1,0:T(8,128)S(1)}, f32[128,128]{1,0:T(8,128)S(1)}, bf16[1152,128]{1,0:T(8,128)(2,1)S(1)}, bf16[32,1152]{1,...) custom-call(f32[1152]{0:T(1024)} %ln_ref.1, f32[72]{0:T(128)} %qg_ref.1, f32[72]{0:T(128)} %kg_ref.1, bf16[1152,3456]{1,0:T(8,128)(2,1)} %wqkv_hbm.1), custom_call_target="tpu_custom_call" | custom-call | bytes 5308416 | tf_op jit(solution)/shard_map/held/pallas_call | solution.py:165
  9.2 8.7 %all-to-all-done.x_ref = bf16[16,8,1152]{2,1,0:T(8,128)(2,1)S(1)} async-done(((bf16[16,8,1152]{2,1,0:T(8,128)(2,1)}), bf16[16,8,1152]{2,1,0:T(8,128)(2,1)S(1)}, u32[]{:S(2)}, u32[]{:S(2)}) %all-to-all-start) | async-done | bytes 294944 | tf_op jit(solution)/shard_map/all_to_all | solution.py:160
  18.0 4.6 %tokens.1 = bf16[16,8,1152]{2,1,0:T(8,128)(2,1)S(1)} custom-call(bf16[16,8,1152]{2,1,0:T(8,128)(2,1)S(1)} %all-to-all-done.x_ref, f32[8,1152]{1,0:T(8,128)S(1)} %get-tuple-element.11.gains_ref, f32[72,128]{1,0:T(8,128)S(1)} %get-tuple-element.12.columns_ref, f32[128,128]{1,0:T(8,128)S(1)} %get-tuple-element.13.same, ...), custom_call_target="tpu_custom_call" | custom-call | tf_op jit(solution)/shard_map/tokens/pallas_call | solution.py:187
  22.6 13.4 %all_to_all.10 = bf16[16,8,1152]{2,1,0:T(8,128)(2,1)S(1)} all-to-all(bf16[16,8,1152]{2,1,0:T(8,128)(2,1)S(1)} %tokens.1), channel_id=1, replica_groups={{0,1,4,5,8,9,12,13,2,3,6,7,10,11,14,15},{16,17,20,21,24,25,28,29,18,19,..., dimensions={0} | all-to-all | bytes 589824 | tf_op jit(solution)/shard_map/all_to_all | solution.py:208
  35.9 0.7 %copy.8 = bf16[4,32,1152]{2,1,0:T(8,128)(2,1)} copy(bf16[4,32,1152]{2,1,0:T(8,128)(2,1)S(1)} %bitcast.2) | data formatting | bytes 589824
Async XLA Ops:
  0.0 18.0 %all-to-all-start = ((bf16[16,8,1152]{2,1,0:T(8,128)(2,1)}), bf16[16,8,1152]{2,1,0:T(8,128)(2,1)S(1)}, u32[]{:S(2)}, u32[]{:S(2)}) async-start(bf16[16,8,1152]{2,1,0:T(8,128)(2,1)} %bitcast.3), calls=%async_computation | async-start | bytes 589824 | tf_op jit(solution)/shard_map/all_to_all | solution.py:160

commit v14 on v10

--- a/solution.py
+++ b/solution.py
@@ -20,12 +20,14 @@
 
 
 def held_kernel(
-    ln_ref, qg_ref, kg_ref, wqkv_ref, gains_out, columns_out, member_out, spread_out, wq_out, ln, qg, kg, sems
+    ln_ref, qg_ref, kg_ref, wqkv_ref, gains_out, columns_out, member_out, spread_out, wq_out, wkv_out, ln, qg, kg, wkv, sems
 ):
     width = wq_out.shape[1]
     pairs = [(ln_ref, ln), (qg_ref, qg), (kg_ref, kg), (wqkv_ref.at[:, pl.ds(0, width)], wq_out)]
+    pairs += [(wqkv_ref.at[:, pl.ds((i + 1) * width, width)], wkv.at[i]) for i in range(2)]
+    pairs += [(wkv.at[i], wkv_out.at[i]) for i in range(2)]
     copies = [pltpu.make_async_copy(src, dst, sems.at[i]) for i, (src, dst) in enumerate(pairs)]
-    for copy in copies:
+    for copy in copies[:6]:
         copy.start()
 
     def belongs(feature, lane):
@@ -43,7 +45,11 @@
     row = jnp.concatenate([qg[...].reshape(1, HEAD_DIM), jnp.zeros((1, LANES - HEAD_DIM), jnp.float32)], axis=1)
     columns_out[...] = jnp.broadcast_to(row, (LANES, LANES)).T[:HEAD_DIM]
     gains_out[1:2, :] = jnp.concatenate([kg[...].reshape(1, HEAD_DIM)] * HEADS, axis=1)
-    copies[3].wait()
+    for i in range(2):
+        copies[4 + i].wait()
+        copies[6 + i].start()
+    for copy in (copies[3], copies[6], copies[7]):
+        copy.wait()
 
 
 def tokens_kernel(
@@ -53,7 +59,7 @@
     member_ref,
     spread_ref,
     wq,
-    wqkv_hbm,
+    wkv_hbm,
     wout_hbm,
     o_ref,
     wkv,
@@ -74,8 +80,8 @@
     bf16, f32 = jnp.bfloat16, jnp.float32
 
     pairs = [
-        (wqkv_hbm.at[:, pl.ds(width, width)], wkv.at[:, pl.ds(0, width)]),
-        (wqkv_hbm.at[:, pl.ds(2 * width, width)], wkv.at[:, pl.ds(width, width)]),
+        (wkv_hbm.at[0], wkv.at[0]),
+        (wkv_hbm.at[1], wkv.at[1]),
         (wout_hbm, wout),
     ]
     copies = [pltpu.make_async_copy(src, dst, sems.at[i]) for i, (src, dst) in enumerate(pairs)]
@@ -115,10 +121,10 @@
         queries_t[rows, :] = jnp.concatenate(heads, axis=0).astype(bf16)
     copies[0].wait()
     copies[2].start()
-    mixed_k[...] = dot(normed[...], wkv[:, :width])
+    mixed_k[...] = dot(normed[...], wkv[0])
     head_norm(mixed_k, 1, keys)
     copies[1].wait()
-    values_t[...] = dot(normed[...], wkv[:, width:]).astype(bf16).T
+    values_t[...] = dot(normed[...], wkv[1]).astype(bf16).T
 
     place = lax.broadcasted_iota(jnp.int32, (tokens, tokens), 0) % positions
     other = lax.broadcasted_iota(jnp.int32, (tokens, tokens), 1) % positions
@@ -166,7 +172,7 @@
     in_hbm = pl.BlockSpec(memory_space=pltpu.HBM)
     bf16, f32 = jnp.bfloat16, jnp.float32
     held = [pltpu.with_memory_space_constraint(a, pltpu.HBM) for a in (ln_gain, q_gain, k_gain, w_qkv, w_out)]
-    gains, columns, member, spread, wq = pl.pallas_call(
+    gains, columns, member, spread, wq, wkv = pl.pallas_call(
         held_kernel,
         out_shape=(
             pltpu.VMEM((8, model), f32),
@@ -174,17 +180,19 @@
             pltpu.VMEM((model, LANES), bf16),
             pltpu.VMEM((2 * HEADS, model), bf16),
             pltpu.VMEM((model, model), bf16),
+            pltpu.HBM((2, model, model), bf16),
         ),
         in_specs=[in_hbm] * 4,
-        out_specs=[in_vmem] * 5,
+        out_specs=[in_vmem] * 5 + [in_hbm],
         scratch_shapes=[
             pltpu.VMEM((model,), f32),
             pltpu.VMEM((HEAD_DIM,), f32),
             pltpu.VMEM((HEAD_DIM,), f32),
-            pltpu.SemaphoreType.DMA((4,)),
+            pltpu.VMEM((2, model, model), bf16),
+            pltpu.SemaphoreType.DMA((8,)),
         ],
-        compiler_params=pltpu.CompilerParams(vmem_limit_bytes=8 * 1024 * 1024),
-        cost_estimate=pl.CostEstimate(flops=0, bytes_accessed=4 * model * model, transcendentals=0),
+        compiler_params=pltpu.CompilerParams(vmem_limit_bytes=16 * 1024 * 1024),
+        cost_estimate=pl.CostEstimate(flops=0, bytes_accessed=12 * model * model, transcendentals=0),
         name="held",
     )(*held[:4])
     result = pl.pallas_call(
@@ -193,7 +201,7 @@
         in_specs=[in_vmem] * 6 + [in_hbm] * 2,
         out_specs=in_vmem,
         scratch_shapes=[
-            pltpu.VMEM((model, 2 * model), bf16),
+            pltpu.VMEM((2, model, model), bf16),
             pltpu.VMEM(w_out.shape, bf16),
             pltpu.VMEM((tokens, model), bf16),
             pltpu.VMEM((model, tokens), f32),
@@ -208,7 +216,7 @@
         ],
         compiler_params=pltpu.CompilerParams(vmem_limit_bytes=40 * 1024 * 1024),
         name="tokens",
-    )(gathered, gains, columns, member, spread, wq, *held[3:])
+    )(gathered, gains, columns, member, spread, wq, pltpu.with_memory_space_constraint(wkv, pltpu.HBM), held[4])
     return exchange(result).reshape(latent.shape)
 
 

time: 36.8 us -> 36.8 us (level)
  Pallas kernels: 6.36 us -> 9.54 us
  waiting for transfers between devices: 8.73 us -> 5.56 us
    all_to_all x1, waiting for transfers between devices: 8.73 us -> 5.56 us  [body(): gathered = exchange(latent.reshape(device_count, per_peer, model))]
    pallas_call x1, Pallas kernels: 1.84 us -> 5.01 us  [body(): pl.pallas_call(held_kernel, out_shape=(pltpu.VMEM((8, model), f32), pltpu...]
  transfers between devices with their start and end apart: 1 -> 1, of which waited for: 1 -> 1; matrix products, arithmetic and copies ran while one was open for 0% -> 0% of each run, Pallas kernels for 5% -> 14%
where the time goes in v14:
time: 36.8 us; the launch traced here: 36.6 us
  blocking collectives  13.3 us (36%)
  Pallas kernels  9.54 us (26%)
  starting transfers between devices  7.38 us (20%)
  waiting for transfers between devices  5.56 us (15%)
  local copies, waits for them, and re-layouts  0.71 us (2%)
    all_to_all x1, blocking collectives, body(): return exchange(result).reshape(latent.shape)  13.3 us
    all_to_all x1, starting transfers between devices, body(): gathered = exchange(latent.reshape(device_count, per_peer, model))  7.38 us
    all_to_all x1, waiting for transfers between devices, body(): gathered = exchange(latent.reshape(device_count, per_peer, model))  5.56 us
    pallas_call x1, Pallas kernels, body(): pl.pallas_call(held_kernel, out_shape=(pltpu.VMEM((8, model), f32), pltpu...  5.01 us
    pallas_call x1, Pallas kernels, body(): pl.pallas_call(tokens_kernel, out_shape=jax.ShapeDtypeStruct(gathered.sha...  4.53 us
  transfers between devices with their start and end apart: 1, of which 1 were waited for; matrix products, arithmetic and copies ran while one was open for 0% of the time, Pallas kernels for 14%

profile of v14, /device:TPU:0, one launch (start us, length us, event | category | flops | bytes accessed | tf_op | source)
XLA Modules:
  0.0 36.6 jit_solution(6610187851332293255)
XLA Ops:
  0.0 7.4 %all-to-all-start = ((bf16[16,8,1152]{2,1,0:T(8,128)(2,1)}), bf16[16,8,1152]{2,1,0:T(8,128)(2,1)S(1)}, u32[]{:S(2)}, u32[]{:S(2)}) async-start(bf16[16,8,1152]{2,1,0:T(8,128)(2,1)} %bitcast.3), calls=%async_computation | async-start | bytes 589824 | tf_op jit(solution)/shard_map/all_to_all | solution.py:170
  7.4 5.0 %held.1 = (f32[8,1152]{1,0:T(8,128)S(1)}, f32[72,128]{1,0:T(8,128)S(1)}, bf16[1152,128]{1,0:T(8,128)(2,1)S(1)}, bf16[32,1152]{1,0:T(8,128)(2,1)S(1)}, bf16[1152,...) custom-call(f32[1152]{0:T(1024)} %ln_ref.1, f32[72]{0:T(128)} %qg_ref.1, f32[72]{0:T(128)} %kg_ref.1, ...), custom_call_target="tpu_custom_call" | custom-call | bytes 15925248 | tf_op jit(solution)/shard_map/held/pallas_call | solution.py:175
  12.4 5.6 %all-to-all-done.x_ref = bf16[16,8,1152]{2,1,0:T(8,128)(2,1)S(1)} async-done(((bf16[16,8,1152]{2,1,0:T(8,128)(2,1)}), bf16[16,8,1152]{2,1,0:T(8,128)(2,1)S(1)}, u32[]{:S(2)}, u32[]{:S(2)}) %all-to-all-start) | async-done | bytes 294944 | tf_op jit(solution)/shard_map/all_to_all | solution.py:170
  18.0 4.5 %tokens.1 = bf16[16,8,1152]{2,1,0:T(8,128)(2,1)S(1)} custom-call(bf16[16,8,1152]{2,1,0:T(8,128)(2,1)S(1)} %all-to-all-done.x_ref, f32[8,1152]{1,0:T(8,128)S(1)} %get-tuple-element.11.gains_ref, f32[72,128]{1,0:T(8,128)S(1)} %get-tuple-element.12.columns_ref, bf16[1152,128]{1,0:T(8,128)(2,1)S(1)} %get-tuple-element.13.member_ref, ...), custom_call_target="tpu_custom_call" | custom-call | tf_op jit(solution)/shard_map/tokens/pallas_call | solution.py:198
  22.5 13.3 %all_to_all.10 = bf16[16,8,1152]{2,1,0:T(8,128)(2,1)S(1)} all-to-all(bf16[16,8,1152]{2,1,0:T(8,128)(2,1)S(1)} %tokens.1), channel_id=1, replica_groups={{0,1,4,5,8,9,12,13,2,3,6,7,10,11,14,15},{16,17,20,21,24,25,28,29,18,19,..., dimensions={0} | all-to-all | bytes 589824 | tf_op jit(solution)/shard_map/all_to_all | solution.py:220
  35.9 0.7 %copy.8 = bf16[4,32,1152]{2,1,0:T(8,128)(2,1)} copy(bf16[4,32,1152]{2,1,0:T(8,128)(2,1)S(1)} %bitcast.2) | data formatting | bytes 589824
Async XLA Ops:
  0.0 18.0 %all-to-all-start = ((bf16[16,8,1152]{2,1,0:T(8,128)(2,1)}), bf16[16,8,1152]{2,1,0:T(8,128)(2,1)S(1)}, u32[]{:S(2)}, u32[]{:S(2)}) async-start(bf16[16,8,1152]{2,1,0:T(8,128)(2,1)} %bitcast.3), calls=%async_computation | async-start | bytes 589824 | tf_op jit(solution)/shard_map/all_to_all | solution.py:170

commit v15 on v10

--- a/solution.py
+++ b/solution.py
@@ -13,6 +13,10 @@
 LANES = 128
 EPS = 1e-06
 EXP2_SCALE = HEAD_DIM**-0.5 * math.log2(math.e)
+
+
+def column_blocks(width):
+    return [slice(i, min(i + 2 * LANES, width)) for i in range(0, width, 2 * LANES)]
 
 
 def dot(a, b):
@@ -104,7 +108,8 @@
         out[...] = (mixed[...] * dot(parts, spread_ref[...]) * gains_ref[row : row + 1, :]).astype(bf16)
 
     copies[1].start()
-    mixed_q[...] = dot(normed[...], wq[...]).T
+    for block in column_blocks(width):
+        mixed_q[block, :] = dot(normed[...], wq[:, block]).T
     for pair in range(HEADS // 2):
         heads = []
         for first in (2 * pair * HEAD_DIM, (2 * pair + 1) * HEAD_DIM):
@@ -115,10 +120,13 @@
         queries_t[rows, :] = jnp.concatenate(heads, axis=0).astype(bf16)
     copies[0].wait()
     copies[2].start()
-    mixed_k[...] = dot(normed[...], wkv[:, :width])
+    for block in column_blocks(width):
+        mixed_k[:, block] = dot(normed[...], wkv[:, block])
     head_norm(mixed_k, 1, keys)
     copies[1].wait()
-    values_t[...] = dot(normed[...], wkv[:, width:]).astype(bf16).T
+    for block in column_blocks(width):
+        part = wkv[:, width + block.start : width + block.stop]
+        values_t[block, :] = dot(normed[...], part).astype(bf16).T
 
     place = lax.broadcasted_iota(jnp.int32, (tokens, tokens), 0) % positions
     other = lax.broadcasted_iota(jnp.int32, (tokens, tokens), 1) % positions
@@ -148,8 +156,9 @@
     attended[...] = attended_t[...].astype(bf16).T
 
     copies[2].wait()
-    branch = dot(attended[...], wout[...])
-    o_ref[...] = (x_ref[...].astype(f32) + branch.reshape(x_ref.shape)).astype(bf16)
+    for block in column_blocks(width):
+        branch = dot(attended[...], wout[:, block]).reshape(frames, positions, -1)
+        o_ref[:, :, block] = (x_ref[:, :, block].astype(f32) + branch).astype(bf16)
 
 
 def body(latent, ln_gain, q_gain, k_gain, w_qkv, w_out):

time: 36.8 us -> 36.8 us (level)
  no operation moved by 1% of the time
where the time goes in v15:
time: 36.8 us; the launch traced here: 36.6 us
  blocking collectives  13.3 us (36%)
  waiting for transfers between devices  8.73 us (24%)
  starting transfers between devices  7.39 us (20%)
  Pallas kernels  6.36 us (17%)
  local copies, waits for them, and re-layouts  0.71 us (2%)
    all_to_all x1, blocking collectives, body(): return exchange(result).reshape(latent.shape)  13.3 us
    all_to_all x1, waiting for transfers between devices, body(): gathered = exchange(latent.reshape(device_count, per_peer, model))  8.73 us
    all_to_all x1, starting transfers between devices, body(): gathered = exchange(latent.reshape(device_count, per_peer, model))  7.39 us
    pallas_call x1, Pallas kernels, body(): pl.pallas_call(tokens_kernel, out_shape=jax.ShapeDtypeStruct(gathered.sha...  4.53 us
    pallas_call x1, Pallas kernels, body(): pl.pallas_call(held_kernel, out_shape=(pltpu.VMEM((8, model), f32), pltpu...  1.84 us
  transfers between devices with their start and end apart: 1, of which 1 were waited for; matrix products, arithmetic and copies ran while one was open for 0% of the time, Pallas kernels for 5%

profile of v15, /device:TPU:0, one launch (start us, length us, event | category | flops | bytes accessed | tf_op | source)
XLA Modules:
  0.0 36.6 jit_solution(14860985435383518596)
XLA Ops:
  0.0 7.4 %all-to-all-start = ((bf16[16,8,1152]{2,1,0:T(8,128)(2,1)}), bf16[16,8,1152]{2,1,0:T(8,128)(2,1)S(1)}, u32[]{:S(2)}, u32[]{:S(2)}) async-start(bf16[16,8,1152]{2,1,0:T(8,128)(2,1)} %bitcast.3), calls=%async_computation | async-start | bytes 589824 | tf_op jit(solution)/shard_map/all_to_all | solution.py:173
  7.4 1.8 %held.1 = (f32[8,1152]{1,0:T(8,128)S(1)}, f32[72,128]{1,0:T(8,128)S(1)}, bf16[1152,128]{1,0:T(8,128)(2,1)S(1)}, bf16[32,1152]{1,0:T(8,128)(2,1)S(1)}, bf16[1152,1152]{1,0:T(8,128)(2,1)S(1)}) custom-call(f32[1152]{0:T(1024)} %ln_ref.1, f32[72]{0:T(128)} %qg_ref.1, f32[72]{0:T(128)} %kg_ref.1, bf16[1152,3456]{1,0:T(8,128)(2,1)} %wqkv_hbm.1), custom_call_target="tpu_custom_call" | custom-call | bytes 5308416 | tf_op jit(solution)/shard_map/held/pallas_call | solution.py:178
  9.2 8.7 %all-to-all-done.x_ref = bf16[16,8,1152]{2,1,0:T(8,128)(2,1)S(1)} async-done(((bf16[16,8,1152]{2,1,0:T(8,128)(2,1)}), bf16[16,8,1152]{2,1,0:T(8,128)(2,1)S(1)}, u32[]{:S(2)}, u32[]{:S(2)}) %all-to-all-start) | async-done | bytes 294944 | tf_op jit(solution)/shard_map/all_to_all | solution.py:173
  18.0 4.5 %tokens.1 = bf16[16,8,1152]{2,1,0:T(8,128)(2,1)S(1)} custom-call(bf16[16,8,1152]{2,1,0:T(8,128)(2,1)S(1)} %all-to-all-done.x_ref, f32[8,1152]{1,0:T(8,128)S(1)} %get-tuple-element.10.gains_ref, f32[72,128]{1,0:T(8,128)S(1)} %get-tuple-element.11.columns_ref, bf16[1152,128]{1,0:T(8,128)(2,1)S(1)} %get-tuple-element.12.member_ref, ...), custom_call_target="tpu_custom_call" | custom-call | tf_op jit(solution)/shard_map/tokens/pallas_call | solution.py:199
  22.5 13.3 %all_to_all.10 = bf16[16,8,1152]{2,1,0:T(8,128)(2,1)S(1)} all-to-all(bf16[16,8,1152]{2,1,0:T(8,128)(2,1)S(1)} %tokens.1), channel_id=1, replica_groups={{0,1,4,5,8,9,12,13,2,3,6,7,10,11,14,15},{16,17,20,21,24,25,28,29,18,19,..., dimensions={0} | all-to-all | bytes 589824 | tf_op jit(solution)/shard_map/all_to_all | solution.py:221
  35.8 0.7 %copy.8 = bf16[4,32,1152]{2,1,0:T(8,128)(2,1)} copy(bf16[4,32,1152]{2,1,0:T(8,128)(2,1)S(1)} %bitcast.2) | data formatting | bytes 589824
Async XLA Ops:
  0.0 18.0 %all-to-all-start = ((bf16[16,8,1152]{2,1,0:T(8,128)(2,1)}), bf16[16,8,1152]{2,1,0:T(8,128)(2,1)S(1)}, u32[]{:S(2)}, u32[]{:S(2)}) async-start(bf16[16,8,1152]{2,1,0:T(8,128)(2,1)} %bitcast.3), calls=%async_computation | async-start | bytes 589824 | tf_op jit(solution)/shard_map/all_to_all | solution.py:173

commit v16 on v10

--- a/solution.py
+++ b/solution.py
@@ -79,7 +79,8 @@
         (wout_hbm, wout),
     ]
     copies = [pltpu.make_async_copy(src, dst, sems.at[i]) for i, (src, dst) in enumerate(pairs)]
-    copies[0].start()
+    for part, copy in enumerate(copies):
+        copy.start(priority=min(part, 1))
 
     gain = gains_ref[0:1, :]
     step = max(1, 16 // positions)
@@ -103,7 +104,6 @@
         parts = jnp.where(lane < HEADS, high, low)[:, : 2 * HEADS]
         out[...] = (mixed[...] * dot(parts, spread_ref[...]) * gains_ref[row : row + 1, :]).astype(bf16)
 
-    copies[1].start()
     mixed_q[...] = dot(normed[...], wq[...]).T
     for pair in range(HEADS // 2):
         heads = []
@@ -114,7 +114,6 @@
         rows = slice(2 * pair * HEAD_DIM, (2 * pair + 2) * HEAD_DIM)
         queries_t[rows, :] = jnp.concatenate(heads, axis=0).astype(bf16)
     copies[0].wait()
-    copies[2].start()
     mixed_k[...] = dot(normed[...], wkv[:, :width])
     head_norm(mixed_k, 1, keys)
     copies[1].wait()

time: 36.8 us -> 36.8 us (level)
  no operation moved by 1% of the time
where the time goes in v16:
time: 36.8 us; the launch traced here: 36.6 us
  blocking collectives  13.4 us (36%)
  waiting for transfers between devices  8.73 us (24%)
  starting transfers between devices  7.39 us (20%)
  Pallas kernels  6.36 us (17%)
  local copies, waits for them, and re-layouts  0.71 us (2%)
    all_to_all x1, blocking collectives, body(): return exchange(result).reshape(latent.shape)  13.4 us
    all_to_all x1, waiting for transfers between devices, body(): gathered = exchange(latent.reshape(device_count, per_peer, model))  8.73 us
    all_to_all x1, starting transfers between devices, body(): gathered = exchange(latent.reshape(device_count, per_peer, model))  7.39 us
    pallas_call x1, Pallas kernels, body(): pl.pallas_call(tokens_kernel, out_shape=jax.ShapeDtypeStruct(gathered.sha...  4.52 us
    pallas_call x1, Pallas kernels, body(): pl.pallas_call(held_kernel, out_shape=(pltpu.VMEM((8, model), f32), pltpu...  1.84 us
  transfers between devices with their start and end apart: 1, of which 1 were waited for; matrix products, arithmetic and copies ran while one was open for 0% of the time, Pallas kernels for 5%

profile of v16, /device:TPU:0, one launch (start us, length us, event | category | flops | bytes accessed | tf_op | source)
XLA Modules:
  0.0 36.6 jit_solution(9084101781524177987)
XLA Ops:
  0.0 7.4 %all-to-all-start = ((bf16[16,8,1152]{2,1,0:T(8,128)(2,1)}), bf16[16,8,1152]{2,1,0:T(8,128)(2,1)S(1)}, u32[]{:S(2)}, u32[]{:S(2)}) async-start(bf16[16,8,1152]{2,1,0:T(8,128)(2,1)} %bitcast.3), calls=%async_computation | async-start | bytes 589824 | tf_op jit(solution)/shard_map/all_to_all | solution.py:163
  7.4 1.8 %held.1 = (f32[8,1152]{1,0:T(8,128)S(1)}, f32[72,128]{1,0:T(8,128)S(1)}, bf16[1152,128]{1,0:T(8,128)(2,1)S(1)}, bf16[32,1152]{1,0:T(8,128)(2,1)S(1)}, bf16[1152,1152]{1,0:T(8,128)(2,1)S(1)}) custom-call(f32[1152]{0:T(1024)} %ln_ref.1, f32[72]{0:T(128)} %qg_ref.1, f32[72]{0:T(128)} %kg_ref.1, bf16[1152,3456]{1,0:T(8,128)(2,1)} %wqkv_hbm.1), custom_call_target="tpu_custom_call" | custom-call | bytes 5308416 | tf_op jit(solution)/shard_map/held/pallas_call | solution.py:168
  9.2 8.7 %all-to-all-done.x_ref = bf16[16,8,1152]{2,1,0:T(8,128)(2,1)S(1)} async-done(((bf16[16,8,1152]{2,1,0:T(8,128)(2,1)}), bf16[16,8,1152]{2,1,0:T(8,128)(2,1)S(1)}, u32[]{:S(2)}, u32[]{:S(2)}) %all-to-all-start) | async-done | bytes 294944 | tf_op jit(solution)/shard_map/all_to_all | solution.py:163
  18.0 4.5 %tokens.1 = bf16[16,8,1152]{2,1,0:T(8,128)(2,1)S(1)} custom-call(bf16[16,8,1152]{2,1,0:T(8,128)(2,1)S(1)} %all-to-all-done.x_ref, f32[8,1152]{1,0:T(8,128)S(1)} %get-tuple-element.10.gains_ref, f32[72,128]{1,0:T(8,128)S(1)} %get-tuple-element.11.columns_ref, bf16[1152,128]{1,0:T(8,128)(2,1)S(1)} %get-tuple-element.12.member_ref, ...), custom_call_target="tpu_custom_call" | custom-call | tf_op jit(solution)/shard_map/tokens/pallas_call | solution.py:189
  22.5 13.4 %all_to_all.10 = bf16[16,8,1152]{2,1,0:T(8,128)(2,1)S(1)} all-to-all(bf16[16,8,1152]{2,1,0:T(8,128)(2,1)S(1)} %tokens.1), channel_id=1, replica_groups={{0,1,4,5,8,9,12,13,2,3,6,7,10,11,14,15},{16,17,20,21,24,25,28,29,18,19,..., dimensions={0} | all-to-all | bytes 589824 | tf_op jit(solution)/shard_map/all_to_all | solution.py:211
  35.8 0.7 %copy.8 = bf16[4,32,1152]{2,1,0:T(8,128)(2,1)} copy(bf16[4,32,1152]{2,1,0:T(8,128)(2,1)S(1)} %bitcast.2) | data formatting | bytes 589824
Async XLA Ops:
  0.0 18.0 %all-to-all-start = ((bf16[16,8,1152]{2,1,0:T(8,128)(2,1)}), bf16[16,8,1152]{2,1,0:T(8,128)(2,1)S(1)}, u32[]{:S(2)}, u32[]{:S(2)}) async-start(bf16[16,8,1152]{2,1,0:T(8,128)(2,1)} %bitcast.3), calls=%async_computation | async-start | bytes 589824 | tf_op jit(solution)/shard_map/all_to_all | solution.py:163

commit v17 on v16

--- a/solution.py
+++ b/solution.py
@@ -80,7 +80,7 @@
     ]
     copies = [pltpu.make_async_copy(src, dst, sems.at[i]) for i, (src, dst) in enumerate(pairs)]
     for part, copy in enumerate(copies):
-        copy.start(priority=min(part, 1))
+        copy.start(priority=int(part == 0))
 
     gain = gains_ref[0:1, :]
     step = max(1, 16 // positions)

time: 36.8 us -> 38.4 us (1.043)
  Pallas kernels: 6.36 us -> 7.95 us
    pallas_call x1, Pallas kernels: 4.52 us -> 6.12 us  [body(): pl.pallas_call(tokens_kernel, out_shape=jax.ShapeDtypeStruct(gathered.sha...]
where the time goes in v17:
time: 38.4 us; the launch traced here: 38.2 us
  blocking collectives  13.3 us (35%)
  waiting for transfers between devices  8.73 us (23%)
  Pallas kernels  7.95 us (21%)
  starting transfers between devices  7.39 us (19%)
  local copies, waits for them, and re-layouts  0.71 us (2%)
    all_to_all x1, blocking collectives, body(): return exchange(result).reshape(latent.shape)  13.3 us
    all_to_all x1, waiting for transfers between devices, body(): gathered = exchange(latent.reshape(device_count, per_peer, model))  8.73 us
    all_to_all x1, starting transfers between devices, body(): gathered = exchange(latent.reshape(device_count, per_peer, model))  7.39 us
    pallas_call x1, Pallas kernels, body(): pl.pallas_call(tokens_kernel, out_shape=jax.ShapeDtypeStruct(gathered.sha...  6.12 us
    pallas_call x1, Pallas kernels, body(): pl.pallas_call(held_kernel, out_shape=(pltpu.VMEM((8, model), f32), pltpu...  1.84 us
  transfers between devices with their start and end apart: 1, of which 1 were waited for; matrix products, arithmetic and copies ran while one was open for 0% of the time, Pallas kernels for 5%

profile of v17, /device:TPU:0, one launch (start us, length us, event | category | flops | bytes accessed | tf_op | source)
XLA Modules:
  0.0 38.2 jit_solution(9933647082871603929)
XLA Ops:
  0.0 7.4 %all-to-all-start = ((bf16[16,8,1152]{2,1,0:T(8,128)(2,1)}), bf16[16,8,1152]{2,1,0:T(8,128)(2,1)S(1)}, u32[]{:S(2)}, u32[]{:S(2)}) async-start(bf16[16,8,1152]{2,1,0:T(8,128)(2,1)} %bitcast.3), calls=%async_computation | async-start | bytes 589824 | tf_op jit(solution)/shard_map/all_to_all | solution.py:163
  7.4 1.8 %held.1 = (f32[8,1152]{1,0:T(8,128)S(1)}, f32[72,128]{1,0:T(8,128)S(1)}, bf16[1152,128]{1,0:T(8,128)(2,1)S(1)}, bf16[32,1152]{1,0:T(8,128)(2,1)S(1)}, bf16[1152,1152]{1,0:T(8,128)(2,1)S(1)}) custom-call(f32[1152]{0:T(1024)} %ln_ref.1, f32[72]{0:T(128)} %qg_ref.1, f32[72]{0:T(128)} %kg_ref.1, bf16[1152,3456]{1,0:T(8,128)(2,1)} %wqkv_hbm.1), custom_call_target="tpu_custom_call" | custom-call | bytes 5308416 | tf_op jit(solution)/shard_map/held/pallas_call | solution.py:168
  9.2 8.7 %all-to-all-done.x_ref = bf16[16,8,1152]{2,1,0:T(8,128)(2,1)S(1)} async-done(((bf16[16,8,1152]{2,1,0:T(8,128)(2,1)}), bf16[16,8,1152]{2,1,0:T(8,128)(2,1)S(1)}, u32[]{:S(2)}, u32[]{:S(2)}) %all-to-all-start) | async-done | bytes 294944 | tf_op jit(solution)/shard_map/all_to_all | solution.py:163
  18.0 6.1 %tokens.1 = bf16[16,8,1152]{2,1,0:T(8,128)(2,1)S(1)} custom-call(bf16[16,8,1152]{2,1,0:T(8,128)(2,1)S(1)} %all-to-all-done.x_ref, f32[8,1152]{1,0:T(8,128)S(1)} %get-tuple-element.10.gains_ref, f32[72,128]{1,0:T(8,128)S(1)} %get-tuple-element.11.columns_ref, bf16[1152,128]{1,0:T(8,128)(2,1)S(1)} %get-tuple-element.12.member_ref, ...), custom_call_target="tpu_custom_call" | custom-call | tf_op jit(solution)/shard_map/tokens/pallas_call | solution.py:189
  24.1 13.3 %all_to_all.10 = bf16[16,8,1152]{2,1,0:T(8,128)(2,1)S(1)} all-to-all(bf16[16,8,1152]{2,1,0:T(8,128)(2,1)S(1)} %tokens.1), channel_id=1, replica_groups={{0,1,4,5,8,9,12,13,2,3,6,7,10,11,14,15},{16,17,20,21,24,25,28,29,18,19,..., dimensions={0} | all-to-all | bytes 589824 | tf_op jit(solution)/shard_map/all_to_all | solution.py:211
  37.4 0.7 %copy.8 = bf16[4,32,1152]{2,1,0:T(8,128)(2,1)} copy(bf16[4,32,1152]{2,1,0:T(8,128)(2,1)S(1)} %bitcast.2) | data formatting | bytes 589824
Async XLA Ops:
  0.0 18.0 %all-to-all-start = ((bf16[16,8,1152]{2,1,0:T(8,128)(2,1)}), bf16[16,8,1152]{2,1,0:T(8,128)(2,1)S(1)}, u32[]{:S(2)}, u32[]{:S(2)}) async-start(bf16[16,8,1152]{2,1,0:T(8,128)(2,1)} %bitcast.3), calls=%async_computation | async-start | bytes 589824 | tf_op jit(solution)/shard_map/all_to_all | solution.py:163

commit v18 on v10

--- a/solution.py
+++ b/solution.py
@@ -80,6 +80,7 @@
     ]
     copies = [pltpu.make_async_copy(src, dst, sems.at[i]) for i, (src, dst) in enumerate(pairs)]
     copies[0].start()
+    copies[2].start(priority=1)
 
     gain = gains_ref[0:1, :]
     step = max(1, 16 // positions)
@@ -114,7 +115,6 @@
         rows = slice(2 * pair * HEAD_DIM, (2 * pair + 2) * HEAD_DIM)
         queries_t[rows, :] = jnp.concatenate(heads, axis=0).astype(bf16)
     copies[0].wait()
-    copies[2].start()
     mixed_k[...] = dot(normed[...], wkv[:, :width])
     head_norm(mixed_k, 1, keys)
     copies[1].wait()

time: 36.8 us -> 36.8 us (level)
  no operation moved by 1% of the time
where the time goes in v18:
time: 36.8 us; the launch traced here: 36.6 us
  blocking collectives  13.4 us (36%)
  waiting for transfers between devices  8.73 us (24%)
  starting transfers between devices  7.39 us (20%)
  Pallas kernels  6.36 us (17%)
  local copies, waits for them, and re-layouts  0.71 us (2%)
    all_to_all x1, blocking collectives, body(): return exchange(result).reshape(latent.shape)  13.4 us
    all_to_all x1, waiting for transfers between devices, body(): gathered = exchange(latent.reshape(device_count, per_peer, model))  8.73 us
    all_to_all x1, starting transfers between devices, body(): gathered = exchange(latent.reshape(device_count, per_peer, model))  7.39 us
    pallas_call x1, Pallas kernels, body(): pl.pallas_call(tokens_kernel, out_shape=jax.ShapeDtypeStruct(gathered.sha...  4.52 us
    pallas_call x1, Pallas kernels, body(): pl.pallas_call(held_kernel, out_shape=(pltpu.VMEM((8, model), f32), pltpu...  1.84 us
  transfers between devices with their start and end apart: 1, of which 1 were waited for; matrix products, arithmetic and copies ran while one was open for 0% of the time, Pallas kernels for 5%

profile of v18, /device:TPU:0, one launch (start us, length us, event | category | flops | bytes accessed | tf_op | source)
XLA Modules:
  0.0 36.6 jit_solution(2273719744448163694)
XLA Ops:
  0.0 7.4 %all-to-all-start = ((bf16[16,8,1152]{2,1,0:T(8,128)(2,1)}), bf16[16,8,1152]{2,1,0:T(8,128)(2,1)S(1)}, u32[]{:S(2)}, u32[]{:S(2)}) async-start(bf16[16,8,1152]{2,1,0:T(8,128)(2,1)} %bitcast.3), calls=%async_computation | async-start | bytes 589824 | tf_op jit(solution)/shard_map/all_to_all | solution.py:164
  7.4 1.8 %held.1 = (f32[8,1152]{1,0:T(8,128)S(1)}, f32[72,128]{1,0:T(8,128)S(1)}, bf16[1152,128]{1,0:T(8,128)(2,1)S(1)}, bf16[32,1152]{1,0:T(8,128)(2,1)S(1)}, bf16[1152,1152]{1,0:T(8,128)(2,1)S(1)}) custom-call(f32[1152]{0:T(1024)} %ln_ref.1, f32[72]{0:T(128)} %qg_ref.1, f32[72]{0:T(128)} %kg_ref.1, bf16[1152,3456]{1,0:T(8,128)(2,1)} %wqkv_hbm.1), custom_call_target="tpu_custom_call" | custom-call | bytes 5308416 | tf_op jit(solution)/shard_map/held/pallas_call | solution.py:169
  9.2 8.7 %all-to-all-done.x_ref = bf16[16,8,1152]{2,1,0:T(8,128)(2,1)S(1)} async-done(((bf16[16,8,1152]{2,1,0:T(8,128)(2,1)}), bf16[16,8,1152]{2,1,0:T(8,128)(2,1)S(1)}, u32[]{:S(2)}, u32[]{:S(2)}) %all-to-all-start) | async-done | bytes 294944 | tf_op jit(solution)/shard_map/all_to_all | solution.py:164
  18.0 4.5 %tokens.1 = bf16[16,8,1152]{2,1,0:T(8,128)(2,1)S(1)} custom-call(bf16[16,8,1152]{2,1,0:T(8,128)(2,1)S(1)} %all-to-all-done.x_ref, f32[8,1152]{1,0:T(8,128)S(1)} %get-tuple-element.10.gains_ref, f32[72,128]{1,0:T(8,128)S(1)} %get-tuple-element.11.columns_ref, bf16[1152,128]{1,0:T(8,128)(2,1)S(1)} %get-tuple-element.12.member_ref, ...), custom_call_target="tpu_custom_call" | custom-call | tf_op jit(solution)/shard_map/tokens/pallas_call | solution.py:190
  22.5 13.4 %all_to_all.10 = bf16[16,8,1152]{2,1,0:T(8,128)(2,1)S(1)} all-to-all(bf16[16,8,1152]{2,1,0:T(8,128)(2,1)S(1)} %tokens.1), channel_id=1, replica_groups={{0,1,4,5,8,9,12,13,2,3,6,7,10,11,14,15},{16,17,20,21,24,25,28,29,18,19,..., dimensions={0} | all-to-all | bytes 589824 | tf_op jit(solution)/shard_map/all_to_all | solution.py:212
  35.8 0.7 %copy.8 = bf16[4,32,1152]{2,1,0:T(8,128)(2,1)} copy(bf16[4,32,1152]{2,1,0:T(8,128)(2,1)S(1)} %bitcast.2) | data formatting | bytes 589824
Async XLA Ops:
  0.0 18.0 %all-to-all-start = ((bf16[16,8,1152]{2,1,0:T(8,128)(2,1)}), bf16[16,8,1152]{2,1,0:T(8,128)(2,1)S(1)}, u32[]{:S(2)}, u32[]{:S(2)}) async-start(bf16[16,8,1152]{2,1,0:T(8,128)(2,1)} %bitcast.3), calls=%async_computation | async-start | bytes 589824 | tf_op jit(solution)/shard_map/all_to_all | solution.py:164

commit v19 on v18

--- a/solution.py
+++ b/solution.py
@@ -66,6 +66,7 @@
     values_t,
     attended_t,
     attended,
+    branch,
     same,
     sems,
 ):
@@ -125,7 +126,12 @@
     same[...] = (place == other).astype(f32)
 
     row = lax.broadcasted_iota(jnp.int32, (2 * LANES, tokens), 0)
+    done = HEADS // 4 * LANES
     for pair in range(HEADS // 2):
+        if pair == HEADS // 4:
+            copies[2].wait()
+            attended[:, :done] = attended_t[:done, :].astype(bf16).T
+            branch[...] = dot(attended[:, :done], wout[:done, :])
         window = slice(pair * LANES, (pair + 2) * LANES)
         begin = pair * (2 * HEAD_DIM - LANES)
         query = queries_t[window, :]
@@ -145,11 +151,9 @@
             attended_t[first : first + HEAD_DIM, :] = heads_out[
                 h * HEAD_DIM : (h + 1) * HEAD_DIM, h * tokens : (h + 1) * tokens
             ]
-    attended[...] = attended_t[...].astype(bf16).T
-
-    copies[2].wait()
-    branch = dot(attended[...], wout[...])
-    o_ref[...] = (x_ref[...].astype(f32) + branch.reshape(x_ref.shape)).astype(bf16)
+    attended[:, done:] = attended_t[done:, :].astype(bf16).T
+    total = branch[...] + dot(attended[:, done:], wout[done:, :])
+    o_ref[...] = (x_ref[...].astype(f32) + total.reshape(x_ref.shape)).astype(bf16)
 
 
 def body(latent, ln_gain, q_gain, k_gain, w_qkv, w_out):
@@ -203,6 +207,7 @@
             pltpu.VMEM((model, tokens), bf16),
             pltpu.VMEM((model, tokens), f32),
             pltpu.VMEM((tokens, model), bf16),
+            pltpu.VMEM((tokens, model), f32),
             pltpu.VMEM((tokens, tokens), f32),
             pltpu.SemaphoreType.DMA((3,)),
         ],

time: 36.8 us -> 37.1 us (level)
  no operation moved by 1% of the time
where the time goes in v19:
time: 37.1 us; the launch traced here: 36.8 us
  blocking collectives  13.4 us (36%)
  waiting for transfers between devices  8.73 us (24%)
  starting transfers between devices  7.39 us (20%)
  Pallas kernels  6.64 us (18%)
  local copies, waits for them, and re-layouts  0.71 us (2%)
    all_to_all x1, blocking collectives, body(): return exchange(result).reshape(latent.shape)  13.4 us
    all_to_all x1, waiting for transfers between devices, body(): gathered = exchange(latent.reshape(device_count, per_peer, model))  8.73 us
    all_to_all x1, starting transfers between devices, body(): gathered = exchange(latent.reshape(device_count, per_peer, model))  7.39 us
    pallas_call x1, Pallas kernels, body(): pl.pallas_call(tokens_kernel, out_shape=jax.ShapeDtypeStruct(gathered.sha...  4.8 us
    pallas_call x1, Pallas kernels, body(): pl.pallas_call(held_kernel, out_shape=(pltpu.VMEM((8, model), f32), pltpu...  1.84 us
  transfers between devices with their start and end apart: 1, of which 1 were waited for; matrix products, arithmetic and copies ran while one was open for 0% of the time, Pallas kernels for 5%

profile of v19, /device:TPU:0, one launch (start us, length us, event | category | flops | bytes accessed | tf_op | source)
XLA Modules:
  0.0 36.8 jit_solution(13292703466627195062)
XLA Ops:
  0.0 7.4 %all-to-all-start = ((bf16[16,8,1152]{2,1,0:T(8,128)(2,1)}), bf16[16,8,1152]{2,1,0:T(8,128)(2,1)S(1)}, u32[]{:S(2)}, u32[]{:S(2)}) async-start(bf16[16,8,1152]{2,1,0:T(8,128)(2,1)} %bitcast.3), calls=%async_computation | async-start | bytes 589824 | tf_op jit(solution)/shard_map/all_to_all | solution.py:168
  7.4 1.8 %held.1 = (f32[8,1152]{1,0:T(8,128)S(1)}, f32[72,128]{1,0:T(8,128)S(1)}, bf16[1152,128]{1,0:T(8,128)(2,1)S(1)}, bf16[32,1152]{1,0:T(8,128)(2,1)S(1)}, bf16[1152,1152]{1,0:T(8,128)(2,1)S(1)}) custom-call(f32[1152]{0:T(1024)} %ln_ref.1, f32[72]{0:T(128)} %qg_ref.1, f32[72]{0:T(128)} %kg_ref.1, bf16[1152,3456]{1,0:T(8,128)(2,1)} %wqkv_hbm.1), custom_call_target="tpu_custom_call" | custom-call | bytes 5308416 | tf_op jit(solution)/shard_map/held/pallas_call | solution.py:173
  9.2 8.7 %all-to-all-done.x_ref = bf16[16,8,1152]{2,1,0:T(8,128)(2,1)S(1)} async-done(((bf16[16,8,1152]{2,1,0:T(8,128)(2,1)}), bf16[16,8,1152]{2,1,0:T(8,128)(2,1)S(1)}, u32[]{:S(2)}, u32[]{:S(2)}) %all-to-all-start) | async-done | bytes 294944 | tf_op jit(solution)/shard_map/all_to_all | solution.py:168
  18.0 4.8 %tokens.1 = bf16[16,8,1152]{2,1,0:T(8,128)(2,1)S(1)} custom-call(bf16[16,8,1152]{2,1,0:T(8,128)(2,1)S(1)} %all-to-all-done.x_ref, f32[8,1152]{1,0:T(8,128)S(1)} %get-tuple-element.10.gains_ref, f32[72,128]{1,0:T(8,128)S(1)} %get-tuple-element.11.columns_ref, bf16[1152,128]{1,0:T(8,128)(2,1)S(1)} %get-tuple-element.12.member_ref, ...), custom_call_target="tpu_custom_call" | custom-call | tf_op jit(solution)/shard_map/tokens/pallas_call | solution.py:194
  22.8 13.4 %all_to_all.10 = bf16[16,8,1152]{2,1,0:T(8,128)(2,1)S(1)} all-to-all(bf16[16,8,1152]{2,1,0:T(8,128)(2,1)S(1)} %tokens.1), channel_id=1, replica_groups={{0,1,4,5,8,9,12,13,2,3,6,7,10,11,14,15},{16,17,20,21,24,25,28,29,18,19,..., dimensions={0} | all-to-all | bytes 589824 | tf_op jit(solution)/shard_map/all_to_all | solution.py:217
  36.1 0.7 %copy.8 = bf16[4,32,1152]{2,1,0:T(8,128)(2,1)} copy(bf16[4,32,1152]{2,1,0:T(8,128)(2,1)S(1)} %bitcast.2) | data formatting | bytes 589824
Async XLA Ops:
  0.0 18.0 %all-to-all-start = ((bf16[16,8,1152]{2,1,0:T(8,128)(2,1)}), bf16[16,8,1152]{2,1,0:T(8,128)(2,1)S(1)}, u32[]{:S(2)}, u32[]{:S(2)}) async-start(bf16[16,8,1152]{2,1,0:T(8,128)(2,1)} %bitcast.3), calls=%async_computation | async-start | bytes 589824 | tf_op jit(solution)/shard_map/all_to_all | solution.py:168

commit v20 on v10

--- a/solution.py
+++ b/solution.py
@@ -20,10 +20,10 @@
 
 
 def held_kernel(
-    ln_ref, qg_ref, kg_ref, wqkv_ref, gains_out, columns_out, member_out, spread_out, wq_out, ln, qg, kg, sems
+    ln_ref, qg_ref, kg_ref, wqkv_ref, gains_out, columns_out, member_out, spread_out, wq_out, ln, qg, kg, wq, sems
 ):
     width = wq_out.shape[1]
-    pairs = [(ln_ref, ln), (qg_ref, qg), (kg_ref, kg), (wqkv_ref.at[:, pl.ds(0, width)], wq_out)]
+    pairs = [(ln_ref, ln), (qg_ref, qg), (kg_ref, kg), (wqkv_ref.at[:, pl.ds(0, width)], wq)]
     copies = [pltpu.make_async_copy(src, dst, sems.at[i]) for i, (src, dst) in enumerate(pairs)]
     for copy in copies:
         copy.start()
@@ -44,6 +44,8 @@
     columns_out[...] = jnp.broadcast_to(row, (LANES, LANES)).T[:HEAD_DIM]
     gains_out[1:2, :] = jnp.concatenate([kg[...].reshape(1, HEAD_DIM)] * HEADS, axis=1)
     copies[3].wait()
+    for row in range(0, width, LANES):
+        wq_out[:, row : row + LANES] = wq[row : row + LANES, :].T
 
 
 def tokens_kernel(
@@ -59,7 +61,7 @@
     wkv,
     wout,
     normed,
-    mixed_q,
+    normed_t,
     mixed_k,
     queries_t,
     keys,
@@ -104,15 +106,16 @@
         out[...] = (mixed[...] * dot(parts, spread_ref[...]) * gains_ref[row : row + 1, :]).astype(bf16)
 
     copies[1].start()
-    mixed_q[...] = dot(normed[...], wq[...]).T
-    for pair in range(HEADS // 2):
+    normed_t[...] = normed[...].T
+    span = 4 * HEAD_DIM
+    for begin in range(0, width, span):
+        mixed = dot(wq[begin : begin + span, :], normed_t[...])
         heads = []
-        for first in (2 * pair * HEAD_DIM, (2 * pair + 1) * HEAD_DIM):
-            head = mixed_q[first : first + HEAD_DIM, :]
+        for first in range(0, span, HEAD_DIM):
+            head = mixed[first : first + HEAD_DIM, :]
             total = jnp.sum(head * head, axis=0, keepdims=True)
             heads.append(head * lax.rsqrt(total * (1.0 / HEAD_DIM) + EPS) * columns_ref[...])
-        rows = slice(2 * pair * HEAD_DIM, (2 * pair + 2) * HEAD_DIM)
-        queries_t[rows, :] = jnp.concatenate(heads, axis=0).astype(bf16)
+        queries_t[begin : begin + span, :] = jnp.concatenate(heads, axis=0).astype(bf16)
     copies[0].wait()
     copies[2].start()
     mixed_k[...] = dot(normed[...], wkv[:, :width])
@@ -181,6 +184,7 @@
             pltpu.VMEM((model,), f32),
             pltpu.VMEM((HEAD_DIM,), f32),
             pltpu.VMEM((HEAD_DIM,), f32),
+            pltpu.VMEM((model, model), bf16),
             pltpu.SemaphoreType.DMA((4,)),
         ],
         compiler_params=pltpu.CompilerParams(vmem_limit_bytes=8 * 1024 * 1024),
@@ -196,7 +200,7 @@
             pltpu.VMEM((model, 2 * model), bf16),
             pltpu.VMEM(w_out.shape, bf16),
             pltpu.VMEM((tokens, model), bf16),
-            pltpu.VMEM((model, tokens), f32),
+            pltpu.VMEM((model, tokens), bf16),
             pltpu.VMEM((tokens, model), f32),
             pltpu.VMEM((model, tokens), bf16),
             pltpu.VMEM((tokens, model), bf16),

time: 36.8 us -> 38 us (1.033)
  Pallas kernels: 6.36 us -> 8.28 us
  waiting for transfers between devices: 8.73 us -> 7.98 us
    pallas_call x1, Pallas kernels: 4.52 us -> 5.7 us  [body(): pl.pallas_call(tokens_kernel, out_shape=jax.ShapeDtypeStruct(gathered.sha...]
    all_to_all x1, waiting for transfers between devices: 8.73 us -> 7.98 us  [body(): gathered = exchange(latent.reshape(device_count, per_peer, model))]
    pallas_call x1, Pallas kernels: 1.84 us -> 2.58 us  [body(): pl.pallas_call(held_kernel, out_shape=(pltpu.VMEM((8, model), f32), pltpu...]
  transfers between devices with their start and end apart: 1 -> 1, of which waited for: 1 -> 1; matrix products, arithmetic and copies ran while one was open for 0% -> 0% of each run, Pallas kernels for 5% -> 7%
where the time goes in v20:
time: 38 us; the launch traced here: 37.7 us
  blocking collectives  13.4 us (35%)
  Pallas kernels  8.28 us (22%)
  waiting for transfers between devices  7.98 us (21%)
  starting transfers between devices  7.39 us (19%)
  local copies, waits for them, and re-layouts  0.71 us (2%)
    all_to_all x1, blocking collectives, body(): return exchange(result).reshape(latent.shape)  13.4 us
    all_to_all x1, waiting for transfers between devices, body(): gathered = exchange(latent.reshape(device_count, per_peer, model))  7.98 us
    all_to_all x1, starting transfers between devices, body(): gathered = exchange(latent.reshape(device_count, per_peer, model))  7.39 us
    pallas_call x1, Pallas kernels, body(): pl.pallas_call(tokens_kernel, out_shape=jax.ShapeDtypeStruct(gathered.sha...  5.7 us
    pallas_call x1, Pallas kernels, body(): pl.pallas_call(held_kernel, out_shape=(pltpu.VMEM((8, model), f32), pltpu...  2.58 us
  transfers between devices with their start and end apart: 1, of which 1 were waited for; matrix products, arithmetic and copies ran while one was open for 0% of the time, Pallas kernels for 7%

profile of v20, /device:TPU:0, one launch (start us, length us, event | category | flops | bytes accessed | tf_op | source)
XLA Modules:
  0.0 37.7 jit_solution(9321025536603110351)
XLA Ops:
  0.0 7.4 %all-to-all-start = ((bf16[16,8,1152]{2,1,0:T(8,128)(2,1)}), bf16[16,8,1152]{2,1,0:T(8,128)(2,1)S(1)}, u32[]{:S(2)}, u32[]{:S(2)}) async-start(bf16[16,8,1152]{2,1,0:T(8,128)(2,1)} %bitcast.3), calls=%async_computation | async-start | bytes 589824 | tf_op jit(solution)/shard_map/all_to_all | solution.py:167
  7.4 2.6 %held.1 = (f32[8,1152]{1,0:T(8,128)S(1)}, f32[72,128]{1,0:T(8,128)S(1)}, bf16[1152,128]{1,0:T(8,128)(2,1)S(1)}, bf16[32,1152]{1,0:T(8,128)(2,1)S(1)}, bf16[1152,1152]{1,0:T(8,128)(2,1)S(1)}) custom-call(f32[1152]{0:T(1024)} %ln_ref.1, f32[72]{0:T(128)} %qg_ref.1, f32[72]{0:T(128)} %kg_ref.1, bf16[1152,3456]{1,0:T(8,128)(2,1)} %wqkv_hbm.1), custom_call_target="tpu_custom_call" | custom-call | bytes 5308416 | tf_op jit(solution)/shard_map/held/pallas_call | solution.py:172
  10.0 8.0 %all-to-all-done.x_ref = bf16[16,8,1152]{2,1,0:T(8,128)(2,1)S(1)} async-done(((bf16[16,8,1152]{2,1,0:T(8,128)(2,1)}), bf16[16,8,1152]{2,1,0:T(8,128)(2,1)S(1)}, u32[]{:S(2)}, u32[]{:S(2)}) %all-to-all-start) | async-done | bytes 294944 | tf_op jit(solution)/shard_map/all_to_all | solution.py:167
  18.0 5.7 %tokens.1 = bf16[16,8,1152]{2,1,0:T(8,128)(2,1)S(1)} custom-call(bf16[16,8,1152]{2,1,0:T(8,128)(2,1)S(1)} %all-to-all-done.x_ref, f32[8,1152]{1,0:T(8,128)S(1)} %get-tuple-element.10.gains_ref, f32[72,128]{1,0:T(8,128)S(1)} %get-tuple-element.11.columns_ref, bf16[1152,128]{1,0:T(8,128)(2,1)S(1)} %get-tuple-element.12.member_ref, ...), custom_call_target="tpu_custom_call" | custom-call | tf_op jit(solution)/shard_map/tokens/pallas_call | solution.py:194
  23.7 13.4 %all_to_all.10 = bf16[16,8,1152]{2,1,0:T(8,128)(2,1)S(1)} all-to-all(bf16[16,8,1152]{2,1,0:T(8,128)(2,1)S(1)} %tokens.1), channel_id=1, replica_groups={{0,1,4,5,8,9,12,13,2,3,6,7,10,11,14,15},{16,17,20,21,24,25,28,29,18,19,..., dimensions={0} | all-to-all | bytes 589824 | tf_op jit(solution)/shard_map/all_to_all | solution.py:216
  37.0 0.7 %copy.8 = bf16[4,32,1152]{2,1,0:T(8,128)(2,1)} copy(bf16[4,32,1152]{2,1,0:T(8,128)(2,1)S(1)} %bitcast.2) | data formatting | bytes 589824
Async XLA Ops:
  0.0 18.0 %all-to-all-start = ((bf16[16,8,1152]{2,1,0:T(8,128)(2,1)}), bf16[16,8,1152]{2,1,0:T(8,128)(2,1)S(1)}, u32[]{:S(2)}, u32[]{:S(2)}) async-start(bf16[16,8,1152]{2,1,0:T(8,128)(2,1)} %bitcast.3), calls=%async_computation | async-start | bytes 589824 | tf_op jit(solution)/shard_map/all_to_all | solution.py:167

commit v21 on v10

--- a/solution.py
+++ b/solution.py
@@ -157,7 +157,7 @@
     rows, columns, model = latent.shape
     tokens = rows * columns
     per_peer = tokens // device_count
-    order = [4 * i + 2 * row + core for row in range(2) for i in range(device_count // 4) for core in range(2)]
+    order = [4 * i + 2 * row + core for core in range(2) for row in range(2) for i in range(device_count // 4)]
     exchange = functools.partial(
         lax.all_to_all, axis_name="frame", split_axis=0, concat_axis=0, axis_index_groups=[order], tiled=True
     )

time: 36.8 us -> 37.6 us (1.022)
  blocking collectives: 13.4 us -> 13.9 us
    all_to_all x1, blocking collectives: 13.4 us -> 13.9 us  [body(): return exchange(result).reshape(latent.shape)]
where the time goes in v21:
time: 37.6 us; the launch traced here: 37.3 us
  blocking collectives  13.9 us (37%)
  waiting for transfers between devices  8.92 us (24%)
  starting transfers between devices  7.39 us (20%)
  Pallas kernels  6.36 us (17%)
  local copies, waits for them, and re-layouts  0.71 us (2%)
    all_to_all x1, blocking collectives, body(): return exchange(result).reshape(latent.shape)  13.9 us
    all_to_all x1, waiting for transfers between devices, body(): gathered = exchange(latent.reshape(device_count, per_peer, model))  8.92 us
    all_to_all x1, starting transfers between devices, body(): gathered = exchange(latent.reshape(device_count, per_peer, model))  7.39 us
    pallas_call x1, Pallas kernels, body(): pl.pallas_call(tokens_kernel, out_shape=jax.ShapeDtypeStruct(gathered.sha...  4.52 us
    pallas_call x1, Pallas kernels, body(): pl.pallas_call(held_kernel, out_shape=(pltpu.VMEM((8, model), f32), pltpu...  1.84 us
  transfers between devices with their start and end apart: 1, of which 1 were waited for; matrix products, arithmetic and copies ran while one was open for 0% of the time, Pallas kernels for 5%

profile of v21, /device:TPU:0, one launch (start us, length us, event | category | flops | bytes accessed | tf_op | source)
XLA Modules:
  0.0 37.3 jit_solution(1018156635890789125)
XLA Ops:
  0.0 7.4 %all-to-all-start = ((bf16[16,8,1152]{2,1,0:T(8,128)(2,1)}), bf16[16,8,1152]{2,1,0:T(8,128)(2,1)S(1)}, u32[]{:S(2)}, u32[]{:S(2)}) async-start(bf16[16,8,1152]{2,1,0:T(8,128)(2,1)} %bitcast.3), calls=%async_computation | async-start | bytes 589824 | tf_op jit(solution)/shard_map/all_to_all | solution.py:164
  7.4 1.8 %held.1 = (f32[8,1152]{1,0:T(8,128)S(1)}, f32[72,128]{1,0:T(8,128)S(1)}, bf16[1152,128]{1,0:T(8,128)(2,1)S(1)}, bf16[32,1152]{1,0:T(8,128)(2,1)S(1)}, bf16[1152,1152]{1,0:T(8,128)(2,1)S(1)}) custom-call(f32[1152]{0:T(1024)} %ln_ref.1, f32[72]{0:T(128)} %qg_ref.1, f32[72]{0:T(128)} %kg_ref.1, bf16[1152,3456]{1,0:T(8,128)(2,1)} %wqkv_hbm.1), custom_call_target="tpu_custom_call" | custom-call | bytes 5308416 | tf_op jit(solution)/shard_map/held/pallas_call | solution.py:169
  9.2 8.9 %all-to-all-done.x_ref = bf16[16,8,1152]{2,1,0:T(8,128)(2,1)S(1)} async-done(((bf16[16,8,1152]{2,1,0:T(8,128)(2,1)}), bf16[16,8,1152]{2,1,0:T(8,128)(2,1)S(1)}, u32[]{:S(2)}, u32[]{:S(2)}) %all-to-all-start) | async-done | bytes 294944 | tf_op jit(solution)/shard_map/all_to_all | solution.py:164
  18.2 4.5 %tokens.1 = bf16[16,8,1152]{2,1,0:T(8,128)(2,1)S(1)} custom-call(bf16[16,8,1152]{2,1,0:T(8,128)(2,1)S(1)} %all-to-all-done.x_ref, f32[8,1152]{1,0:T(8,128)S(1)} %get-tuple-element.10.gains_ref, f32[72,128]{1,0:T(8,128)S(1)} %get-tuple-element.11.columns_ref, bf16[1152,128]{1,0:T(8,128)(2,1)S(1)} %get-tuple-element.12.member_ref, ...), custom_call_target="tpu_custom_call" | custom-call | tf_op jit(solution)/shard_map/tokens/pallas_call | solution.py:190
  22.7 13.9 %all_to_all.10 = bf16[16,8,1152]{2,1,0:T(8,128)(2,1)S(1)} all-to-all(bf16[16,8,1152]{2,1,0:T(8,128)(2,1)S(1)} %tokens.1), channel_id=1, replica_groups={{0,4,8,12,2,6,10,14,1,5,9,13,3,7,11,15},{16,20,24,28,18,22,26,30,17,21,..., dimensions={0} | all-to-all | bytes 589824 | tf_op jit(solution)/shard_map/all_to_all | solution.py:212
  36.6 0.7 %copy.8 = bf16[4,32,1152]{2,1,0:T(8,128)(2,1)} copy(bf16[4,32,1152]{2,1,0:T(8,128)(2,1)S(1)} %bitcast.2) | data formatting | bytes 589824
Async XLA Ops:
  0.0 18.2 %all-to-all-start = ((bf16[16,8,1152]{2,1,0:T(8,128)(2,1)}), bf16[16,8,1152]{2,1,0:T(8,128)(2,1)S(1)}, u32[]{:S(2)}, u32[]{:S(2)}) async-start(bf16[16,8,1152]{2,1,0:T(8,128)(2,1)} %bitcast.3), calls=%async_computation | async-start | bytes 589824 | tf_op jit(solution)/shard_map/all_to_all | solution.py:164

commit v22 on v21

--- a/solution.py
+++ b/solution.py
@@ -157,7 +157,8 @@
     rows, columns, model = latent.shape
     tokens = rows * columns
     per_peer = tokens // device_count
-    order = [4 * i + 2 * row + core for core in range(2) for row in range(2) for i in range(device_count // 4)]
+    line = list(range(device_count // 4))
+    order = [4 * i + 2 * row + core for row, walk in enumerate((line, line[::-1])) for i in walk for core in range(2)]
     exchange = functools.partial(
         lax.all_to_all, axis_name="frame", split_axis=0, concat_axis=0, axis_index_groups=[order], tiled=True
     )

time: 37.6 us -> 36.3 us (0.965)
  the two profiles are of different devices: /device:TPU:0 before, /device:TPU:1 now
where the time goes in v22:
time: 36.3 us; the launch traced here: 36.1 us
  blocking collectives  13.2 us (36%)
  waiting for transfers between devices  8.42 us (23%)
  starting transfers between devices  7.35 us (20%)
  Pallas kernels  6.35 us (17%)
  local copies, waits for them, and re-layouts  0.71 us (2%)
    all_to_all x1, blocking collectives, body(): return exchange(result).reshape(latent.shape)  13.2 us
    all_to_all x1, waiting for transfers between devices, body(): gathered = exchange(latent.reshape(device_count, per_peer, model))  8.42 us
    all_to_all x1, starting transfers between devices, body(): gathered = exchange(latent.reshape(device_count, per_peer, model))  7.35 us
    pallas_call x1, Pallas kernels, body(): pl.pallas_call(tokens_kernel, out_shape=jax.ShapeDtypeStruct(gathered.sha...  4.52 us
    pallas_call x1, Pallas kernels, body(): pl.pallas_call(held_kernel, out_shape=(pltpu.VMEM((8, model), f32), pltpu...  1.83 us
  transfers between devices with their start and end apart: 1, of which 1 were waited for; matrix products, arithmetic and copies ran while one was open for 0% of the time, Pallas kernels for 5%

profile of v22, /device:TPU:1, one launch (start us, length us, event | category | flops | bytes accessed | tf_op | source)
XLA Modules:
  0.0 36.1 jit_solution(8644779285693136990)
XLA Ops:
  0.0 7.3 %all-to-all-start = ((bf16[16,8,1152]{2,1,0:T(8,128)(2,1)}), bf16[16,8,1152]{2,1,0:T(8,128)(2,1)S(1)}, u32[]{:S(2)}, u32[]{:S(2)}) async-start(bf16[16,8,1152]{2,1,0:T(8,128)(2,1)} %bitcast.3), calls=%async_computation | async-start | bytes 589824 | tf_op jit(solution)/shard_map/all_to_all | solution.py:165
  7.4 1.8 %held.1 = (f32[8,1152]{1,0:T(8,128)S(1)}, f32[72,128]{1,0:T(8,128)S(1)}, bf16[1152,128]{1,0:T(8,128)(2,1)S(1)}, bf16[32,1152]{1,0:T(8,128)(2,1)S(1)}, bf16[1152,1152]{1,0:T(8,128)(2,1)S(1)}) custom-call(f32[1152]{0:T(1024)} %ln_ref.1, f32[72]{0:T(128)} %qg_ref.1, f32[72]{0:T(128)} %kg_ref.1, bf16[1152,3456]{1,0:T(8,128)(2,1)} %wqkv_hbm.1), custom_call_target="tpu_custom_call" | custom-call | bytes 5308416 | tf_op jit(solution)/shard_map/held/pallas_call | solution.py:170
  9.2 8.4 %all-to-all-done.x_ref = bf16[16,8,1152]{2,1,0:T(8,128)(2,1)S(1)} async-done(((bf16[16,8,1152]{2,1,0:T(8,128)(2,1)}), bf16[16,8,1152]{2,1,0:T(8,128)(2,1)S(1)}, u32[]{:S(2)}, u32[]{:S(2)}) %all-to-all-start) | async-done | bytes 294944 | tf_op jit(solution)/shard_map/all_to_all | solution.py:165
  17.6 4.5 %tokens.1 = bf16[16,8,1152]{2,1,0:T(8,128)(2,1)S(1)} custom-call(bf16[16,8,1152]{2,1,0:T(8,128)(2,1)S(1)} %all-to-all-done.x_ref, f32[8,1152]{1,0:T(8,128)S(1)} %get-tuple-element.10.gains_ref, f32[72,128]{1,0:T(8,128)S(1)} %get-tuple-element.11.columns_ref, bf16[1152,128]{1,0:T(8,128)(2,1)S(1)} %get-tuple-element.12.member_ref, ...), custom_call_target="tpu_custom_call" | custom-call | tf_op jit(solution)/shard_map/tokens/pallas_call | solution.py:191
  22.1 13.2 %all_to_all.10 = bf16[16,8,1152]{2,1,0:T(8,128)(2,1)S(1)} all-to-all(bf16[16,8,1152]{2,1,0:T(8,128)(2,1)S(1)} %tokens.1), channel_id=1, replica_groups={{0,1,4,5,8,9,12,13,14,15,10,11,6,7,2,3},{16,17,20,21,24,25,28,29,30,31,..., dimensions={0} | all-to-all | bytes 589824 | tf_op jit(solution)/shard_map/all_to_all | solution.py:213
  35.3 0.7 %copy.8 = bf16[4,32,1152]{2,1,0:T(8,128)(2,1)} copy(bf16[4,32,1152]{2,1,0:T(8,128)(2,1)S(1)} %bitcast.2) | data formatting | bytes 589824
Async XLA Ops:
  0.0 17.6 %all-to-all-start = ((bf16[16,8,1152]{2,1,0:T(8,128)(2,1)}), bf16[16,8,1152]{2,1,0:T(8,128)(2,1)S(1)}, u32[]{:S(2)}, u32[]{:S(2)}) async-start(bf16[16,8,1152]{2,1,0:T(8,128)(2,1)} %bitcast.3), calls=%async_computation | async-start | bytes 589824 | tf_op jit(solution)/shard_map/all_to_all | solution.py:165

commit v23 on v22

--- a/solution.py
+++ b/solution.py
@@ -158,7 +158,8 @@
     tokens = rows * columns
     per_peer = tokens // device_count
     line = list(range(device_count // 4))
-    order = [4 * i + 2 * row + core for row, walk in enumerate((line, line[::-1])) for i in walk for core in range(2)]
+    chips = [2 * i + row for row, walk in enumerate((line, line[::-1])) for i in walk]
+    order = [2 * chip + (core + place) % 2 for place, chip in enumerate(chips) for core in range(2)]
     exchange = functools.partial(
         lax.all_to_all, axis_name="frame", split_axis=0, concat_axis=0, axis_index_groups=[order], tiled=True
     )

time: 36.3 us -> 37.1 us (1.022)
  the two profiles are of different devices: /device:TPU:1 before, /device:TPU:0 now
where the time goes in v23:
time: 37.1 us; the launch traced here: 36.9 us
  blocking collectives  13.4 us (36%)
  waiting for transfers between devices  8.97 us (24%)
  starting transfers between devices  7.39 us (20%)
  Pallas kernels  6.36 us (17%)
  local copies, waits for them, and re-layouts  0.71 us (2%)
    all_to_all x1, blocking collectives, body(): return exchange(result).reshape(latent.shape)  13.4 us
    all_to_all x1, waiting for transfers between devices, body(): gathered = exchange(latent.reshape(device_count, per_peer, model))  8.97 us
    all_to_all x1, starting transfers between devices, body(): gathered = exchange(latent.reshape(device_count, per_peer, model))  7.39 us
    pallas_call x1, Pallas kernels, body(): pl.pallas_call(tokens_kernel, out_shape=jax.ShapeDtypeStruct(gathered.sha...  4.52 us
    pallas_call x1, Pallas kernels, body(): pl.pallas_call(held_kernel, out_shape=(pltpu.VMEM((8, model), f32), pltpu...  1.84 us
  transfers between devices with their start and end apart: 1, of which 1 were waited for; matrix products, arithmetic and copies ran while one was open for 0% of the time, Pallas kernels for 5%

profile of v23, /device:TPU:0, one launch (start us, length us, event | category | flops | bytes accessed | tf_op | source)
XLA Modules:
  0.0 36.9 jit_solution(309592007828395082)
XLA Ops:
  0.0 7.4 %all-to-all-start = ((bf16[16,8,1152]{2,1,0:T(8,128)(2,1)}), bf16[16,8,1152]{2,1,0:T(8,128)(2,1)S(1)}, u32[]{:S(2)}, u32[]{:S(2)}) async-start(bf16[16,8,1152]{2,1,0:T(8,128)(2,1)} %bitcast.3), calls=%async_computation | async-start | bytes 589824 | tf_op jit(solution)/shard_map/all_to_all | solution.py:166
  7.4 1.8 %held.1 = (f32[8,1152]{1,0:T(8,128)S(1)}, f32[72,128]{1,0:T(8,128)S(1)}, bf16[1152,128]{1,0:T(8,128)(2,1)S(1)}, bf16[32,1152]{1,0:T(8,128)(2,1)S(1)}, bf16[1152,1152]{1,0:T(8,128)(2,1)S(1)}) custom-call(f32[1152]{0:T(1024)} %ln_ref.1, f32[72]{0:T(128)} %qg_ref.1, f32[72]{0:T(128)} %kg_ref.1, bf16[1152,3456]{1,0:T(8,128)(2,1)} %wqkv_hbm.1), custom_call_target="tpu_custom_call" | custom-call | bytes 5308416 | tf_op jit(solution)/shard_map/held/pallas_call | solution.py:171
  9.2 9.0 %all-to-all-done.x_ref = bf16[16,8,1152]{2,1,0:T(8,128)(2,1)S(1)} async-done(((bf16[16,8,1152]{2,1,0:T(8,128)(2,1)}), bf16[16,8,1152]{2,1,0:T(8,128)(2,1)S(1)}, u32[]{:S(2)}, u32[]{:S(2)}) %all-to-all-start) | async-done | bytes 294944 | tf_op jit(solution)/shard_map/all_to_all | solution.py:166
  18.2 4.5 %tokens.1 = bf16[16,8,1152]{2,1,0:T(8,128)(2,1)S(1)} custom-call(bf16[16,8,1152]{2,1,0:T(8,128)(2,1)S(1)} %all-to-all-done.x_ref, f32[8,1152]{1,0:T(8,128)S(1)} %get-tuple-element.10.gains_ref, f32[72,128]{1,0:T(8,128)S(1)} %get-tuple-element.11.columns_ref, bf16[1152,128]{1,0:T(8,128)(2,1)S(1)} %get-tuple-element.12.member_ref, ...), custom_call_target="tpu_custom_call" | custom-call | tf_op jit(solution)/shard_map/tokens/pallas_call | solution.py:192
  22.7 13.4 %all_to_all.10 = bf16[16,8,1152]{2,1,0:T(8,128)(2,1)S(1)} all-to-all(bf16[16,8,1152]{2,1,0:T(8,128)(2,1)S(1)} %tokens.1), channel_id=1, replica_groups={{0,1,5,4,8,9,13,12,14,15,11,10,6,7,3,2},{16,17,21,20,24,25,29,28,30,31,..., dimensions={0} | all-to-all | bytes 589824 | tf_op jit(solution)/shard_map/all_to_all | solution.py:214
  36.1 0.7 %copy.8 = bf16[4,32,1152]{2,1,0:T(8,128)(2,1)} copy(bf16[4,32,1152]{2,1,0:T(8,128)(2,1)S(1)} %bitcast.2) | data formatting | bytes 589824
Async XLA Ops:
  0.0 18.2 %all-to-all-start = ((bf16[16,8,1152]{2,1,0:T(8,128)(2,1)}), bf16[16,8,1152]{2,1,0:T(8,128)(2,1)S(1)}, u32[]{:S(2)}, u32[]{:S(2)}) async-start(bf16[16,8,1152]{2,1,0:T(8,128)(2,1)} %bitcast.3), calls=%async_computation | async-start | bytes 589824 | tf_op jit(solution)/shard_map/all_to_all | solution.py:166

commit v24 on v22

--- a/solution.py
+++ b/solution.py
@@ -158,7 +158,7 @@
     tokens = rows * columns
     per_peer = tokens // device_count
     line = list(range(device_count // 4))
-    order = [4 * i + 2 * row + core for row, walk in enumerate((line, line[::-1])) for i in walk for core in range(2)]
+    order = [4 * i + member for i in line[::2] + line[1::2][::-1] for member in range(4)]
     exchange = functools.partial(
         lax.all_to_all, axis_name="frame", split_axis=0, concat_axis=0, axis_index_groups=[order], tiled=True
     )

time: 36.3 us -> 37.2 us (1.025)
  the two profiles are of different devices: /device:TPU:1 before, /device:TPU:0 now
where the time goes in v24:
time: 37.2 us; the launch traced here: 36.7 us
  blocking collectives  13.8 us (37%)
  waiting for transfers between devices  8.33 us (22%)
  starting transfers between devices  7.39 us (20%)
  Pallas kernels  6.36 us (17%)
  local copies, waits for them, and re-layouts  0.71 us (2%)
    all_to_all x1, blocking collectives, body(): return exchange(result).reshape(latent.shape)  13.8 us
    all_to_all x1, waiting for transfers between devices, body(): gathered = exchange(latent.reshape(device_count, per_peer, model))  8.33 us
    all_to_all x1, starting transfers between devices, body(): gathered = exchange(latent.reshape(device_count, per_peer, model))  7.39 us
    pallas_call x1, Pallas kernels, body(): pl.pallas_call(tokens_kernel, out_shape=jax.ShapeDtypeStruct(gathered.sha...  4.52 us
    pallas_call x1, Pallas kernels, body(): pl.pallas_call(held_kernel, out_shape=(pltpu.VMEM((8, model), f32), pltpu...  1.84 us
  transfers between devices with their start and end apart: 1, of which 1 were waited for; matrix products, arithmetic and copies ran while one was open for 0% of the time, Pallas kernels for 5%

profile of v24, /device:TPU:0, one launch (start us, length us, event | category | flops | bytes accessed | tf_op | source)
XLA Modules:
  0.0 36.7 jit_solution(17234383827047446764)
XLA Ops:
  0.0 7.4 %all-to-all-start = ((bf16[16,8,1152]{2,1,0:T(8,128)(2,1)}), bf16[16,8,1152]{2,1,0:T(8,128)(2,1)S(1)}, u32[]{:S(2)}, u32[]{:S(2)}) async-start(bf16[16,8,1152]{2,1,0:T(8,128)(2,1)} %bitcast.3), calls=%async_computation | async-start | bytes 589824 | tf_op jit(solution)/shard_map/all_to_all | solution.py:165
  7.4 1.8 %held.1 = (f32[8,1152]{1,0:T(8,128)S(1)}, f32[72,128]{1,0:T(8,128)S(1)}, bf16[1152,128]{1,0:T(8,128)(2,1)S(1)}, bf16[32,1152]{1,0:T(8,128)(2,1)S(1)}, bf16[1152,1152]{1,0:T(8,128)(2,1)S(1)}) custom-call(f32[1152]{0:T(1024)} %ln_ref.1, f32[72]{0:T(128)} %qg_ref.1, f32[72]{0:T(128)} %kg_ref.1, bf16[1152,3456]{1,0:T(8,128)(2,1)} %wqkv_hbm.1), custom_call_target="tpu_custom_call" | custom-call | bytes 5308416 | tf_op jit(solution)/shard_map/held/pallas_call | solution.py:170
  9.2 8.3 %all-to-all-done.x_ref = bf16[16,8,1152]{2,1,0:T(8,128)(2,1)S(1)} async-done(((bf16[16,8,1152]{2,1,0:T(8,128)(2,1)}), bf16[16,8,1152]{2,1,0:T(8,128)(2,1)S(1)}, u32[]{:S(2)}, u32[]{:S(2)}) %all-to-all-start) | async-done | bytes 294944 | tf_op jit(solution)/shard_map/all_to_all | solution.py:165
  17.6 4.5 %tokens.1 = bf16[16,8,1152]{2,1,0:T(8,128)(2,1)S(1)} custom-call(bf16[16,8,1152]{2,1,0:T(8,128)(2,1)S(1)} %all-to-all-done.x_ref, f32[8,1152]{1,0:T(8,128)S(1)} %get-tuple-element.10.gains_ref, f32[72,128]{1,0:T(8,128)S(1)} %get-tuple-element.11.columns_ref, bf16[1152,128]{1,0:T(8,128)(2,1)S(1)} %get-tuple-element.12.member_ref, ...), custom_call_target="tpu_custom_call" | custom-call | tf_op jit(solution)/shard_map/tokens/pallas_call | solution.py:191
  22.1 13.8 %all_to_all.10 = bf16[16,8,1152]{2,1,0:T(8,128)(2,1)S(1)} all-to-all(bf16[16,8,1152]{2,1,0:T(8,128)(2,1)S(1)} %tokens.1), channel_id=1, replica_groups={{0,1,2,3,8,9,10,11,12,13,14,15,4,5,6,7},{16,17,18,19,24,25,26,27,28,29,..., dimensions={0} | all-to-all | bytes 589824 | tf_op jit(solution)/shard_map/all_to_all | solution.py:213
  35.9 0.7 %copy.8 = bf16[4,32,1152]{2,1,0:T(8,128)(2,1)} copy(bf16[4,32,1152]{2,1,0:T(8,128)(2,1)S(1)} %bitcast.2) | data formatting | bytes 589824
Async XLA Ops:
  0.0 17.6 %all-to-all-start = ((bf16[16,8,1152]{2,1,0:T(8,128)(2,1)}), bf16[16,8,1152]{2,1,0:T(8,128)(2,1)S(1)}, u32[]{:S(2)}, u32[]{:S(2)}) async-start(bf16[16,8,1152]{2,1,0:T(8,128)(2,1)} %bitcast.3), calls=%async_computation | async-start | bytes 589824 | tf_op jit(solution)/shard_map/all_to_all | solution.py:165

commit v25 on v23

--- a/solution.py
+++ b/solution.py
@@ -159,7 +159,7 @@
     per_peer = tokens // device_count
     line = list(range(device_count // 4))
     chips = [2 * i + row for row, walk in enumerate((line, line[::-1])) for i in walk]
-    order = [2 * chip + (core + place) % 2 for place, chip in enumerate(chips) for core in range(2)]
+    order = [2 * chips[3 * place % len(chips)] + core for place in range(len(chips)) for core in range(2)]
     exchange = functools.partial(
         lax.all_to_all, axis_name="frame", split_axis=0, concat_axis=0, axis_index_groups=[order], tiled=True
     )

time: 37.1 us -> 38 us (1.024)
  blocking collectives: 13.4 us -> 13.9 us
  waiting for transfers between devices: 8.97 us -> 9.4 us
    all_to_all x1, blocking collectives: 13.4 us -> 13.9 us  [body(): return exchange(result).reshape(latent.shape)]
    all_to_all x1, waiting for transfers between devices: 8.97 us -> 9.4 us  [body(): gathered = exchange(latent.reshape(device_count, per_peer, model))]
where the time goes in v25:
time: 38 us; the launch traced here: 37.8 us
  blocking collectives  13.9 us (37%)
  waiting for transfers between devices  9.4 us (25%)
  starting transfers between devices  7.39 us (19%)
  Pallas kernels  6.35 us (17%)
  local copies, waits for them, and re-layouts  0.71 us (2%)
    all_to_all x1, blocking collectives, body(): return exchange(result).reshape(latent.shape)  13.9 us
    all_to_all x1, waiting for transfers between devices, body(): gathered = exchange(latent.reshape(device_count, per_peer, model))  9.4 us
    all_to_all x1, starting transfers between devices, body(): gathered = exchange(latent.reshape(device_count, per_peer, model))  7.39 us
    pallas_call x1, Pallas kernels, body(): pl.pallas_call(tokens_kernel, out_shape=jax.ShapeDtypeStruct(gathered.sha...  4.52 us
    pallas_call x1, Pallas kernels, body(): pl.pallas_call(held_kernel, out_shape=(pltpu.VMEM((8, model), f32), pltpu...  1.84 us
  transfers between devices with their start and end apart: 1, of which 1 were waited for; matrix products, arithmetic and copies ran while one was open for 0% of the time, Pallas kernels for 5%

profile of v25, /device:TPU:0, one launch (start us, length us, event | category | flops | bytes accessed | tf_op | source)
XLA Modules:
  0.0 37.8 jit_solution(10314673161680668748)
XLA Ops:
  0.0 7.4 %all-to-all-start = ((bf16[16,8,1152]{2,1,0:T(8,128)(2,1)}), bf16[16,8,1152]{2,1,0:T(8,128)(2,1)S(1)}, u32[]{:S(2)}, u32[]{:S(2)}) async-start(bf16[16,8,1152]{2,1,0:T(8,128)(2,1)} %bitcast.3), calls=%async_computation | async-start | bytes 589824 | tf_op jit(solution)/shard_map/all_to_all | solution.py:166
  7.4 1.8 %held.1 = (f32[8,1152]{1,0:T(8,128)S(1)}, f32[72,128]{1,0:T(8,128)S(1)}, bf16[1152,128]{1,0:T(8,128)(2,1)S(1)}, bf16[32,1152]{1,0:T(8,128)(2,1)S(1)}, bf16[1152,1152]{1,0:T(8,128)(2,1)S(1)}) custom-call(f32[1152]{0:T(1024)} %ln_ref.1, f32[72]{0:T(128)} %qg_ref.1, f32[72]{0:T(128)} %kg_ref.1, bf16[1152,3456]{1,0:T(8,128)(2,1)} %wqkv_hbm.1), custom_call_target="tpu_custom_call" | custom-call | bytes 5308416 | tf_op jit(solution)/shard_map/held/pallas_call | solution.py:171
  9.2 9.4 %all-to-all-done.x_ref = bf16[16,8,1152]{2,1,0:T(8,128)(2,1)S(1)} async-done(((bf16[16,8,1152]{2,1,0:T(8,128)(2,1)}), bf16[16,8,1152]{2,1,0:T(8,128)(2,1)S(1)}, u32[]{:S(2)}, u32[]{:S(2)}) %all-to-all-start) | async-done | bytes 294944 | tf_op jit(solution)/shard_map/all_to_all | solution.py:166
  18.6 4.5 %tokens.1 = bf16[16,8,1152]{2,1,0:T(8,128)(2,1)S(1)} custom-call(bf16[16,8,1152]{2,1,0:T(8,128)(2,1)S(1)} %all-to-all-done.x_ref, f32[8,1152]{1,0:T(8,128)S(1)} %get-tuple-element.10.gains_ref, f32[72,128]{1,0:T(8,128)S(1)} %get-tuple-element.11.columns_ref, bf16[1152,128]{1,0:T(8,128)(2,1)S(1)} %get-tuple-element.12.member_ref, ...), custom_call_target="tpu_custom_call" | custom-call | tf_op jit(solution)/shard_map/tokens/pallas_call | solution.py:192
  23.2 13.9 %all_to_all.10 = bf16[16,8,1152]{2,1,0:T(8,128)(2,1)S(1)} all-to-all(bf16[16,8,1152]{2,1,0:T(8,128)(2,1)S(1)} %tokens.1), channel_id=1, replica_groups={{0,1,12,13,6,7,4,5,14,15,2,3,8,9,10,11},{16,17,28,29,22,23,20,21,30,31,..., dimensions={0} | all-to-all | bytes 589824 | tf_op jit(solution)/shard_map/all_to_all | solution.py:214
  37.1 0.7 %copy.8 = bf16[4,32,1152]{2,1,0:T(8,128)(2,1)} copy(bf16[4,32,1152]{2,1,0:T(8,128)(2,1)S(1)} %bitcast.2) | data formatting | bytes 589824
Async XLA Ops:
  0.0 18.6 %all-to-all-start = ((bf16[16,8,1152]{2,1,0:T(8,128)(2,1)}), bf16[16,8,1152]{2,1,0:T(8,128)(2,1)S(1)}, u32[]{:S(2)}, u32[]{:S(2)}) async-start(bf16[16,8,1152]{2,1,0:T(8,128)(2,1)} %bitcast.3), calls=%async_computation | async-start | bytes 589824 | tf_op jit(solution)/shard_map/all_to_all | solution.py:166

commit v26 on v24

--- a/solution.py
+++ b/solution.py
@@ -158,7 +158,7 @@
     tokens = rows * columns
     per_peer = tokens // device_count
     line = list(range(device_count // 4))
-    order = [4 * i + member for i in line[::2] + line[1::2][::-1] for member in range(4)]
+    order = [4 * i + 2 * row + core for row, walk in enumerate((line[::-1], line)) for i in walk for core in range(2)]
     exchange = functools.partial(
         lax.all_to_all, axis_name="frame", split_axis=0, concat_axis=0, axis_index_groups=[order], tiled=True
     )

time: 37.2 us -> 35 us (0.941)
  waiting for transfers between devices: 8.33 us -> 6.08 us
  starting transfers between devices: 7.39 us -> 8.41 us
  blocking collectives: 13.8 us -> 13.2 us
    all_to_all x1, waiting for transfers between devices: 8.33 us -> 6.08 us  [body(): gathered = exchange(latent.reshape(device_count, per_peer, model))]
    all_to_all x1, starting transfers between devices: 7.39 us -> 8.41 us  [body(): gathered = exchange(latent.reshape(device_count, per_peer, model))]
    all_to_all x1, blocking collectives: 13.8 us -> 13.2 us  [body(): return exchange(result).reshape(latent.shape)]
where the time goes in v26:
time: 35 us; the launch traced here: 34.8 us
  blocking collectives  13.2 us (38%)
  starting transfers between devices  8.41 us (24%)
  Pallas kernels  6.36 us (18%)
  waiting for transfers between devices  6.08 us (17%)
  local copies, waits for them, and re-layouts  0.71 us (2%)
    all_to_all x1, blocking collectives, body(): return exchange(result).reshape(latent.shape)  13.2 us
    all_to_all x1, starting transfers between devices, body(): gathered = exchange(latent.reshape(device_count, per_peer, model))  8.41 us
    all_to_all x1, waiting for transfers between devices, body(): gathered = exchange(latent.reshape(device_count, per_peer, model))  6.08 us
    pallas_call x1, Pallas kernels, body(): pl.pallas_call(tokens_kernel, out_shape=jax.ShapeDtypeStruct(gathered.sha...  4.52 us
    pallas_call x1, Pallas kernels, body(): pl.pallas_call(held_kernel, out_shape=(pltpu.VMEM((8, model), f32), pltpu...  1.83 us
    unnamed x1, local copies, waits for them, and re-layouts  0.71 us
  transfers between devices with their start and end apart: 1, of which 1 were waited for; matrix products, arithmetic and copies ran while one was open for 0% of the time, Pallas kernels for 5%

profile of v26, /device:TPU:0, one launch (start us, length us, event | category | flops | bytes accessed | tf_op | source)
XLA Modules:
  0.0 34.8 jit_solution(3020359053035674802)
XLA Ops:
  0.0 8.4 %all-to-all-start = ((bf16[16,8,1152]{2,1,0:T(8,128)(2,1)}), bf16[16,8,1152]{2,1,0:T(8,128)(2,1)S(1)}, u32[]{:S(2)}, u32[]{:S(2)}) async-start(bf16[16,8,1152]{2,1,0:T(8,128)(2,1)} %bitcast.3), calls=%async_computation | async-start | bytes 589824 | tf_op jit(solution)/shard_map/all_to_all | solution.py:165
  8.4 1.8 %held.1 = (f32[8,1152]{1,0:T(8,128)S(1)}, f32[72,128]{1,0:T(8,128)S(1)}, bf16[1152,128]{1,0:T(8,128)(2,1)S(1)}, bf16[32,1152]{1,0:T(8,128)(2,1)S(1)}, bf16[1152,1152]{1,0:T(8,128)(2,1)S(1)}) custom-call(f32[1152]{0:T(1024)} %ln_ref.1, f32[72]{0:T(128)} %qg_ref.1, f32[72]{0:T(128)} %kg_ref.1, bf16[1152,3456]{1,0:T(8,128)(2,1)} %wqkv_hbm.1), custom_call_target="tpu_custom_call" | custom-call | bytes 5308416 | tf_op jit(solution)/shard_map/held/pallas_call | solution.py:170
  10.3 6.1 %all-to-all-done.x_ref = bf16[16,8,1152]{2,1,0:T(8,128)(2,1)S(1)} async-done(((bf16[16,8,1152]{2,1,0:T(8,128)(2,1)}), bf16[16,8,1152]{2,1,0:T(8,128)(2,1)S(1)}, u32[]{:S(2)}, u32[]{:S(2)}) %all-to-all-start) | async-done | bytes 294944 | tf_op jit(solution)/shard_map/all_to_all | solution.py:165
  16.3 4.5 %tokens.1 = bf16[16,8,1152]{2,1,0:T(8,128)(2,1)S(1)} custom-call(bf16[16,8,1152]{2,1,0:T(8,128)(2,1)S(1)} %all-to-all-done.x_ref, f32[8,1152]{1,0:T(8,128)S(1)} %get-tuple-element.10.gains_ref, f32[72,128]{1,0:T(8,128)S(1)} %get-tuple-element.11.columns_ref, bf16[1152,128]{1,0:T(8,128)(2,1)S(1)} %get-tuple-element.12.member_ref, ...), custom_call_target="tpu_custom_call" | custom-call | tf_op jit(solution)/shard_map/tokens/pallas_call | solution.py:191
  20.9 13.2 %all_to_all.10 = bf16[16,8,1152]{2,1,0:T(8,128)(2,1)S(1)} all-to-all(bf16[16,8,1152]{2,1,0:T(8,128)(2,1)S(1)} %tokens.1), channel_id=1, replica_groups={{12,13,8,9,4,5,0,1,2,3,6,7,10,11,14,15},{28,29,24,25,20,21,16,17,18,19,..., dimensions={0} | all-to-all | bytes 589824 | tf_op jit(solution)/shard_map/all_to_all | solution.py:213
  34.1 0.7 %copy.8 = bf16[4,32,1152]{2,1,0:T(8,128)(2,1)} copy(bf16[4,32,1152]{2,1,0:T(8,128)(2,1)S(1)} %bitcast.2) | data formatting | bytes 589824
Async XLA Ops:
  0.0 16.3 %all-to-all-start = ((bf16[16,8,1152]{2,1,0:T(8,128)(2,1)}), bf16[16,8,1152]{2,1,0:T(8,128)(2,1)S(1)}, u32[]{:S(2)}, u32[]{:S(2)}) async-start(bf16[16,8,1152]{2,1,0:T(8,128)(2,1)} %bitcast.3), calls=%async_computation | async-start | bytes 589824 | tf_op jit(solution)/shard_map/all_to_all | solution.py:165
